TPU v7x, 32 devices: a whole 2x2x4 slice. The times are simulated.
32 devices in a mesh: seq: 16 (over z, x, core), wt: 2 (over y).
Axes of the slice: x: 2, y: 2, z: 4, core: 2. Of those that a mesh axis runs over, the one named last changes fastest.
Arguments:
- tokens: int32 [2, 2048], P('wt', 'seq'), may hold values from 0 to 511
- embed_table: bfloat16 [512, 8192], P(None, 'wt'), may hold values from -8 to 8
- norm_gain: bfloat16 [8192], P('wt'), may hold values from 0.099609375 to 1.8984375
- w_in: bfloat16 [8192, 3, 4096], P('wt', None, 'seq'), may hold values from -0.0625 to 0.0625
- short_taps: bfloat16 [3, 3, 4096], P(None, None, 'seq'), may hold values from -3 to 3
- filters: bfloat16 [256, 128], P('seq'), may hold values from -2 to 2
- w_out: bfloat16 [8192, 4096], P('wt'), may hold values from -0.09375 to 0.09375
Outputs:
- block_out: bfloat16 [2, 2048, 8192], P(None, 'seq', 'wt')
All inputs are finite; a program needn't handle non-finite values.
Results may differ from a plain program's by a relative error of at most 0.0088.
Values may be sent and summed in bfloat16 or wider, within the bound.
No kernel may reach another device: no remote copies, remote signals or barrier semaphores. Data moves between devices by JAX's collectives and lax.ppermute only.
A program may use at most 128 MiB of HBM per device.

v0:
```python
import functools

import jax
import jax.numpy as jnp
from jax import lax
from jax.experimental import pallas as pl
from jax.experimental.pallas import tpu as pltpu
from jax.sharding import PartitionSpec as P

LANES = 128
MIB = 1 << 20


def shifted(shard, axis, by):
    size = lax.axis_size(axis)
    pairs = [(i, i + by) for i in range(size) if 0 <= i + by < size]
    return lax.ppermute(shard, axis, pairs)


def causal_pair(filter_vals):
    tap_count = filter_vals.shape[1]
    group_count = filter_vals.shape[0]
    tiled_taps = jnp.tile(filter_vals, (1, 2 * tap_count - 1)).reshape(
        group_count, tap_count, 2 * tap_count - 1
    )[:, :, :tap_count]
    circulant = jnp.swapaxes(tiled_taps, 1, 2)
    row_pos = lax.broadcasted_iota(jnp.int32, (tap_count, tap_count), 0)
    col_pos = lax.broadcasted_iota(jnp.int32, (tap_count, tap_count), 1)
    lower_mask = (row_pos >= col_pos)[None]
    zero_mat = jnp.zeros_like(circulant)
    return (jnp.where(lower_mask, circulant, zero_mat), jnp.where(lower_mask, zero_mat, circulant))


def short_mix(extended, tap_vals):
    row_count = extended.shape[0] - 2
    ext_vals = extended.astype(jnp.float32)
    return (
        tap_vals[0] * ext_vals[2 : 2 + row_count]
        + tap_vals[1] * ext_vals[1 : 1 + row_count]
        + tap_vals[2] * ext_vals[0:row_count]
    )


def run_filter(extended, lower_mat, upper_mat):
    tap_count = lower_mat.shape[1]
    group_count = lower_mat.shape[0]
    chan_count = extended.shape[1]
    blocks = extended.shape[0] // tap_count
    stacked = extended.reshape(blocks, tap_count, group_count, chan_count // group_count)
    filtered = jnp.einsum(
        "gij,bjgc->bigc", lower_mat, stacked[1:], preferred_element_type=jnp.float32
    )
    filtered = filtered + jnp.einsum(
        "gij,bjgc->bigc", upper_mat, stacked[:-1], preferred_element_type=jnp.float32
    )
    return filtered.reshape((blocks - 1) * tap_count, chan_count)


def plain_block(tokens, embed_table, norm_gain, w_in, short_taps, filters, w_out):
    token_ids = tokens[0]
    own_len = token_ids.shape[0]
    tap_count = filters.shape[1]
    table_vals = embed_table.astype(jnp.float32)
    square_sums = lax.psum(jnp.sum(table_vals * table_vals, axis=1, keepdims=True), "wt")
    feature_count = embed_table.shape[1] * lax.axis_size("wt")
    row_scale = lax.rsqrt(square_sums / feature_count + 1e-06)
    normed = (table_vals * row_scale * norm_gain.astype(jnp.float32)).astype(jnp.bfloat16)
    local_chans = w_in.shape[2]
    w_flat = w_in.reshape(w_in.shape[0], 3 * local_chans)
    vocab_size = embed_table.shape[0]
    partial_sum = jnp.dot(normed, w_flat, preferred_element_type=jnp.float32)
    vocab_flat = lax.psum(partial_sum, "wt").astype(jnp.bfloat16)
    vocab_proj = vocab_flat.reshape(vocab_size, 3, local_chans)
    vocab_all, tap_all, filter_all = (
        lax.all_gather(vocab_proj, "seq", axis=2, tiled=True),
        lax.all_gather(short_taps, "seq", axis=2, tiled=True),
        lax.all_gather(filters, "seq", axis=0, tiled=True),
    )
    projected = jnp.take(vocab_all, token_ids, axis=0)
    edge_prev = shifted(projected[own_len - 2 :], "seq", 1)
    mixture = short_mix(
        jnp.concatenate([edge_prev, projected], axis=0), tap_all.astype(jnp.float32)
    )
    product = (mixture[:, 0] * mixture[:, 2]).astype(jnp.bfloat16)
    tail_prev = shifted(product[own_len - tap_count + 1 :], "seq", 1)
    chan_count = product.shape[1]
    extended = jnp.concatenate(
        [jnp.zeros((1, chan_count), jnp.bfloat16), tail_prev, product], axis=0
    )
    lower_mat, upper_mat = causal_pair(filter_all)
    filtered = run_filter(extended, lower_mat, upper_mat)
    gated = (mixture[:, 1] * filtered).astype(jnp.bfloat16)
    everyone = lax.all_gather(tokens, "wt", axis=0, tiled=True)
    branch = jnp.einsum(
        "knc,dc->knd",
        lax.all_gather(gated[None], "wt", axis=0, tiled=True),
        w_out,
        preferred_element_type=jnp.float32,
    )
    embedded = jnp.take(embed_table, everyone, axis=0)
    return (embedded.astype(jnp.float32) + branch).astype(jnp.bfloat16)


def vocab_share_body(half_ref, emb_ref, gain_ref, w_ref, out_ref, *rest, steps, squares):
    if squares:
        sq_ref, acc_ref, sq_acc = rest
    else:
        (acc_ref,) = rest
    step = pl.program_id(0)
    emb = emb_ref[...]
    scaled = emb * gain_ref[...]
    weights = jnp.concatenate([w_ref[s] for s in range(w_ref.shape[0])], axis=1)
    term = jnp.dot(scaled, weights, preferred_element_type=jnp.float32)
    if squares:
        vals = emb.astype(jnp.float32)
        vals = vals * vals
        part = vals[:, :LANES]
        for i in range(1, vals.shape[1] // LANES):
            part = part + vals[:, i * LANES : (i + 1) * LANES]

    @pl.when(step == 0)
    def _():
        acc_ref[...] = term
        if squares:
            sq_acc[...] = part

    @pl.when(step > 0)
    def _():
        acc_ref[...] += term
        if squares:
            sq_acc[...] += part

    @pl.when(step == steps - 1)
    def _():
        out_ref[...] = acc_ref[...].astype(out_ref.dtype)
        if squares:
            sq_ref[...] = jnp.sum(sq_acc[...].T, axis=0, keepdims=True)


def vocab_share(half, embed_table, gain_row, w_streams, out_dtype, squares):
    vocab, feats = embed_table.shape
    streams, _, local_chans = w_streams.shape
    chans = local_chans // 2
    depth = feats // 4 if feats % (4 * LANES) == 0 else feats
    steps = feats // depth
    width = streams * chans
    out_shape = [jax.ShapeDtypeStruct((vocab, width), out_dtype)]
    out_specs = [pl.BlockSpec((vocab, width), lambda k, h: (0, 0))]
    scratch = [pltpu.VMEM((vocab, width), jnp.float32)]
    if squares:
        out_shape.append(jax.ShapeDtypeStruct((1, vocab), jnp.float32))
        out_specs.append(pl.BlockSpec((1, vocab), lambda k, h: (0, 0)))
        scratch.append(pltpu.VMEM((vocab, LANES), jnp.float32))
    return pl.pallas_call(
        functools.partial(vocab_share_body, steps=steps, squares=squares),
        grid_spec=pltpu.PrefetchScalarGridSpec(
            num_scalar_prefetch=1,
            grid=(steps,),
            in_specs=[
                pl.BlockSpec((vocab, depth), lambda k, h: (0, k)),
                pl.BlockSpec((1, depth), lambda k, h: (0, k)),
                pl.BlockSpec((streams, depth, chans), lambda k, h: (0, k, h[0])),
            ],
            out_specs=out_specs,
            scratch_shapes=scratch,
        ),
        out_shape=out_shape,
        compiler_params=pltpu.CompilerParams(vmem_limit_bytes=40 * MIB),
        cost_estimate=pl.CostEstimate(
            flops=2 * vocab * feats * width,
            bytes_accessed=2 * feats * (vocab + width),
            transcendentals=0,
        ),
        name="vocab_share",
    )(half, embed_table, gain_row, w_streams)


def mixer_body(
    place_ref, tok_ref, own_ref, got_ref, sq_ref, sq_got_ref, taps_ref, filt_ref, out_ref,
    vocab_t, toeplitz, tap_cols, carry, prod, gate, conv, *, feature_count, chunk,
):
    chans = out_ref.shape[-1]
    vocab = vocab_t.shape[1]
    length = tok_ref.shape[-1]
    groups = filt_ref.shape[0]
    taps = filt_ref.shape[1]
    gsz = chans // groups
    blocks = length // taps

    @pl.when(pl.program_id(0) == 0)
    def _():
        sums = (own_ref[...] + got_ref[...].astype(jnp.float32)).T
        scale = lax.rsqrt((sq_ref[...] + sq_got_ref[...]) / feature_count + 1e-06)
        vocab_t[...] = (sums * scale).astype(jnp.bfloat16)
        row = lax.broadcasted_iota(jnp.int32, (taps, taps), 0)
        col = lax.broadcasted_iota(jnp.int32, (taps, taps), 1)
        filt = filt_ref[...].astype(jnp.float32)
        for g in range(groups):
            circ = pltpu.roll(
                jnp.broadcast_to(filt[g : g + 1], (taps, taps)), 0, 1, stride=1, stride_axis=0
            )
            toeplitz[g, :taps] = jnp.where(col < row, circ, 0.0).astype(jnp.bfloat16)
            toeplitz[g, taps:] = jnp.where(col >= row, circ, 0.0).astype(jnp.bfloat16)
        tap_cols[...] = taps_ref[...].T
        prod[:, :gsz, :] = jnp.zeros((groups, gsz, taps), jnp.bfloat16)

    for k in range(2):
        carry[k] = jnp.zeros(carry.shape[1:], jnp.float32)

    ids = lax.broadcasted_iota(jnp.int32, (vocab, chunk), 0)
    lane = lax.broadcasted_iota(jnp.int32, (chans, LANES), 1)
    for n in range(length // chunk):
        picks = jnp.where(ids == tok_ref[0, :, n * chunk : (n + 1) * chunk], 1.0, 0.0)
        proj = jnp.dot(vocab_t[...], picks.astype(jnp.bfloat16), preferred_element_type=jnp.float32)
        mixed = []
        for s in range(3):
            cur = proj[s * chans : (s + 1) * chans]
            total = tap_cols[:, s : s + 1] * cur
            for k in (1, 2):
                back = pltpu.roll(cur, k, 1)
                head = jnp.where(lane < k, carry[k - 1, s], back[:, :LANES])
                carry[k - 1, s] = back[:, :LANES]
                back = jnp.concatenate([head, back[:, LANES:]], axis=1)
                total = total + tap_cols[:, 3 * k + s : 3 * k + s + 1] * back
            mixed.append(total)
        gate[:, n * chunk : (n + 1) * chunk] = mixed[1]
        inner = (mixed[0] * mixed[2]).astype(jnp.bfloat16)
        for b in range(chunk // taps):
            at = (n * (chunk // taps) + b + 1) * gsz
            for g in range(groups):
                prod[g, at : at + gsz, :] = inner[g * gsz : (g + 1) * gsz, b * taps : (b + 1) * taps]
    rows = blocks * gsz
    for g in range(groups):
        pair = jnp.concatenate([prod[g, :rows], prod[g, gsz : gsz + rows]], axis=1)
        conv[g] = jnp.dot(pair, toeplitz[g], preferred_element_type=jnp.float32)
    for b in range(blocks):
        filtered = jnp.concatenate(
            [conv[g, b * gsz : (b + 1) * gsz, :] for g in range(groups)], axis=0
        )
        gated = gate[:, b * taps : (b + 1) * taps] * filtered
        out_ref[b, 0] = gated.T.astype(jnp.bfloat16)


def mixer(place, tokens, own, got, squares, squares_got, taps_rows, filt, feature_count):
    genomes, length = tokens.shape
    vocab, width = own.shape
    chans = width // 3
    groups, taps = filt.shape
    gsz = chans // groups
    blocks = length // taps
    chunk = 2 * taps
    whole = lambda *shape: pl.BlockSpec(shape, lambda g, p: (0,) * len(shape))
    return pl.pallas_call(
        functools.partial(mixer_body, feature_count=feature_count, chunk=chunk),
        grid_spec=pltpu.PrefetchScalarGridSpec(
            num_scalar_prefetch=1,
            grid=(genomes,),
            in_specs=[
                pl.BlockSpec((1, 1, length), lambda g, p: (g, 0, 0)),
                whole(vocab, width),
                whole(vocab, width),
                whole(1, vocab),
                whole(1, vocab),
                whole(*taps_rows.shape),
                whole(groups, taps),
            ],
            out_specs=pl.BlockSpec((blocks, 1, taps, chans), lambda g, p: (0, g, 0, 0)),
            scratch_shapes=[
                pltpu.VMEM((width, vocab), jnp.bfloat16),
                pltpu.VMEM((groups, 2 * taps, taps), jnp.bfloat16),
                pltpu.VMEM((chans, taps_rows.shape[0]), jnp.float32),
                pltpu.VMEM((2, 3, chans, LANES), jnp.float32),
                pltpu.VMEM((groups, (blocks + 1) * gsz, taps), jnp.bfloat16),
                pltpu.VMEM((chans, length), jnp.float32),
                pltpu.VMEM((groups, blocks * gsz, taps), jnp.float32),
            ],
        ),
        out_shape=jax.ShapeDtypeStruct((blocks, genomes, taps, chans), jnp.bfloat16),
        compiler_params=pltpu.CompilerParams(vmem_limit_bytes=40 * MIB),
        cost_estimate=pl.CostEstimate(
            flops=2 * genomes * length * vocab * width,
            bytes_accessed=6 * vocab * width + 2 * genomes * length * chans,
            transcendentals=0,
        ),
        name="mixer",
    )(place, tokens[:, None, :], own, got, squares, squares_got, taps_rows, filt)


def project_body(tok_ref, mine_ref, other_ref, table_ref, w_ref, out_ref, gated, picks, *, which):
    sources, genomes, rows, chans = mine_ref.shape

    @pl.when(pl.program_id(0) == 0)
    def _():
        vocab = table_ref.shape[0]
        ids = lax.broadcasted_iota(jnp.int32, (vocab, genomes * rows), 0)
        hot = jnp.where(ids == tok_ref[...], 1.0, 0.0)
        picks[...] = hot.T.astype(jnp.bfloat16)
        me = lax.axis_index("wt")
        for ref, at in ((mine_ref, me), (other_ref, 1 - me)):
            for s in range(sources):
                lanes = pl.ds(pl.multiple_of((2 * s + at) * chans, LANES), chans)
                for g in range(genomes):
                    gated[g * rows : (g + 1) * rows, lanes] = ref[s, g]

    total = lax.dot_general(
        gated[...], w_ref[...], (((1,), (1,)), ((), ())), preferred_element_type=jnp.float32
    )
    total = total + jnp.dot(picks[...], table_ref[...], preferred_element_type=jnp.float32)
    for g in range(genomes):
        out_ref[g] = total[g * rows : (g + 1) * rows].astype(jnp.bfloat16)


def project(tok_row, mine, other, embed_table, w_out):
    sources, genomes, rows, chans = mine.shape
    feats, depth = w_out.shape
    vocab = embed_table.shape[0]
    tile = 512
    whole = lambda *shape: pl.BlockSpec(shape, lambda f: (0,) * len(shape))
    return pl.pallas_call(
        functools.partial(project_body, which=None),
        grid=(feats // tile,),
        in_specs=[
            whole(1, genomes * rows),
            whole(*mine.shape),
            whole(*mine.shape),
            pl.BlockSpec((vocab, tile), lambda f: (0, f)),
            pl.BlockSpec((tile, depth), lambda f: (f, 0)),
        ],
        out_specs=pl.BlockSpec((genomes, rows, tile), lambda f: (0, 0, f)),
        scratch_shapes=[
            pltpu.VMEM((genomes * rows, depth), jnp.bfloat16),
            pltpu.VMEM((genomes * rows, vocab), jnp.bfloat16),
        ],
        out_shape=jax.ShapeDtypeStruct((genomes, rows, feats), jnp.bfloat16),
        compiler_params=pltpu.CompilerParams(vmem_limit_bytes=40 * MIB),
        cost_estimate=pl.CostEstimate(
            flops=2 * genomes * rows * feats * (depth + vocab),
            bytes_accessed=2 * feats * (depth + vocab + genomes * rows),
            transcendentals=0,
        ),
        name="project",
    )(tok_row, mine, other, embed_table, w_out)


def swap_wt(shard):
    return lax.ppermute(shard, "wt", [(0, 1), (1, 0)])


def shared_block(tokens, embed_table, norm_gain, w_in, short_taps, filters, w_out):
    me = lax.axis_index("wt")
    local_chans = w_in.shape[2]
    chans = local_chans // 2
    groups = filters.shape[0] // 2
    feature_count = embed_table.shape[1] * lax.axis_size("wt")
    w_streams = jnp.transpose(w_in, (1, 0, 2))
    gain_row = norm_gain[None]
    pick = lambda which: jnp.reshape(which, (1,)).astype(jnp.int32)
    sent, squares = vocab_share(pick(1 - me), embed_table, gain_row, w_streams, jnp.bfloat16, True)
    got = swap_wt(sent)
    squares_got = swap_wt(squares)
    (own,) = vocab_share(pick(me), embed_table, gain_row, w_streams, jnp.float32, False)
    other_tokens = swap_wt(tokens)
    both = jnp.where(
        me == 0,
        jnp.concatenate([tokens, other_tokens], axis=0),
        jnp.concatenate([other_tokens, tokens], axis=0),
    )
    all_tokens = lax.all_gather(both, "seq", axis=1, tiled=True)
    taps_rows = lax.dynamic_slice_in_dim(
        short_taps.astype(jnp.float32).reshape(9, local_chans), me * chans, chans, 1
    )
    taps_rows = jnp.pad(taps_rows, ((0, 7), (0, 0)))
    filt = lax.dynamic_slice_in_dim(filters, me * groups, groups, 0)
    gated = mixer(pick(me), all_tokens, own, got, squares, squares_got, taps_rows, filt, feature_count)
    mine = lax.all_to_all(gated, "seq", 0, 0, tiled=True)
    other = swap_wt(mine)
    return project(both.reshape(1, -1), mine, other, embed_table, w_out)


def local(*args):
    tokens, embed_table, norm_gain, w_in, short_taps, filters, w_out = args
    wide = lax.axis_size("wt") == 2 and w_in.shape[2] % (2 * LANES) == 0
    aligned = tokens.shape[1] == filters.shape[1] == LANES and w_out.shape[0] % 512 == 0
    if wide and aligned and w_in.shape[2] == 2 * LANES:
        return shared_block(*args)
    return plain_block(*args)


def solution(mesh):
    placed = (
        P("wt", "seq"),
        P(None, "wt"),
        P("wt"),
        P("wt", None, "seq"),
        P(None, None, "seq"),
        P("seq", None),
        P("wt", None),
    )
    return jax.shard_map(
        local, mesh=mesh, in_specs=placed, out_specs=P(None, "seq", "wt"), check_vma=False
    )
```

profile of v0, /device:TPU:0, one launch (start us, length us, event | category | flops | bytes accessed | tf_op | source)
XLA Modules:
  0.0 125.4 jit_solution(1861882859642474158)
XLA Ops:
  0.0 0.0 copy-start
  0.0 0.0 copy-start.6
  0.0 3.0 %collective-permute-start = (s32[1,128]{1,0:T(1,128)}, s32[1,128]{1,0:T(1,128)S(1)}, u32[]{:S(2)}, u32[]{:S(2)}) collective-permute-start(s32[1,128]{1,0:T(1,128)} %param.7), channel_id=1, source_target_pairs={{0,1},{1,0},{2,3},{3,2},{4,5},{5,4},{6,7},{7,6},{8,9},{9,8},{10,11... | collective-permute-start | bytes 1544 | tf_op jit(solution)/shard_map/ppermute | solution.py:346
  3.0 0.7 broadcast_in_dim.7.gain_ref
  3.7 0.0 copy-start.1
  3.7 2.2 %copy-done.1 = bf16[512,4096]{1,0:T(8,128)(2,1)S(1)} copy-done((bf16[512,4096]{1,0:T(8,128)(2,1)S(1)}, bf16[512,4096]{1,0:T(8,128)(2,1)}, u32[]{:S(2)}) %copy-start.1) | copy-done | bytes 4194328
  5.9 0.0 copy-start.4
  5.9 2.8 %copy-done.4 = bf16[4096,3,256]{2,0,1:T(8,128)(2,1)S(1)} copy-done((bf16[4096,3,256]{2,0,1:T(8,128)(2,1)S(1)}, bf16[4096,3,256]{2,0,1:T(8,128)(2,1)}, u32[]{:S(2)}) %copy-start.4) | copy-done | bytes 6291480
  8.7 4.3 %vocab_share.3 = (bf16[512,384]{1,0:T(8,128)(2,1)S(1)}, f32[1,512]{1,0:T(1,128)S(1)}) custom-call(s32[1]{0:T(128)} %bitcast.3.half_ref, bf16[512,4096]{1,0:T(8,128)(2,1)S(1)} %copy-done.1, bf16[1,4096]{1,0:T(2,128)(2,1)S(1)} %broadcast_in_dim.7.gain_ref, bf16[3,4096,256]{2,1,0:T(8,128)(2,1)S(1)} %bitcast.4), custom_call_target="tpu_custom_call" | custom-call | flops 1610612736 | bytes 7340032 | tf_op jit(solution)/shard_map/vocab_share/pallas_call | solution.py:154
  13.0 0.0 copy-start.7
  13.0 0.1 collective-permute-start.2
  13.1 2.0 %collective-permute-start.1 = (bf16[512,384]{1,0:T(8,128)(2,1)S(1)}, bf16[512,384]{1,0:T(8,128)(2,1)S(1)}, u32[]{:S(2)}, u32[]{:S(2)}) collective-permute-start(bf16[512,384]{1,0:T(8,128)(2,1)S(1)} %get-tuple-element.7), channel_id=1, source_target_pairs={{0,1},{1,0},{2,3},{3,2},{4,5},{5,4},{6,7},{7,6},{8,9},{9,8},{10,11... | collective-permute-start | bytes 1179656 | tf_op jit(solution)/shard_map/ppermute | solution.py:346
  15.1 0.0 copy-done.6
  15.1 0.0 copy-start.2
  15.1 2.2 %copy-done.2 = bf16[512,4096]{1,0:T(8,128)(2,1)S(1)} copy-done((bf16[512,4096]{1,0:T(8,128)(2,1)S(1)}, bf16[512,4096]{1,0:T(8,128)(2,1)}, u32[]{:S(2)}) %copy-start.2) | copy-done | bytes 4194328
  17.3 0.0 copy-start.5
  17.3 2.8 %copy-done.5 = bf16[4096,3,256]{2,0,1:T(8,128)(2,1)S(1)} copy-done((bf16[4096,3,256]{2,0,1:T(8,128)(2,1)S(1)}, bf16[4096,3,256]{2,0,1:T(8,128)(2,1)}, u32[]{:S(2)}) %copy-start.5) | copy-done | bytes 6291480
  20.1 4.1 %vocab_share.2.own_ref = f32[512,384]{1,0:T(8,128)S(1)} custom-call(s32[1]{0:T(128)} %bitcast.1.half_ref.place_ref, bf16[512,4096]{1,0:T(8,128)(2,1)S(1)} %copy-done.2, bf16[1,4096]{1,0:T(2,128)(2,1)S(1)} %broadcast_in_dim.7.gain_ref, bf16[3,4096,256]{2,1,0:T(8,128)(2,1)S(1)} %bitcast.5), custom_call_target="tpu_custom_call" | custom-call | flops 1610612736 | bytes 7340032 | tf_op jit(solution)/shard_map/vocab_share/pallas_call | solution.py:154
  24.1 0.0 copy-done
  24.2 0.0 copy-start.3
  24.2 0.0 collective-permute-done
  24.2 0.0 copy-done.7
  24.2 21.8 %all_gather.3 = s32[2,2048]{1,0:T(2,128)S(1)} all-gather(s32[2,128]{1,0:T(2,128)S(1)} %add_select_fusion), channel_id=1, replica_groups=mesh['seq'=16,'wt'=2] {'seq'}, dimensions={1}, use_global_device_ids=true | all-gather | bytes 17408 | tf_op jit(solution)/shard_map/all_gather | solution.py:368
  46.0 0.0 collective-permute-done.2.sq_got_ref
  46.0 0.0 collective-permute-done.1.got_ref
  46.0 8.1 %mixer.1 = bf16[16,2,128,128]{3,2,1,0:T(8,128)(2,1)S(1)} custom-call(s32[1]{0:T(128)} %bitcast.1.half_ref.place_ref, s32[2,1,2048]{2,1,0:T(1,128)S(1)} %broadcast_in_dim.6.tok_ref, f32[512,384]{1,0:T(8,128)S(1)} %vocab_share.2.own_ref, bf16[512,384]{1,0:T(8,128)(2,1)S(1)} %collective-permute-done.1.got_ref, f32[1,512]{1,0:T(1,128)S(1)} %get-tuple-element.8.sq_ref, ...), custom_call_target="tpu_custom_call" | custom-call | flops 1610612736 | bytes 2228224 | tf_op jit(solution)/shard_map/mixer/pallas_call | solution.py:253
  54.2 27.4 %all_to_all.5.mine_ref = bf16[16,2,128,128]{3,2,1,0:T(8,128)(2,1)S(1)} all-to-all(bf16[16,2,128,128]{3,2,1,0:T(8,128)(2,1)S(1)} %mixer.1), channel_id=1, replica_groups=mesh['seq'=16,'wt'=2] {'seq'}, dimensions={0} | all-to-all | bytes 2097152 | tf_op jit(solution)/shard_map/all_to_all | solution.py:375
  81.6 0.5 collective-permute-start.3
  82.1 25.3 %collective-permute-done.3.other_ref = bf16[16,2,128,128]{3,2,1,0:T(8,128)(2,1)S(1)} collective-permute-done((bf16[16,2,128,128]{3,2,1,0:T(8,128)(2,1)S(1)}, bf16[16,2,128,128]{3,2,1,0:T(8,128)(2,1)S(1)}, u32[]{:S(2)}, u32[]{:S(2)}) %collective-permute-start.3) | collective-permute-done | bytes 1048608 | tf_op jit(solution)/shard_map/ppermute | solution.py:346
  107.5 0.0 copy-done.3
  107.5 17.9 %project.1 = bf16[2,128,4096]{2,1,0:T(8,128)(2,1)} custom-call(s32[1,256]{1,0:T(1,128)S(1)} %bitcast.6, bf16[16,2,128,128]{3,2,1,0:T(8,128)(2,1)S(1)} %all_to_all.5.mine_ref, bf16[16,2,128,128]{3,2,1,0:T(8,128)(2,1)S(1)} %collective-permute-done.3.other_ref, bf16[512,4096]{1,0:T(8,128)(2,1)S(1)} %copy-done.3, bf16[4096,4096]{1,0:T(8,128)(2,1)} %w_ref.1), custom_call_target="tpu_custom_call" | custom-call | flops 9663676416 | bytes 39845888 | tf_op jit(solution)/shard_map/project/pallas_call | solution.py:319
  (6 shorter events, 0.1 us)
Async XLA Ops:
  0.0 24.2 %copy-start = (bf16[16,128]{1,0:T(8,128)(2,1)S(1)}, bf16[16,128]{1,0:T(8,128)(2,1)}, u32[]{:S(2)}) copy-start(bf16[16,128]{1,0:T(8,128)(2,1)} %param.12) | copy-start | bytes 12292
  0.0 15.1 %copy-start.6 = (bf16[3,3,256]{2,1,0:T(4,128)(2,1)S(1)}, bf16[3,3,256]{2,1,0:T(4,128)(2,1)}, u32[]{:S(2)}) copy-start(bf16[3,3,256]{2,1,0:T(4,128)(2,1)} %param.11) | copy-start | bytes 13828
  0.0 24.2 %collective-permute-start = (s32[1,128]{1,0:T(1,128)}, s32[1,128]{1,0:T(1,128)S(1)}, u32[]{:S(2)}, u32[]{:S(2)}) collective-permute-start(s32[1,128]{1,0:T(1,128)} %param.7), channel_id=1, source_target_pairs={{0,1},{1,0},{2,3},{3,2},{4,5},{5,4},{6,7},{7,6},{8,9},{9,8},{10,11... | collective-permute-start | bytes 1544 | tf_op jit(solution)/shard_map/ppermute | solution.py:346
  3.7 2.2 %copy-start.1 = (bf16[512,4096]{1,0:T(8,128)(2,1)S(1)}, bf16[512,4096]{1,0:T(8,128)(2,1)}, u32[]{:S(2)}) copy-start(bf16[512,4096]{1,0:T(8,128)(2,1)} %table_ref.1) | copy-start | bytes 12582916
  5.9 2.8 %copy-start.4 = (bf16[4096,3,256]{2,0,1:T(8,128)(2,1)S(1)}, bf16[4096,3,256]{2,0,1:T(8,128)(2,1)}, u32[]{:S(2)}) copy-start(bf16[4096,3,256]{2,0,1:T(8,128)(2,1)} %param.10) | copy-start | bytes 18874372
  13.0 11.3 %copy-start.7 = (s32[1,128]{1,0:T(1,128)S(1)}, s32[1,128]{1,0:T(1,128)}, u32[]{:S(2)}) copy-start(s32[1,128]{1,0:T(1,128)} %param.7) | copy-start | bytes 1540
  13.0 33.1 %collective-permute-start.2 = (f32[1,512]{1,0:T(1,128)S(1)}, f32[1,512]{1,0:T(1,128)S(1)}, u32[]{:S(2)}, u32[]{:S(2)}) collective-permute-start(f32[1,512]{1,0:T(1,128)S(1)} %get-tuple-element.8.sq_ref), channel_id=1, source_target_pairs={{0,1},{1,0},{2,3},{3,2},{4,5},{5,4},{6,7},{7,6},{8,9},{9,8},{10,11... | collective-permute-start | bytes 6152 | tf_op jit(solution)/shard_map/ppermute | solution.py:346
  13.1 33.0 %collective-permute-start.1 = (bf16[512,384]{1,0:T(8,128)(2,1)S(1)}, bf16[512,384]{1,0:T(8,128)(2,1)S(1)}, u32[]{:S(2)}, u32[]{:S(2)}) collective-permute-start(bf16[512,384]{1,0:T(8,128)(2,1)S(1)} %get-tuple-element.7), channel_id=1, source_target_pairs={{0,1},{1,0},{2,3},{3,2},{4,5},{5,4},{6,7},{7,6},{8,9},{9,8},{10,11... | collective-permute-start | bytes 1179656 | tf_op jit(solution)/shard_map/ppermute | solution.py:346
  15.1 2.2 %copy-start.2 = (bf16[512,4096]{1,0:T(8,128)(2,1)S(1)}, bf16[512,4096]{1,0:T(8,128)(2,1)}, u32[]{:S(2)}) copy-start(bf16[512,4096]{1,0:T(8,128)(2,1)} %table_ref.1) | copy-start | bytes 12582916
  17.3 2.8 %copy-start.5 = (bf16[4096,3,256]{2,0,1:T(8,128)(2,1)S(1)}, bf16[4096,3,256]{2,0,1:T(8,128)(2,1)}, u32[]{:S(2)}) copy-start(bf16[4096,3,256]{2,0,1:T(8,128)(2,1)} %param.10) | copy-start | bytes 18874372
  24.2 83.3 %copy-start.3 = (bf16[512,4096]{1,0:T(8,128)(2,1)S(1)}, bf16[512,4096]{1,0:T(8,128)(2,1)}, u32[]{:S(2)}) copy-start(bf16[512,4096]{1,0:T(8,128)(2,1)} %table_ref.1) | copy-start | bytes 12582916
  81.6 25.8 %collective-permute-start.3 = (bf16[16,2,128,128]{3,2,1,0:T(8,128)(2,1)S(1)}, bf16[16,2,128,128]{3,2,1,0:T(8,128)(2,1)S(1)}, u32[]{:S(2)}, u32[]{:S(2)}) collective-permute-start(bf16[16,2,128,128]{3,2,1,0:T(8,128)(2,1)S(1)} %all_to_all.5.mine_ref), channel_id=1, source_target_pairs={{0,1},{1,0},{2,3},{3,2},{4,5},{5,4},{6,7},{7,6},{8,9},{9,8},{10,11... | collective-permute-start | bytes 3145736 | tf_op jit(solution)/shard_map/ppermute | solution.py:346
where the time goes:
time: 126 us; the launch traced here: 125 us
  blocking collectives  49.2 us (39%)
  Pallas kernels  34.4 us (27%)
  waiting for transfers between devices  25.3 us (20%)
  local copies, waits for them, and re-layouts  10.7 us (8%)
  starting transfers between devices  5.57 us (4%)
    all_to_all x1, blocking collectives, shared_block(): mine = lax.all_to_all(gated, 'seq', 0, 0, tiled=True)  27.4 us
    ppermute x4, waiting for transfers between devices, swap_wt(): return lax.ppermute(shard, 'wt', [(0, 1), (1, 0)])  25.3 us
    all_gather x1, blocking collectives, shared_block(): all_tokens = lax.all_gather(both, 'seq', axis=1, tiled=True)  21.8 us
    pallas_call x1, Pallas kernels, project(): pl.pallas_call(functools.partial(project_body, which=None), grid=(feats /...  17.9 us
    unnamed x16, local copies, waits for them, and re-layouts  9.96 us
    pallas_call x2, Pallas kernels, vocab_share(): pl.pallas_call(functools.partial(vocab_share_body, steps=steps, squares=s...  8.36 us
    pallas_call x1, Pallas kernels, mixer(): pl.pallas_call(functools.partial(mixer_body, feature_count=feature_count,...  8.15 us
    ppermute x4, starting transfers between devices, swap_wt(): return lax.ppermute(shard, 'wt', [(0, 1), (1, 0)])  5.57 us
  transfers between devices with their start and end apart: 4, of which 1 were waited for; matrix products, arithmetic and copies ran while one was open for 1% of the time, Pallas kernels for 7%

commit v1 on v0

v1 whole, which is shorter than its diff:
```python
import functools

import jax
import jax.numpy as jnp
from jax import lax
from jax.experimental import pallas as pl
from jax.experimental.pallas import tpu as pltpu
from jax.sharding import PartitionSpec as P

LANES = 128
MIB = 1 << 20


def shifted(shard, axis, by):
    size = lax.axis_size(axis)
    pairs = [(i, i + by) for i in range(size) if 0 <= i + by < size]
    return lax.ppermute(shard, axis, pairs)


def causal_pair(filter_vals):
    tap_count = filter_vals.shape[1]
    group_count = filter_vals.shape[0]
    tiled_taps = jnp.tile(filter_vals, (1, 2 * tap_count - 1)).reshape(
        group_count, tap_count, 2 * tap_count - 1
    )[:, :, :tap_count]
    circulant = jnp.swapaxes(tiled_taps, 1, 2)
    row_pos = lax.broadcasted_iota(jnp.int32, (tap_count, tap_count), 0)
    col_pos = lax.broadcasted_iota(jnp.int32, (tap_count, tap_count), 1)
    lower_mask = (row_pos >= col_pos)[None]
    zero_mat = jnp.zeros_like(circulant)
    return (jnp.where(lower_mask, circulant, zero_mat), jnp.where(lower_mask, zero_mat, circulant))


def short_mix(extended, tap_vals):
    row_count = extended.shape[0] - 2
    ext_vals = extended.astype(jnp.float32)
    return (
        tap_vals[0] * ext_vals[2 : 2 + row_count]
        + tap_vals[1] * ext_vals[1 : 1 + row_count]
        + tap_vals[2] * ext_vals[0:row_count]
    )


def run_filter(extended, lower_mat, upper_mat):
    tap_count = lower_mat.shape[1]
    group_count = lower_mat.shape[0]
    chan_count = extended.shape[1]
    blocks = extended.shape[0] // tap_count
    stacked = extended.reshape(blocks, tap_count, group_count, chan_count // group_count)
    filtered = jnp.einsum(
        "gij,bjgc->bigc", lower_mat, stacked[1:], preferred_element_type=jnp.float32
    )
    filtered = filtered + jnp.einsum(
        "gij,bjgc->bigc", upper_mat, stacked[:-1], preferred_element_type=jnp.float32
    )
    return filtered.reshape((blocks - 1) * tap_count, chan_count)


def plain_block(tokens, embed_table, norm_gain, w_in, short_taps, filters, w_out):
    token_ids = tokens[0]
    own_len = token_ids.shape[0]
    tap_count = filters.shape[1]
    table_vals = embed_table.astype(jnp.float32)
    square_sums = lax.psum(jnp.sum(table_vals * table_vals, axis=1, keepdims=True), "wt")
    feature_count = embed_table.shape[1] * lax.axis_size("wt")
    row_scale = lax.rsqrt(square_sums / feature_count + 1e-06)
    normed = (table_vals * row_scale * norm_gain.astype(jnp.float32)).astype(jnp.bfloat16)
    local_chans = w_in.shape[2]
    w_flat = w_in.reshape(w_in.shape[0], 3 * local_chans)
    vocab_size = embed_table.shape[0]
    partial_sum = jnp.dot(normed, w_flat, preferred_element_type=jnp.float32)
    vocab_flat = lax.psum(partial_sum, "wt").astype(jnp.bfloat16)
    vocab_proj = vocab_flat.reshape(vocab_size, 3, local_chans)
    vocab_all, tap_all, filter_all = (
        lax.all_gather(vocab_proj, "seq", axis=2, tiled=True),
        lax.all_gather(short_taps, "seq", axis=2, tiled=True),
        lax.all_gather(filters, "seq", axis=0, tiled=True),
    )
    projected = jnp.take(vocab_all, token_ids, axis=0)
    edge_prev = shifted(projected[own_len - 2 :], "seq", 1)
    mixture = short_mix(
        jnp.concatenate([edge_prev, projected], axis=0), tap_all.astype(jnp.float32)
    )
    product = (mixture[:, 0] * mixture[:, 2]).astype(jnp.bfloat16)
    tail_prev = shifted(product[own_len - tap_count + 1 :], "seq", 1)
    chan_count = product.shape[1]
    extended = jnp.concatenate(
        [jnp.zeros((1, chan_count), jnp.bfloat16), tail_prev, product], axis=0
    )
    lower_mat, upper_mat = causal_pair(filter_all)
    filtered = run_filter(extended, lower_mat, upper_mat)
    gated = (mixture[:, 1] * filtered).astype(jnp.bfloat16)
    everyone = lax.all_gather(tokens, "wt", axis=0, tiled=True)
    branch = jnp.einsum(
        "knc,dc->knd",
        lax.all_gather(gated[None], "wt", axis=0, tiled=True),
        w_out,
        preferred_element_type=jnp.float32,
    )
    embedded = jnp.take(embed_table, everyone, axis=0)
    return (embedded.astype(jnp.float32) + branch).astype(jnp.bfloat16)


def vocab_share_body(half_ref, gain_ref, *refs, slabs, steps, squares):
    embs, weights = refs[:slabs], refs[slabs : 2 * slabs]
    out_ref = refs[2 * slabs]
    if squares:
        sq_ref, acc_ref, sq_acc = refs[2 * slabs + 1 :]
    else:
        acc_ref = refs[2 * slabs + 1]
    step = pl.program_id(0)
    depth = embs[0].shape[1]
    term = part = None
    for j in range(slabs):
        emb = embs[j][...]
        at = pl.multiple_of((step * slabs + j) * depth, LANES)
        scaled = emb * gain_ref[pl.ds(at, depth)][None]
        wide = jnp.concatenate([weights[j][s] for s in range(weights[j].shape[0])], axis=1)
        more = jnp.dot(scaled, wide, preferred_element_type=jnp.float32)
        term = more if term is None else term + more
        if squares:
            vals = emb.astype(jnp.float32)
            vals = vals * vals
            for i in range(depth // LANES):
                piece = vals[:, i * LANES : (i + 1) * LANES]
                part = piece if part is None else part + piece

    @pl.when(step == 0)
    def _():
        acc_ref[...] = term
        if squares:
            sq_acc[...] = part

    @pl.when(step > 0)
    def _():
        acc_ref[...] += term
        if squares:
            sq_acc[...] += part

    @pl.when(step == steps - 1)
    def _():
        out_ref[...] = acc_ref[...].astype(out_ref.dtype)
        if squares:
            sq_ref[...] = jnp.sum(sq_acc[...].T, axis=0, keepdims=True)


def vocab_share(half, embed_table, norm_gain, w_streams, out_dtype, squares):
    vocab, feats = embed_table.shape
    streams, _, local_chans = w_streams.shape
    chans = local_chans // 2
    slabs, steps = 2, 2
    depth = feats // (slabs * steps)
    width = streams * chans
    out_shape = [jax.ShapeDtypeStruct((vocab, width), out_dtype)]
    out_specs = [pl.BlockSpec((vocab, width), lambda k, h: (0, 0))]
    scratch = [pltpu.VMEM((vocab, width), jnp.float32)]
    if squares:
        out_shape.append(jax.ShapeDtypeStruct((1, vocab), jnp.float32))
        out_specs.append(pl.BlockSpec((1, vocab), lambda k, h: (0, 0)))
        scratch.append(pltpu.VMEM((vocab, LANES), jnp.float32))
    emb_spec = lambda j: pl.BlockSpec((vocab, depth), lambda k, h: (0, k * slabs + j))
    w_spec = lambda j: pl.BlockSpec((streams, depth, chans), lambda k, h: (0, k * slabs + j, h[0]))
    return pl.pallas_call(
        functools.partial(vocab_share_body, slabs=slabs, steps=steps, squares=squares),
        grid_spec=pltpu.PrefetchScalarGridSpec(
            num_scalar_prefetch=1,
            grid=(steps,),
            in_specs=[pl.BlockSpec((feats,), lambda k, h: (0,))]
            + [emb_spec(j) for j in range(slabs)]
            + [w_spec(j) for j in range(slabs)],
            out_specs=out_specs,
            scratch_shapes=scratch,
        ),
        out_shape=out_shape,
        compiler_params=pltpu.CompilerParams(vmem_limit_bytes=60 * MIB),
        cost_estimate=pl.CostEstimate(
            flops=2 * vocab * feats * width,
            bytes_accessed=2 * feats * (vocab + width),
            transcendentals=0,
        ),
        name="vocab_share",
    )(half, norm_gain, *([embed_table] * slabs), *([w_streams] * slabs))


def mixer_body(
    place_ref, tok_ref, own_ref, got_ref, sq_ref, sq_got_ref, taps_ref, filt_ref, *refs,
    feature_count, chunk,
):
    hops = len(refs) - 8
    near, far = refs[:hops], refs[hops]
    vocab_t, toeplitz, tap_cols, carry, prod, gate, conv = refs[hops + 1 :]
    chans = far.shape[-1]
    vocab = vocab_t.shape[1]
    blocks = tok_ref.shape[0]
    groups, taps = filt_ref.shape
    gsz = chans // groups
    length = blocks * taps
    genome = pl.program_id(0)

    @pl.when(genome == 0)
    def _():
        sums = (own_ref[...] + got_ref[...].astype(jnp.float32)).T
        scale = lax.rsqrt((sq_ref[...] + sq_got_ref[...]) / feature_count + 1e-06)
        vocab_t[...] = (sums * scale).astype(jnp.bfloat16)
        row = lax.broadcasted_iota(jnp.int32, (taps, taps), 0)
        col = lax.broadcasted_iota(jnp.int32, (taps, taps), 1)
        filt = filt_ref[...].astype(jnp.float32)
        for g in range(groups):
            circ = pltpu.roll(
                jnp.broadcast_to(filt[g : g + 1], (taps, taps)), 0, 1, stride=1, stride_axis=0
            )
            toeplitz[g, :taps] = jnp.where(col < row, circ, 0.0).astype(jnp.bfloat16)
            toeplitz[g, taps:] = jnp.where(col >= row, circ, 0.0).astype(jnp.bfloat16)
        tap_cols[...] = taps_ref[...].T
        prod[:, :gsz, :] = jnp.zeros((groups, gsz, taps), jnp.bfloat16)

    for k in range(2):
        carry[k] = jnp.zeros(carry.shape[1:], jnp.float32)

    ids = lax.broadcasted_iota(jnp.int32, (vocab, chunk), 0)
    lane = lax.broadcasted_iota(jnp.int32, (chans, LANES), 1)
    per = chunk // taps
    for n in range(length // chunk):
        toks = jnp.concatenate(
            [tok_ref[n * per + b, pl.ds(genome, 1), :] for b in range(per)], axis=1
        )
        picks = jnp.where(ids == toks, 1.0, 0.0)
        proj = jnp.dot(vocab_t[...], picks.astype(jnp.bfloat16), preferred_element_type=jnp.float32)
        mixed = []
        for s in range(3):
            cur = proj[s * chans : (s + 1) * chans]
            total = tap_cols[:, s : s + 1] * cur
            for k in (1, 2):
                back = pltpu.roll(cur, k, 1)
                head = jnp.where(lane < k, carry[k - 1, s], back[:, :LANES])
                carry[k - 1, s] = back[:, :LANES]
                back = jnp.concatenate([head, back[:, LANES:]], axis=1)
                total = total + tap_cols[:, 3 * k + s : 3 * k + s + 1] * back
            mixed.append(total)
        inner = (mixed[0] * mixed[2]).astype(jnp.bfloat16)
        for b in range(per):
            gate[n * per + b] = mixed[1][:, b * taps : (b + 1) * taps]
            at = (n * per + b + 1) * gsz
            for g in range(groups):
                prod[g, at : at + gsz, :] = inner[g * gsz : (g + 1) * gsz, b * taps : (b + 1) * taps]
    rows = blocks * gsz
    for g in range(groups):
        pair = jnp.concatenate([prod[g, :rows], prod[g, gsz : gsz + rows]], axis=1)
        conv[g] = jnp.dot(pair, toeplitz[g], preferred_element_type=jnp.float32)
    for r in range(blocks):
        b = place_ref[0] ^ r
        at = pl.ds(pl.multiple_of(b * gsz, gsz), gsz)
        filtered = jnp.concatenate([conv[g, at, :] for g in range(groups)], axis=0)
        gated = (gate[b] * filtered).T.astype(jnp.bfloat16)
        if r & 2:
            far[r >> 2, r & 1, 0] = gated
        else:
            near[r >> 2][r & 1, 0] = gated


def mixer(place, tokens, own, got, squares, squares_got, taps_rows, filt, feature_count):
    blocks, genomes, taps = tokens.shape
    vocab, width = own.shape
    chans = width // 3
    groups, _ = filt.shape
    gsz = chans // groups
    hops = blocks // 4
    length = blocks * taps
    whole = lambda *shape: pl.BlockSpec(shape, lambda g, p: (0,) * len(shape))
    near_shape = (2, genomes, taps, chans)
    return pl.pallas_call(
        functools.partial(mixer_body, feature_count=feature_count, chunk=2 * taps),
        grid_spec=pltpu.PrefetchScalarGridSpec(
            num_scalar_prefetch=1,
            grid=(genomes,),
            in_specs=[
                whole(blocks, genomes, taps),
                whole(vocab, width),
                whole(vocab, width),
                whole(1, vocab),
                whole(1, vocab),
                whole(*taps_rows.shape),
                whole(groups, taps),
            ],
            out_specs=[pl.BlockSpec((2, 1, taps, chans), lambda g, p: (0, g, 0, 0))] * hops
            + [pl.BlockSpec((hops, 2, 1, taps, chans), lambda g, p: (0, 0, g, 0, 0))],
            scratch_shapes=[
                pltpu.VMEM((width, vocab), jnp.bfloat16),
                pltpu.VMEM((groups, 2 * taps, taps), jnp.bfloat16),
                pltpu.VMEM((chans, taps_rows.shape[0]), jnp.float32),
                pltpu.VMEM((2, 3, chans, LANES), jnp.float32),
                pltpu.VMEM((groups, (blocks + 1) * gsz, taps), jnp.bfloat16),
                pltpu.VMEM((blocks, chans, taps), jnp.float32),
                pltpu.VMEM((groups, blocks * gsz, taps), jnp.float32),
            ],
        ),
        out_shape=[jax.ShapeDtypeStruct(near_shape, jnp.bfloat16)] * hops
        + [jax.ShapeDtypeStruct((hops,) + near_shape, jnp.bfloat16)],
        compiler_params=pltpu.CompilerParams(vmem_limit_bytes=26 * MIB),
        cost_estimate=pl.CostEstimate(
            flops=2 * genomes * length * vocab * width,
            bytes_accessed=6 * vocab * width + 2 * genomes * length * chans,
            transcendentals=0,
        ),
        name="mixer",
    )(place, tokens, own, got, squares, squares_got, taps_rows, filt)


def project_body(place_ref, *refs, hops, first):
    mine, other, cross = refs[:hops], refs[hops : 2 * hops], refs[2 * hops]
    weights = refs[2 * hops + 1 : 3 * hops + 1]
    rest = refs[3 * hops + 1 :]
    chans = cross.shape[-1]
    genomes, rows = cross.shape[1:3]
    if first:
        tok_ref, table_ref, out_ref, gated, picks = rest
    else:
        acc_ref, out_ref, gated = rest

    @pl.when(pl.program_id(0) == 0)
    def _():
        core, plane = place_ref[0] & 1, place_ref[1]
        for j in range(hops):
            pieces = (
                (mine[j], 0, core, plane),
                (other[j], 0, core, 1 - plane),
                (cross, j, 1 - core, plane),
                (cross, hops + j, 1 - core, 1 - plane),
            )
            for ref, lead, from_core, from_plane in pieces:
                at = (2 * from_core + from_plane) * chans
                lanes = pl.ds(pl.multiple_of(at, LANES), chans)
                for g in range(genomes):
                    gated[j, g * rows : (g + 1) * rows, lanes] = ref[lead, g]
        if first:
            vocab = table_ref.shape[0]
            toks = tok_ref[place_ref[0]]
            toks = jnp.concatenate([toks[g : g + 1] for g in range(genomes)], axis=1)
            ids = lax.broadcasted_iota(jnp.int32, (vocab, genomes * rows), 0)
            picks[...] = jnp.where(ids == toks, 1.0, 0.0).T.astype(jnp.bfloat16)

    if first:
        total = jnp.dot(picks[...], table_ref[...], preferred_element_type=jnp.float32)
    else:
        total = jnp.concatenate([acc_ref[g] for g in range(genomes)], axis=0)
    for j in range(hops):
        total = total + lax.dot_general(
            gated[j], weights[j][...], (((1,), (1,)), ((), ())), preferred_element_type=jnp.float32
        )
    for g in range(genomes):
        out_ref[g] = total[g * rows : (g + 1) * rows].astype(out_ref.dtype)


def project(place, mine, other, cross, side, w_out, start, out_dtype):
    hops = len(mine)
    columns = [2 * k + side for k in range(hops)]
    other = [other[k] for k in range(hops)]
    first = isinstance(start, tuple)
    _, genomes, rows, chans = cross.shape
    feats = w_out.shape[0]
    tile = 1024
    whole = lambda a: pl.BlockSpec(a.shape, lambda f, p: (0,) * a.ndim)
    slab = pl.BlockSpec((genomes, rows, tile), lambda f, p: (0, 0, f))
    w_spec = lambda c: pl.BlockSpec((tile, 4 * chans), lambda f, p: (f, (p[0] >> 1) ^ c))
    in_specs = [whole(a) for a in mine + other] + [whole(cross)] + [w_spec(c) for c in columns]
    operands = mine + other + [cross] + [w_out] * hops
    scratch = [pltpu.VMEM((hops, genomes * rows, 4 * chans), jnp.bfloat16)]
    depth = hops * 4 * chans
    if first:
        tokens, table = start
        vocab = table.shape[0]
        in_specs += [whole(tokens), pl.BlockSpec((vocab, tile), lambda f, p: (0, f))]
        scratch.append(pltpu.VMEM((genomes * rows, vocab), jnp.bfloat16))
        operands += [tokens, table]
        depth += vocab
    else:
        in_specs.append(slab)
        operands.append(start)
    return pl.pallas_call(
        functools.partial(project_body, hops=hops, first=first),
        grid_spec=pltpu.PrefetchScalarGridSpec(
            num_scalar_prefetch=1,
            grid=(feats // tile,),
            in_specs=in_specs,
            out_specs=slab,
            scratch_shapes=scratch,
        ),
        out_shape=jax.ShapeDtypeStruct((genomes, rows, feats), out_dtype),
        compiler_params=pltpu.CompilerParams(vmem_limit_bytes=26 * MIB),
        cost_estimate=pl.CostEstimate(
            flops=2 * genomes * rows * feats * depth,
            bytes_accessed=2 * feats * depth + 6 * genomes * rows * feats,
            transcendentals=0,
        ),
        name="project",
    )(place, *operands)


def swap_wt(shard):
    return lax.ppermute(shard, "wt", [(0, 1), (1, 0)])


def swap_seq(shard, step):
    return lax.ppermute(shard, "seq", [(i, i ^ step) for i in range(lax.axis_size("seq"))])


def swap_core(mine, other):
    parts = [a[1] for a in mine] + [other[j, 1] for j in range(len(mine))]
    return swap_seq(jnp.stack(parts), 1)


def gather_tokens(tokens):
    size = lax.axis_size("seq") * lax.axis_size("wt")
    copies = jnp.broadcast_to(tokens[None], (size,) + tokens.shape)
    everyone = lax.all_to_all(copies, ("seq", "wt"), 0, 0, tiled=True)
    return everyone.reshape(lax.axis_size("seq"), lax.axis_size("wt"), tokens.shape[1])


def shared_block(tokens, embed_table, norm_gain, w_in, short_taps, filters, w_out):
    me = lax.axis_index("wt")
    local_chans = w_in.shape[2]
    chans = local_chans // 2
    groups = filters.shape[0] // 2
    feature_count = embed_table.shape[1] * lax.axis_size("wt")
    w_streams = jnp.transpose(w_in, (1, 0, 2))
    place = jnp.stack([lax.axis_index("seq"), me]).astype(jnp.int32)
    pick = lambda which: jnp.reshape(which, (1,)).astype(jnp.int32)
    sent, squares = vocab_share(
        pick(1 - me), embed_table, norm_gain, w_streams, jnp.bfloat16, True
    )
    tokens, sent, squares = lax.optimization_barrier((tokens, sent, squares))
    got = swap_wt(sent)
    squares_got = swap_wt(squares)
    all_tokens = gather_tokens(tokens)
    (own,) = vocab_share(pick(me), embed_table, norm_gain, w_streams, jnp.float32, False)
    taps_rows = lax.dynamic_slice_in_dim(
        short_taps.astype(jnp.float32).reshape(9, local_chans), me * chans, chans, 1
    )
    taps_rows = jnp.pad(taps_rows, ((0, 7), (0, 0)))
    filt = lax.dynamic_slice_in_dim(filters, me * groups, groups, 0)
    *near, far = mixer(
        place, all_tokens, own, got, squares, squares_got, taps_rows, filt, feature_count
    )
    hops = len(near)
    order = sorted(range(1, hops), key=lambda k: (k == 1, k))
    arrived = swap_seq(far, 2)
    near_side = near[:1] + [None] * (hops - 1)
    far_side = [arrived[0]] + [None] * (hops - 1)
    for k in order:
        near_side[k] = swap_seq(near[k], 4 * k)
    for k in order:
        far_side[k] = swap_seq(arrived[k], 4 * k)
    near_other = swap_wt(jnp.stack(near_side))
    near_cross = swap_core(near_side, near_other)
    far_other = swap_wt(jnp.stack(far_side))
    near_cross, _ = lax.optimization_barrier((near_cross, far_side[1]))
    total = project(
        place, near_side, near_other, near_cross, 0, w_out, (all_tokens, embed_table), jnp.float32
    )
    far_other, total = lax.optimization_barrier((far_other, total))
    far_cross = swap_core(far_side, far_other)
    return project(place, far_side, far_other, far_cross, 1, w_out, total, jnp.bfloat16)


def local(*args):
    tokens, embed_table, norm_gain, w_in, short_taps, filters, w_out = args
    ranks = lax.axis_size("seq")
    wide = lax.axis_size("wt") == 2 and w_in.shape[2] == 2 * LANES and ranks in (8, 16, 32)
    aligned = tokens.shape[1] == filters.shape[1] == LANES and w_out.shape[0] % 1024 == 0
    if wide and aligned and tokens.shape[0] == 1:
        return shared_block(*args)
    return plain_block(*args)


def solution(mesh):
    placed = (
        P("wt", "seq"),
        P(None, "wt"),
        P("wt"),
        P("wt", None, "seq"),
        P(None, None, "seq"),
        P("seq", None),
        P("wt", None),
    )
    return jax.shard_map(
        local, mesh=mesh, in_specs=placed, out_specs=P(None, "seq", "wt"), check_vma=False
    )
```

time: 126 us -> 91.5 us (0.73)
  blocking collectives: 49.2 us -> 0 us
  starting transfers between devices: 5.57 us -> 22.7 us
  local copies, waits for them, and re-layouts: 10.7 us -> 2.16 us
  Pallas kernels: 34.4 us -> 41.1 us
    all_to_all x1 -> x0, blocking collectives: 27.4 us -> none  [shared_block(): mine = lax.all_to_all(gated, 'seq', 0, 0, tiled=True)]
    all_gather x1 -> x0, blocking collectives: 21.8 us -> none  [shared_block(): all_tokens = lax.all_gather(both, 'seq', axis=1, tiled=True)]
    ppermute x4, waiting for transfers between devices: 25.3 us -> 9.06 us  [swap_wt(): return lax.ppermute(shard, 'wt', [(0, 1), (1, 0)])]
    ppermute x0 -> x9, waiting for transfers between devices: none -> 15.9 us  [swap_seq(): lax.ppermute(shard, 'seq', [(i, i ^ step) for i in range(lax.axis_size('s...]
    ppermute x0 -> x9, starting transfers between devices: none -> 10.7 us  [swap_seq(): lax.ppermute(shard, 'seq', [(i, i ^ step) for i in range(lax.axis_size('s...]
    unnamed x16 -> x26, local copies, waits for them, and re-layouts: 9.96 us -> 1.34 us
    pallas_call x3 -> x4, Pallas kernels: 26.3 us -> 32.1 us  [the longest x2 20.7 us: project(): pl.pallas_call(functools.partial(project_body, hops=hops, first=first), g...]
    all_to_all x0 -> x1, starting transfers between devices: none -> 4.89 us  [gather_tokens(): everyone = lax.all_to_all(copies, ('seq', 'wt'), 0, 0, tiled=True)]
  transfers between devices with their start and end apart: 4 -> 14, of which waited for: 1 -> 9; matrix products, arithmetic and copies ran while one was open for 1% -> 1% of each run, Pallas kernels for 7% -> 18%
where the time goes in v1:
time: 91.5 us; the launch traced here: 91.3 us
  Pallas kernels  41.1 us (45%)
  waiting for transfers between devices  25 us (27%)
  starting transfers between devices  22.7 us (25%)
  local copies, waits for them, and re-layouts  2.16 us (2%)
    pallas_call x2, Pallas kernels, project(): pl.pallas_call(functools.partial(project_body, hops=hops, first=first), g...  20.7 us
    ppermute x9, waiting for transfers between devices, swap_seq(): lax.ppermute(shard, 'seq', [(i, i ^ step) for i in range(lax.axis_size('s...  15.9 us
    pallas_call x2, Pallas kernels, vocab_share(): pl.pallas_call(functools.partial(vocab_share_body, slabs=slabs, steps=ste...  11.4 us
    ppermute x9, starting transfers between devices, swap_seq(): lax.ppermute(shard, 'seq', [(i, i ^ step) for i in range(lax.axis_size('s...  10.7 us
    ppermute x4, waiting for transfers between devices, swap_wt(): return lax.ppermute(shard, 'wt', [(0, 1), (1, 0)])  9.06 us
    pallas_call x1, Pallas kernels, mixer(): pl.pallas_call(functools.partial(mixer_body, feature_count=feature_count,...  9.04 us
    ppermute x4, starting transfers between devices, swap_wt(): return lax.ppermute(shard, 'wt', [(0, 1), (1, 0)])  7.05 us
    all_to_all x1, starting transfers between devices, gather_tokens(): everyone = lax.all_to_all(copies, ('seq', 'wt'), 0, 0, tiled=True)  4.89 us
  transfers between devices with their start and end apart: 14, of which 9 were waited for; matrix products, arithmetic and copies ran while one was open for 1% of the time, Pallas kernels for 18%

profile of v1, /device:TPU:0, one launch (start us, length us, event | category | flops | bytes accessed | tf_op | source)
XLA Modules:
  0.0 91.3 jit_solution(5401829143699471012)
XLA Ops:
  0.0 0.0 copy-start
  0.0 0.0 copy-start.5
  0.0 5.7 %vocab_share.2 = (bf16[512,384]{1,0:T(8,128)(2,1)}, f32[1,512]{1,0:T(1,128)}) custom-call(s32[1]{0:T(128)} %bitcast.2.half_ref, bf16[4096]{0:T(1024)(128)(2,1)} %gain_ref.3, bf16[512,4096]{1,0:T(8,128)(2,1)} %refs_14_.1, bf16[512,4096]{1,0:T(8,128)(2,1)} %refs_14_.1, bf16[3,4096,256]{2,1,0:T(8,128)(2,1)} %bitcast.74, bf16[3,4096,256]{2,1,0:T(8,128)(2,1)} %bitcast.75), custom_call_target="tpu_custom_call" | custom-call | flops 1610612736 | bytes 7340032 | tf_op jit(solution)/shard_map/vocab_share/pallas_call | solution.py:163
  5.7 3.0 %collective-permute-start.1 = (f32[1,512]{1,0:T(1,128)}, f32[1,512]{1,0:T(1,128)S(1)}, u32[]{:S(2)}, u32[]{:S(2)}) collective-permute-start(f32[1,512]{1,0:T(1,128)} %get-tuple-element.22.sq_ref), channel_id=1, source_target_pairs={{0,1},{1,0},{2,3},{3,2},{4,5},{5,4},{6,7},{7,6},{8,9},{9,8},{10,11... | collective-permute-start | bytes 6152 | tf_op jit(solution)/shard_map/ppermute | solution.py:400
  8.7 0.0 copy-done.5
  8.7 0.6 broadcast_in_dim.9
  9.3 4.9 %all-to-all-start = ((s32[32,1,128]{2,1,0:T(1,128)}), s32[32,1,128]{2,1,0:T(1,128)S(1)}, u32[]{:S(2)}, u32[]{:S(2)}) async-start(s32[32,1,128]{2,1,0:T(1,128)} %broadcast_in_dim.9), calls=%async_computation | async-start | bytes 32768 | tf_op jit(solution)/shard_map/all_to_all | solution.py:415
  14.2 1.8 %collective-permute-start = (bf16[512,384]{1,0:T(8,128)(2,1)}, bf16[512,384]{1,0:T(8,128)(2,1)S(1)}, u32[]{:S(2)}, u32[]{:S(2)}) collective-permute-start(bf16[512,384]{1,0:T(8,128)(2,1)} %get-tuple-element.21), channel_id=1, source_target_pairs={{0,1},{1,0},{2,3},{3,2},{4,5},{5,4},{6,7},{7,6},{8,9},{9,8},{10,11... | collective-permute-start | bytes 1179656 | tf_op jit(solution)/shard_map/ppermute | solution.py:400
  16.0 0.0 copy-done
  16.0 0.0 copy-done.4
  16.1 0.0 copy-start.3
  16.1 5.7 %vocab_share.3.own_ref = f32[512,384]{1,0:T(8,128)} custom-call(s32[1]{0:T(128)} %bitcast.1.half_ref, bf16[4096]{0:T(1024)(128)(2,1)} %gain_ref.3, bf16[512,4096]{1,0:T(8,128)(2,1)} %refs_14_.1, bf16[512,4096]{1,0:T(8,128)(2,1)} %refs_14_.1, bf16[3,4096,256]{2,1,0:T(8,128)(2,1)} %bitcast.76, bf16[3,4096,256]{2,1,0:T(8,128)(2,1)} %bitcast.77), custom_call_target="tpu_custom_call" | custom-call | flops 1610612736 | bytes 7340032 | tf_op jit(solution)/shard_map/vocab_share/pallas_call | solution.py:163
  21.7 0.1 pad_add_fusion.place_ref
  21.8 0.0 collective-permute-done.1.sq_got_ref
  21.8 0.0 all-to-all-done
  21.8 4.1 %collective-permute-done.got_ref = bf16[512,384]{1,0:T(8,128)(2,1)S(1)} collective-permute-done((bf16[512,384]{1,0:T(8,128)(2,1)}, bf16[512,384]{1,0:T(8,128)(2,1)S(1)}, u32[]{:S(2)}, u32[]{:S(2)}) %collective-permute-start) | collective-permute-done | bytes 393248 | tf_op jit(solution)/shard_map/ppermute | solution.py:400
  25.9 0.0 copy-done.3
  25.9 1.1 %copy-done.2 = f32[512,384]{1,0:T(8,128)S(1)} copy-done((f32[512,384]{1,0:T(8,128)S(1)}, f32[512,384]{1,0:T(8,128)}, u32[]{:S(2)}) %copy-start.2) | copy-done | bytes 786456
  27.0 9.0 %mixer.1 = (bf16[2,2,128,128]{3,2,1,0:T(8,128)(2,1)S(1)}, bf16[2,2,128,128]{3,2,1,0:T(8,128)(2,1)S(1)}, bf16[2,2,128,128]{3,2,1,0:T(8,128)(2,1)S(1)}, bf16[2,2,1...) custom-call(s32[2]{0:T(128)S(1)} %pad_add_fusion.place_ref, s32[16,2,128]{2,1,0:T(2,128)S(1)} %bitcast.72, ...), custom_call_target="tpu_custom_call" | custom-call | flops 1610612736 | bytes 2228224 | tf_op jit(solution)/shard_map/mixer/pallas_call | solution.py:271
  36.1 0.0 copy-start.1
  36.1 1.7 %collective-permute-start.7 = (bf16[2,2,128,128]{3,2,1,0:T(8,128)(2,1)S(1)}, bf16[2,2,128,128]{3,2,1,0:T(8,128)(2,1)S(1)}, u32[]{:S(2)}, u32[]{:S(2)}) collective-permute-start(bf16[2,2,128,128]{3,2,1,0:T(8,128)(2,1)S(1)} %get-tuple-element.25), channel_id=1, source_target_pairs={{0,8},{2,10},{4,12},{6,14},{8,0},{10,2},{12,4},{14,6},{16,24},{18,... | collective-permute-start | bytes 393224 | tf_op jit(solution)/shard_map/ppermute | solution.py:404
  37.8 2.4 %collective-permute-start.8 = (bf16[2,2,128,128]{3,2,1,0:T(8,128)(2,1)S(1)}, bf16[2,2,128,128]{3,2,1,0:T(8,128)(2,1)S(1)}, u32[]{:S(2)}, u32[]{:S(2)}) collective-permute-start(bf16[2,2,128,128]{3,2,1,0:T(8,128)(2,1)S(1)} %get-tuple-element.26), channel_id=1, source_target_pairs={{0,16},{2,18},{4,20},{6,22},{8,24},{10,26},{12,28},{14,30},{16,0},... | collective-permute-start | bytes 393224 | tf_op jit(solution)/shard_map/ppermute | solution.py:404
  40.2 0.4 collective-permute-start.9
  40.5 1.7 %collective-permute-start.2 = (bf16[4,2,2,128,128]{4,3,2,1,0:T(8,128)(2,1)S(1)}, bf16[4,2,2,128,128]{4,3,2,1,0:T(8,128)(2,1)S(1)}, u32[]{:S(2)}, u32[]{:S(2)}) collective-permute-start(bf16[4,2,2,128,128]{4,3,2,1,0:T(8,128)(2,1)S(1)} %get-tuple-element.23), channel_id=1, source_target_pairs={{0,4},{2,6},{4,0},{6,2},{8,12},{10,14},{12,8},{14,10},{16,20},{18,... | collective-permute-start | bytes 1572872 | tf_op jit(solution)/shard_map/ppermute | solution.py:404
  42.2 0.4 collective-permute-done.7.refs_1_
  42.6 7.7 %collective-permute-done.8.refs_2_ = bf16[2,2,128,128]{3,2,1,0:T(8,128)(2,1)S(1)} collective-permute-done((bf16[2,2,128,128]{3,2,1,0:T(8,128)(2,1)S(1)}, bf16[2,2,128,128]{3,2,1,0:T(8,128)(2,1)S(1)}, u32[]{:S(2)}, u32[]{:S(2)}) %collective-permute-start.8) | collective-permute-done | bytes 131104 | tf_op jit(solution)/shard_map/ppermute | solution.py:404
  50.3 0.0 collective-permute-done.9.refs_3_
  50.3 0.1 pad_maximum_fusion.1
  50.3 1.4 %collective-permute-start.10 = (bf16[4,2,2,128,128]{4,3,2,1,0:T(8,128)(2,1)S(1)}, bf16[4,2,2,128,128]{4,3,2,1,0:T(8,128)(2,1)S(1)}, u32[]{:S(2)}, u32[]{:S(2)}) collective-permute-start(bf16[4,2,2,128,128]{4,3,2,1,0:T(8,128)(2,1)S(1)} %pad_maximum_fusion.1), channel_id=1, source_target_pairs={{0,1},{1,0},{2,3},{3,2},{4,5},{5,4},{6,7},{7,6},{8,9},{9,8},{10,11... | collective-permute-start | bytes 1572872 | tf_op jit(solution)/shard_map/ppermute | solution.py:400
  51.8 1.1 %collective-permute-done.2 = bf16[4,2,2,128,128]{4,3,2,1,0:T(8,128)(2,1)S(1)} collective-permute-done((bf16[4,2,2,128,128]{4,3,2,1,0:T(8,128)(2,1)S(1)}, bf16[4,2,2,128,128]{4,3,2,1,0:T(8,128)(2,1)S(1)}, u32[]{:S(2)}, u32[]{:S(2)}) %collective-permute-start.2) | collective-permute-done | bytes 524320 | tf_op jit(solution)/shard_map/ppermute | solution.py:404
  53.0 0.1 fusion.5
  53.1 3.5 %collective-permute-start.5 = (bf16[2,2,128,128]{3,2,1,0:T(8,128)(2,1)S(1)}, bf16[2,2,128,128]{3,2,1,0:T(8,128)(2,1)S(1)}, u32[]{:S(2)}, u32[]{:S(2)}) collective-permute-start(bf16[2,2,128,128]{3,2,1,0:T(8,128)(2,1)S(1)} %get-tuple-element.41), channel_id=1, source_target_pairs={{0,24},{2,26},{4,28},{6,30},{8,16},{10,18},{12,20},{14,22},{16,8},... | collective-permute-start | bytes 393224 | tf_op jit(solution)/shard_map/ppermute | solution.py:404
  56.5 0.0 collective-permute-start.4
  56.5 1.0 %collective-permute-start.3 = (bf16[2,2,128,128]{3,2,1,0:T(8,128)(2,1)S(1)}, bf16[2,2,128,128]{3,2,1,0:T(8,128)(2,1)S(1)}, u32[]{:S(2)}, u32[]{:S(2)}) collective-permute-start(bf16[2,2,128,128]{3,2,1,0:T(8,128)(2,1)S(1)} %get-tuple-element.43), channel_id=1, source_target_pairs={{0,8},{2,10},{4,12},{6,14},{8,0},{10,2},{12,4},{14,6},{16,24},{18,... | collective-permute-start | bytes 393224 | tf_op jit(solution)/shard_map/ppermute | solution.py:404
  57.5 3.1 %collective-permute-done.10 = bf16[4,2,2,128,128]{4,3,2,1,0:T(8,128)(2,1)S(1)} collective-permute-done((bf16[4,2,2,128,128]{4,3,2,1,0:T(8,128)(2,1)S(1)}, bf16[4,2,2,128,128]{4,3,2,1,0:T(8,128)(2,1)S(1)}, u32[]{:S(2)}, u32[]{:S(2)}) %collective-permute-start.10) | collective-permute-done | bytes 524320 | tf_op jit(solution)/shard_map/ppermute | solution.py:400
  60.7 0.1 collective-permute-start.11
  60.8 0.4 collective-permute-done.5.refs_3_
  61.2 4.5 %collective-permute-done.4.refs_2_ = bf16[2,2,128,128]{3,2,1,0:T(8,128)(2,1)S(1)} collective-permute-done((bf16[2,2,128,128]{3,2,1,0:T(8,128)(2,1)S(1)}, bf16[2,2,128,128]{3,2,1,0:T(8,128)(2,1)S(1)}, u32[]{:S(2)}, u32[]{:S(2)}) %collective-permute-start.4) | collective-permute-done | bytes 131104 | tf_op jit(solution)/shard_map/ppermute | solution.py:404
  65.7 0.0 collective-permute-done.3.refs_1_
  65.7 0.1 pad_maximum_fusion
  65.8 0.8 collective-permute-start.6
  66.7 0.0 collective-permute-done.11.refs_8_
  66.7 0.0 copy-done.1
  66.7 10.4 %project.2.refs_13_ = f32[2,128,4096]{2,1,0:T(8,128)S(1)} custom-call(s32[2]{0:T(128)S(1)} %pad_add_fusion.place_ref, bf16[2,2,128,128]{3,2,1,0:T(8,128)(2,1)S(1)} %get-tuple-element.24.refs_0_, bf16[2,2,128,128]{3,2,1,0:T(8,128)(2,1)S(1)} %collective-permute-done.7.refs_1_, bf16[2,2,128,128]{3,2,1,0:T(8,128)(2,1)S(1)} %collective-permute-done.8.refs_2_, ...), custom_call_target="tpu_custom_call" | custom-call | flops 5368709120 | bytes 27262976 | tf_op jit(solution)/shard_map/project/pallas_call | solution.py:379
  77.1 1.8 %collective-permute-done.6 = bf16[4,2,2,128,128]{4,3,2,1,0:T(8,128)(2,1)S(1)} collective-permute-done((bf16[4,2,2,128,128]{4,3,2,1,0:T(8,128)(2,1)S(1)}, bf16[4,2,2,128,128]{4,3,2,1,0:T(8,128)(2,1)S(1)}, u32[]{:S(2)}, u32[]{:S(2)}) %collective-permute-start.6) | collective-permute-done | bytes 524320 | tf_op jit(solution)/shard_map/ppermute | solution.py:400
  79.0 0.1 collective-permute-start.12
  79.1 1.9 %collective-permute-done.12.refs_8_ = bf16[8,2,128,128]{3,2,1,0:T(8,128)(2,1)S(1)} collective-permute-done((bf16[8,2,128,128]{3,2,1,0:T(8,128)(2,1)S(1)}, bf16[8,2,128,128]{3,2,1,0:T(8,128)(2,1)S(1)}, u32[]{:S(2)}, u32[]{:S(2)}) %collective-permute-start.12) | collective-permute-done | bytes 524320 | tf_op jit(solution)/shard_map/ppermute | solution.py:404
  81.0 10.4 %project.3 = bf16[2,128,4096]{2,1,0:T(8,128)(2,1)} custom-call(s32[2]{0:T(128)S(1)} %pad_add_fusion.place_ref, bf16[2,2,128,128]{3,2,1,0:T(8,128)(2,1)S(1)} %get-tuple-element.40.refs_0_, bf16[2,2,128,128]{3,2,1,0:T(8,128)(2,1)S(1)} %collective-permute-done.3.refs_1_, bf16[2,2,128,128]{3,2,1,0:T(8,128)(2,1)S(1)} %collective-permute-done.4.refs_2_, ...), custom_call_target="tpu_custom_call" | custom-call | flops 4294967296 | bytes 23068672 | tf_op jit(solution)/shard_map/project/pallas_call | solution.py:379
  (24 shorter events, 0.3 us)
Async XLA Ops:
  0.0 16.0 %copy-start = (bf16[16,128]{1,0:T(8,128)(2,1)S(1)}, bf16[16,128]{1,0:T(8,128)(2,1)}, u32[]{:S(2)}) copy-start(bf16[16,128]{1,0:T(8,128)(2,1)} %param.12) | copy-start | bytes 12292
  0.0 8.7 %copy-start.5 = (s32[1,128]{1,0:T(1,128)S(1)}, s32[1,128]{1,0:T(1,128)}, u32[]{:S(2)}) copy-start(s32[1,128]{1,0:T(1,128)} %param.7) | copy-start | bytes 1540
  0.0 16.0 %copy-start.4 = (bf16[3,3,256]{2,1,0:T(4,128)(2,1)S(1)}, bf16[3,3,256]{2,1,0:T(4,128)(2,1)}, u32[]{:S(2)}) copy-start(bf16[3,3,256]{2,1,0:T(4,128)(2,1)} %param.11) | copy-start | bytes 13828
  5.7 16.1 %collective-permute-start.1 = (f32[1,512]{1,0:T(1,128)}, f32[1,512]{1,0:T(1,128)S(1)}, u32[]{:S(2)}, u32[]{:S(2)}) collective-permute-start(f32[1,512]{1,0:T(1,128)} %get-tuple-element.22.sq_ref), channel_id=1, source_target_pairs={{0,1},{1,0},{2,3},{3,2},{4,5},{5,4},{6,7},{7,6},{8,9},{9,8},{10,11... | collective-permute-start | bytes 6152 | tf_op jit(solution)/shard_map/ppermute | solution.py:400
  9.3 12.5 %all-to-all-start = ((s32[32,1,128]{2,1,0:T(1,128)}), s32[32,1,128]{2,1,0:T(1,128)S(1)}, u32[]{:S(2)}, u32[]{:S(2)}) async-start(s32[32,1,128]{2,1,0:T(1,128)} %broadcast_in_dim.9), calls=%async_computation | async-start | bytes 32768 | tf_op jit(solution)/shard_map/all_to_all | solution.py:415
  14.2 11.7 %collective-permute-start = (bf16[512,384]{1,0:T(8,128)(2,1)}, bf16[512,384]{1,0:T(8,128)(2,1)S(1)}, u32[]{:S(2)}, u32[]{:S(2)}) collective-permute-start(bf16[512,384]{1,0:T(8,128)(2,1)} %get-tuple-element.21), channel_id=1, source_target_pairs={{0,1},{1,0},{2,3},{3,2},{4,5},{5,4},{6,7},{7,6},{8,9},{9,8},{10,11... | collective-permute-start | bytes 1179656 | tf_op jit(solution)/shard_map/ppermute | solution.py:400
  16.1 9.8 %copy-start.3 = (f32[1,512]{1,0:T(1,128)S(1)}, f32[1,512]{1,0:T(1,128)}, u32[]{:S(2)}) copy-start(f32[1,512]{1,0:T(1,128)} %get-tuple-element.22.sq_ref) | copy-start | bytes 6148
  25.9 1.1 %copy-start.2 = (f32[512,384]{1,0:T(8,128)S(1)}, f32[512,384]{1,0:T(8,128)}, u32[]{:S(2)}) copy-start(f32[512,384]{1,0:T(8,128)} %vocab_share.3.own_ref) | copy-start | bytes 2359300
  36.1 30.6 %copy-start.1 = (bf16[512,4096]{1,0:T(8,128)(2,1)S(1)}, bf16[512,4096]{1,0:T(8,128)(2,1)}, u32[]{:S(2)}) copy-start(bf16[512,4096]{1,0:T(8,128)(2,1)} %refs_14_.1) | copy-start | bytes 12582916
  36.1 6.5 %collective-permute-start.7 = (bf16[2,2,128,128]{3,2,1,0:T(8,128)(2,1)S(1)}, bf16[2,2,128,128]{3,2,1,0:T(8,128)(2,1)S(1)}, u32[]{:S(2)}, u32[]{:S(2)}) collective-permute-start(bf16[2,2,128,128]{3,2,1,0:T(8,128)(2,1)S(1)} %get-tuple-element.25), channel_id=1, source_target_pairs={{0,8},{2,10},{4,12},{6,14},{8,0},{10,2},{12,4},{14,6},{16,24},{18,... | collective-permute-start | bytes 393224 | tf_op jit(solution)/shard_map/ppermute | solution.py:404
  37.8 12.4 %collective-permute-start.8 = (bf16[2,2,128,128]{3,2,1,0:T(8,128)(2,1)S(1)}, bf16[2,2,128,128]{3,2,1,0:T(8,128)(2,1)S(1)}, u32[]{:S(2)}, u32[]{:S(2)}) collective-permute-start(bf16[2,2,128,128]{3,2,1,0:T(8,128)(2,1)S(1)} %get-tuple-element.26), channel_id=1, source_target_pairs={{0,16},{2,18},{4,20},{6,22},{8,24},{10,26},{12,28},{14,30},{16,0},... | collective-permute-start | bytes 393224 | tf_op jit(solution)/shard_map/ppermute | solution.py:404
  40.2 10.1 %collective-permute-start.9 = (bf16[2,2,128,128]{3,2,1,0:T(8,128)(2,1)S(1)}, bf16[2,2,128,128]{3,2,1,0:T(8,128)(2,1)S(1)}, u32[]{:S(2)}, u32[]{:S(2)}) collective-permute-start(bf16[2,2,128,128]{3,2,1,0:T(8,128)(2,1)S(1)} %get-tuple-element.27), channel_id=1, source_target_pairs={{0,24},{2,26},{4,28},{6,30},{8,16},{10,18},{12,20},{14,22},{16,8},... | collective-permute-start | bytes 393224 | tf_op jit(solution)/shard_map/ppermute | solution.py:404
  40.5 12.4 %collective-permute-start.2 = (bf16[4,2,2,128,128]{4,3,2,1,0:T(8,128)(2,1)S(1)}, bf16[4,2,2,128,128]{4,3,2,1,0:T(8,128)(2,1)S(1)}, u32[]{:S(2)}, u32[]{:S(2)}) collective-permute-start(bf16[4,2,2,128,128]{4,3,2,1,0:T(8,128)(2,1)S(1)} %get-tuple-element.23), channel_id=1, source_target_pairs={{0,4},{2,6},{4,0},{6,2},{8,12},{10,14},{12,8},{14,10},{16,20},{18,... | collective-permute-start | bytes 1572872 | tf_op jit(solution)/shard_map/ppermute | solution.py:404
  50.3 10.3 %collective-permute-start.10 = (bf16[4,2,2,128,128]{4,3,2,1,0:T(8,128)(2,1)S(1)}, bf16[4,2,2,128,128]{4,3,2,1,0:T(8,128)(2,1)S(1)}, u32[]{:S(2)}, u32[]{:S(2)}) collective-permute-start(bf16[4,2,2,128,128]{4,3,2,1,0:T(8,128)(2,1)S(1)} %pad_maximum_fusion.1), channel_id=1, source_target_pairs={{0,1},{1,0},{2,3},{3,2},{4,5},{5,4},{6,7},{7,6},{8,9},{9,8},{10,11... | collective-permute-start | bytes 1572872 | tf_op jit(solution)/shard_map/ppermute | solution.py:400
  53.1 8.2 %collective-permute-start.5 = (bf16[2,2,128,128]{3,2,1,0:T(8,128)(2,1)S(1)}, bf16[2,2,128,128]{3,2,1,0:T(8,128)(2,1)S(1)}, u32[]{:S(2)}, u32[]{:S(2)}) collective-permute-start(bf16[2,2,128,128]{3,2,1,0:T(8,128)(2,1)S(1)} %get-tuple-element.41), channel_id=1, source_target_pairs={{0,24},{2,26},{4,28},{6,30},{8,16},{10,18},{12,20},{14,22},{16,8},... | collective-permute-start | bytes 393224 | tf_op jit(solution)/shard_map/ppermute | solution.py:404
  56.5 9.2 %collective-permute-start.4 = (bf16[2,2,128,128]{3,2,1,0:T(8,128)(2,1)S(1)}, bf16[2,2,128,128]{3,2,1,0:T(8,128)(2,1)S(1)}, u32[]{:S(2)}, u32[]{:S(2)}) collective-permute-start(bf16[2,2,128,128]{3,2,1,0:T(8,128)(2,1)S(1)} %get-tuple-element.42), channel_id=1, source_target_pairs={{0,16},{2,18},{4,20},{6,22},{8,24},{10,26},{12,28},{14,30},{16,0},... | collective-permute-start | bytes 393224 | tf_op jit(solution)/shard_map/ppermute | solution.py:404
  56.5 9.2 %collective-permute-start.3 = (bf16[2,2,128,128]{3,2,1,0:T(8,128)(2,1)S(1)}, bf16[2,2,128,128]{3,2,1,0:T(8,128)(2,1)S(1)}, u32[]{:S(2)}, u32[]{:S(2)}) collective-permute-start(bf16[2,2,128,128]{3,2,1,0:T(8,128)(2,1)S(1)} %get-tuple-element.43), channel_id=1, source_target_pairs={{0,8},{2,10},{4,12},{6,14},{8,0},{10,2},{12,4},{14,6},{16,24},{18,... | collective-permute-start | bytes 393224 | tf_op jit(solution)/shard_map/ppermute | solution.py:404
  60.7 6.0 %collective-permute-start.11 = (bf16[8,2,128,128]{3,2,1,0:T(8,128)(2,1)S(1)}, bf16[8,2,128,128]{3,2,1,0:T(8,128)(2,1)S(1)}, u32[]{:S(2)}, u32[]{:S(2)}) collective-permute-start(bf16[8,2,128,128]{3,2,1,0:T(8,128)(2,1)S(1)} %fusion.1), channel_id=1, source_target_pairs={{0,2},{2,0},{4,6},{6,4},{8,10},{10,8},{12,14},{14,12},{16,18},{18,... | collective-permute-start | bytes 1572872 | tf_op jit(solution)/shard_map/ppermute | solution.py:404
  65.8 13.1 %collective-permute-start.6 = (bf16[4,2,2,128,128]{4,3,2,1,0:T(8,128)(2,1)S(1)}, bf16[4,2,2,128,128]{4,3,2,1,0:T(8,128)(2,1)S(1)}, u32[]{:S(2)}, u32[]{:S(2)}) collective-permute-start(bf16[4,2,2,128,128]{4,3,2,1,0:T(8,128)(2,1)S(1)} %pad_maximum_fusion), channel_id=1, source_target_pairs={{0,1},{1,0},{2,3},{3,2},{4,5},{5,4},{6,7},{7,6},{8,9},{9,8},{10,11... | collective-permute-start | bytes 1572872 | tf_op jit(solution)/shard_map/ppermute | solution.py:400
  79.0 2.0 %collective-permute-start.12 = (bf16[8,2,128,128]{3,2,1,0:T(8,128)(2,1)S(1)}, bf16[8,2,128,128]{3,2,1,0:T(8,128)(2,1)S(1)}, u32[]{:S(2)}, u32[]{:S(2)}) collective-permute-start(bf16[8,2,128,128]{3,2,1,0:T(8,128)(2,1)S(1)} %bitcast_dynamic-update-slice_fusion), channel_id=1, source_target_pairs={{0,2},{2,0},{4,6},{6,4},{8,10},{10,8},{12,14},{14,12},{16,18},{18,... | collective-permute-start | bytes 1572872 | tf_op jit(solution)/shard_map/ppermute | solution.py:404

commit v2 on v1

--- a/solution.py
+++ b/solution.py
@@ -8,6 +8,7 @@
 from jax.sharding import PartitionSpec as P
 
 LANES = 128
+SQ_ROWS = 16
 MIB = 1 << 20
 
 
@@ -101,13 +102,20 @@
     return (embedded.astype(jnp.float32) + branch).astype(jnp.bfloat16)
 
 
+def three_parts(vals):
+    parts = []
+    for _ in range(3):
+        parts.append(vals.astype(jnp.bfloat16).astype(jnp.float32))
+        vals = vals - parts[-1]
+    return parts
+
+
 def vocab_share_body(half_ref, gain_ref, *refs, slabs, steps, squares):
     embs, weights = refs[:slabs], refs[slabs : 2 * slabs]
-    out_ref = refs[2 * slabs]
     if squares:
-        sq_ref, acc_ref, sq_acc = refs[2 * slabs + 1 :]
+        tok_ref, out_ref, sq_ref, copies_ref, acc_ref, sq_acc = refs[2 * slabs :]
     else:
-        acc_ref = refs[2 * slabs + 1]
+        out_ref, acc_ref = refs[2 * slabs :]
     step = pl.program_id(0)
     depth = embs[0].shape[1]
     term = part = None
@@ -139,24 +147,40 @@
 
     @pl.when(step == steps - 1)
     def _():
-        out_ref[...] = acc_ref[...].astype(out_ref.dtype)
+        vocab = acc_ref.shape[0]
+        out_ref[:vocab] = acc_ref[...].astype(out_ref.dtype)
         if squares:
-            sq_ref[...] = jnp.sum(sq_acc[...].T, axis=0, keepdims=True)
-
-
-def vocab_share(half, embed_table, norm_gain, w_streams, out_dtype, squares):
+            sums = jnp.sum(sq_acc[...].T, axis=0, keepdims=True)
+            sq_ref[...] = sums
+            tail = jnp.zeros((SQ_ROWS, vocab), jnp.float32)
+            row = lax.broadcasted_iota(jnp.int32, tail.shape, 0)
+            for i, piece in enumerate(three_parts(sums)):
+                tail = jnp.where(row == i, piece, tail)
+            for i in range(vocab // LANES):
+                at = vocab + (i // 2) * SQ_ROWS
+                out_ref[at : at + SQ_ROWS, (i % 2) * LANES : (i % 2 + 1) * LANES] = tail[
+                    :, i * LANES : (i + 1) * LANES
+                ].astype(out_ref.dtype)
+            copies_ref[...] = jnp.broadcast_to(tok_ref[...][None], copies_ref.shape)
+
+
+def vocab_share(half, embed_table, norm_gain, w_streams, out_dtype, tokens=None, ranks=0):
+    squares = tokens is not None
     vocab, feats = embed_table.shape
     streams, _, local_chans = w_streams.shape
     chans = local_chans // 2
     slabs, steps = 2, 2
     depth = feats // (slabs * steps)
     width = streams * chans
-    out_shape = [jax.ShapeDtypeStruct((vocab, width), out_dtype)]
-    out_specs = [pl.BlockSpec((vocab, width), lambda k, h: (0, 0))]
+    whole = lambda *shape: pl.BlockSpec(shape, lambda k, h: (0,) * len(shape))
+    rows = vocab + (SQ_ROWS * vocab // (2 * LANES) if squares else 0)
+    out_shape = [jax.ShapeDtypeStruct((rows, width), out_dtype)]
     scratch = [pltpu.VMEM((vocab, width), jnp.float32)]
+    extra_specs, extra = [], []
     if squares:
+        extra_specs, extra = [whole(*tokens.shape)], [tokens]
         out_shape.append(jax.ShapeDtypeStruct((1, vocab), jnp.float32))
-        out_specs.append(pl.BlockSpec((1, vocab), lambda k, h: (0, 0)))
+        out_shape.append(jax.ShapeDtypeStruct((ranks,) + tokens.shape, tokens.dtype))
         scratch.append(pltpu.VMEM((vocab, LANES), jnp.float32))
     emb_spec = lambda j: pl.BlockSpec((vocab, depth), lambda k, h: (0, k * slabs + j))
     w_spec = lambda j: pl.BlockSpec((streams, depth, chans), lambda k, h: (0, k * slabs + j, h[0]))
@@ -167,28 +191,23 @@
             grid=(steps,),
             in_specs=[pl.BlockSpec((feats,), lambda k, h: (0,))]
             + [emb_spec(j) for j in range(slabs)]
-            + [w_spec(j) for j in range(slabs)],
-            out_specs=out_specs,
+            + [w_spec(j) for j in range(slabs)]
+            + extra_specs,
+            out_specs=[whole(*a.shape) for a in out_shape],
             scratch_shapes=scratch,
         ),
         out_shape=out_shape,
         compiler_params=pltpu.CompilerParams(vmem_limit_bytes=60 * MIB),
-        cost_estimate=pl.CostEstimate(
-            flops=2 * vocab * feats * width,
-            bytes_accessed=2 * feats * (vocab + width),
-            transcendentals=0,
-        ),
         name="vocab_share",
-    )(half, norm_gain, *([embed_table] * slabs), *([w_streams] * slabs))
+    )(half, norm_gain, *([embed_table] * slabs), *([w_streams] * slabs), *extra)
 
 
 def mixer_body(
-    place_ref, tok_ref, own_ref, got_ref, sq_ref, sq_got_ref, taps_ref, filt_ref, *refs,
+    place_ref, tok_ref, own_ref, got_ref, sq_ref, taps_ref, filt_ref, *refs,
     feature_count, chunk,
 ):
-    hops = len(refs) - 8
-    near, far = refs[:hops], refs[hops]
-    vocab_t, toeplitz, tap_cols, carry, prod, gate, conv = refs[hops + 1 :]
+    home, *near, far = refs[:-7]
+    vocab_t, toeplitz, tap_cols, carry, prod, gate, conv = refs[-7:]
     chans = far.shape[-1]
     vocab = vocab_t.shape[1]
     blocks = tok_ref.shape[0]
@@ -199,8 +218,15 @@
 
     @pl.when(genome == 0)
     def _():
-        sums = (own_ref[...] + got_ref[...].astype(jnp.float32)).T
-        scale = lax.rsqrt((sq_ref[...] + sq_got_ref[...]) / feature_count + 1e-06)
+        sums = (own_ref[...] + got_ref[:vocab].astype(jnp.float32)).T
+        tails = []
+        for i in range(vocab // LANES):
+            at = vocab + (i // 2) * SQ_ROWS
+            tail = got_ref[at : at + SQ_ROWS, (i % 2) * LANES : (i % 2 + 1) * LANES]
+            tail = tail.astype(jnp.float32)
+            tails.append(tail[0:1] + tail[1:2] + tail[2:3])
+        squares = sq_ref[...] + jnp.concatenate(tails, axis=1)
+        scale = lax.rsqrt(squares / feature_count + 1e-06)
         vocab_t[...] = (sums * scale).astype(jnp.bfloat16)
         row = lax.broadcasted_iota(jnp.int32, (taps, taps), 0)
         col = lax.broadcasted_iota(jnp.int32, (taps, taps), 1)
@@ -252,13 +278,16 @@
         at = pl.ds(pl.multiple_of(b * gsz, gsz), gsz)
         filtered = jnp.concatenate([conv[g, at, :] for g in range(groups)], axis=0)
         gated = (gate[b] * filtered).T.astype(jnp.bfloat16)
-        if r & 2:
-            far[r >> 2, r & 1, 0] = gated
+        k, dx, dc = r >> 2, (r >> 1) & 1, r & 1
+        if k == 0:
+            home[dx, dc, 0] = gated
+        elif dx == 1:
+            far[k - 1, dc, 0] = gated
         else:
-            near[r >> 2][r & 1, 0] = gated
-
-
-def mixer(place, tokens, own, got, squares, squares_got, taps_rows, filt, feature_count):
+            near[k - 1][dc, 0] = gated
+
+
+def mixer(place, tokens, own, got, squares, taps_rows, filt, feature_count):
     blocks, genomes, taps = tokens.shape
     vocab, width = own.shape
     chans = width // 3
@@ -268,6 +297,7 @@
     length = blocks * taps
     whole = lambda *shape: pl.BlockSpec(shape, lambda g, p: (0,) * len(shape))
     near_shape = (2, genomes, taps, chans)
+    packs = lambda n: pl.BlockSpec((n, 2, 1, taps, chans), lambda g, p: (0, 0, g, 0, 0))
     return pl.pallas_call(
         functools.partial(mixer_body, feature_count=feature_count, chunk=2 * taps),
         grid_spec=pltpu.PrefetchScalarGridSpec(
@@ -276,14 +306,14 @@
             in_specs=[
                 whole(blocks, genomes, taps),
                 whole(vocab, width),
-                whole(vocab, width),
-                whole(1, vocab),
+                whole(*got.shape),
                 whole(1, vocab),
                 whole(*taps_rows.shape),
                 whole(groups, taps),
             ],
-            out_specs=[pl.BlockSpec((2, 1, taps, chans), lambda g, p: (0, g, 0, 0))] * hops
-            + [pl.BlockSpec((hops, 2, 1, taps, chans), lambda g, p: (0, 0, g, 0, 0))],
+            out_specs=[packs(2)]
+            + [pl.BlockSpec((2, 1, taps, chans), lambda g, p: (0, g, 0, 0))] * (hops - 1)
+            + [packs(hops - 1)],
             scratch_shapes=[
                 pltpu.VMEM((width, vocab), jnp.bfloat16),
                 pltpu.VMEM((groups, 2 * taps, taps), jnp.bfloat16),
@@ -294,8 +324,9 @@
                 pltpu.VMEM((groups, blocks * gsz, taps), jnp.float32),
             ],
         ),
-        out_shape=[jax.ShapeDtypeStruct(near_shape, jnp.bfloat16)] * hops
-        + [jax.ShapeDtypeStruct((hops,) + near_shape, jnp.bfloat16)],
+        out_shape=[jax.ShapeDtypeStruct((2,) + near_shape, jnp.bfloat16)]
+        + [jax.ShapeDtypeStruct(near_shape, jnp.bfloat16)] * (hops - 1)
+        + [jax.ShapeDtypeStruct((hops - 1,) + near_shape, jnp.bfloat16)],
         compiler_params=pltpu.CompilerParams(vmem_limit_bytes=26 * MIB),
         cost_estimate=pl.CostEstimate(
             flops=2 * genomes * length * vocab * width,
@@ -303,93 +334,119 @@
             transcendentals=0,
         ),
         name="mixer",
-    )(place, tokens, own, got, squares, squares_got, taps_rows, filt)
-
-
-def project_body(place_ref, *refs, hops, first):
-    mine, other, cross = refs[:hops], refs[hops : 2 * hops], refs[2 * hops]
-    weights = refs[2 * hops + 1 : 3 * hops + 1]
-    rest = refs[3 * hops + 1 :]
+    )(place, tokens, own, got, squares, taps_rows, filt)
+
+
+def project_body(place_ref, *refs, columns, first, last, tile):
+    hops = len(columns)
+    mine, other, cross, w_hbm = refs[:hops], refs[hops : 2 * hops], refs[2 * hops], refs[2 * hops + 1]
+    rest = refs[2 * hops + 2 :]
+    if first:
+        tok_ref, table_ref, out_ref, gated, slabs, arrivals, picks = rest
+    elif last:
+        acc_ref, out_ref, gated, slabs, arrivals, ready, leaving = rest
+    else:
+        acc_ref, out_ref, gated, slabs, arrivals = rest
     chans = cross.shape[-1]
     genomes, rows = cross.shape[1:3]
+    wide = 4 * chans
+    tiles = w_hbm.shape[0] // tile
+    arriving = []
+    for t in range(tiles):
+        for j, c in enumerate(columns):
+            at = pl.multiple_of(((place_ref[0] >> 1) ^ c) * wide, wide)
+            copy = pltpu.make_async_copy(
+                w_hbm.at[pl.ds(t * tile, tile), pl.ds(at, wide)],
+                slabs.at[t, :, pl.ds(j * wide, wide)],
+                arrivals.at[t, j],
+            )
+            copy.start()
+            arriving.append(copy)
+
+    core, plane = place_ref[0] & 1, place_ref[1]
+    for j in range(hops):
+        pieces = (
+            (mine[j], 0, core, plane),
+            (other[j], 0, core, 1 - plane),
+            (cross, j, 1 - core, plane),
+            (cross, hops + j, 1 - core, 1 - plane),
+        )
+        for ref, lead, from_core, from_plane in pieces:
+            at = j * wide + (2 * from_core + from_plane) * chans
+            lanes = pl.ds(pl.multiple_of(at, LANES), chans)
+            for g in range(genomes):
+                gated[g * rows : (g + 1) * rows, lanes] = ref[lead, g]
     if first:
-        tok_ref, table_ref, out_ref, gated, picks = rest
-    else:
-        acc_ref, out_ref, gated = rest
-
-    @pl.when(pl.program_id(0) == 0)
-    def _():
-        core, plane = place_ref[0] & 1, place_ref[1]
+        vocab = table_ref.shape[0]
+        toks = tok_ref[place_ref[0]]
+        toks = jnp.concatenate([toks[g : g + 1] for g in range(genomes)], axis=1)
+        ids = lax.broadcasted_iota(jnp.int32, (vocab, genomes * rows), 0)
+        picks[...] = jnp.where(ids == toks, 1.0, 0.0).T.astype(jnp.bfloat16)
+
+    sending = []
+    for t in range(tiles):
+        at = slice(t * tile, (t + 1) * tile)
         for j in range(hops):
-            pieces = (
-                (mine[j], 0, core, plane),
-                (other[j], 0, core, 1 - plane),
-                (cross, j, 1 - core, plane),
-                (cross, hops + j, 1 - core, 1 - plane),
+            arriving[t * hops + j].wait()
+        total = lax.dot_general(
+            gated[...], slabs[t], (((1,), (1,)), ((), ())), preferred_element_type=jnp.float32
+        )
+        if first:
+            total = total + jnp.dot(
+                picks[...], table_ref[:, at], preferred_element_type=jnp.float32
             )
-            for ref, lead, from_core, from_plane in pieces:
-                at = (2 * from_core + from_plane) * chans
-                lanes = pl.ds(pl.multiple_of(at, LANES), chans)
-                for g in range(genomes):
-                    gated[j, g * rows : (g + 1) * rows, lanes] = ref[lead, g]
-        if first:
-            vocab = table_ref.shape[0]
-            toks = tok_ref[place_ref[0]]
-            toks = jnp.concatenate([toks[g : g + 1] for g in range(genomes)], axis=1)
-            ids = lax.broadcasted_iota(jnp.int32, (vocab, genomes * rows), 0)
-            picks[...] = jnp.where(ids == toks, 1.0, 0.0).T.astype(jnp.bfloat16)
-
-    if first:
-        total = jnp.dot(picks[...], table_ref[...], preferred_element_type=jnp.float32)
-    else:
-        total = jnp.concatenate([acc_ref[g] for g in range(genomes)], axis=0)
-    for j in range(hops):
-        total = total + lax.dot_general(
-            gated[j], weights[j][...], (((1,), (1,)), ((), ())), preferred_element_type=jnp.float32
-        )
-    for g in range(genomes):
-        out_ref[g] = total[g * rows : (g + 1) * rows].astype(out_ref.dtype)
-
-
-def project(place, mine, other, cross, side, w_out, start, out_dtype):
+        for g in range(genomes):
+            part = total[g * rows : (g + 1) * rows]
+            if not first:
+                part = part + acc_ref[g, :, at]
+            if last:
+                ready[g, :, at] = part.astype(ready.dtype)
+            else:
+                out_ref[g, :, at] = part
+        if last:
+            copy = pltpu.make_async_copy(ready.at[:, :, at], out_ref.at[:, :, at], leaving.at[t])
+            copy.start()
+            sending.append(copy)
+    for copy in sending:
+        copy.wait()
+
+
+def project(place, mine, other, cross, columns, w_out, start, last=False):
     hops = len(mine)
-    columns = [2 * k + side for k in range(hops)]
-    other = [other[k] for k in range(hops)]
     first = isinstance(start, tuple)
     _, genomes, rows, chans = cross.shape
     feats = w_out.shape[0]
     tile = 1024
-    whole = lambda a: pl.BlockSpec(a.shape, lambda f, p: (0,) * a.ndim)
-    slab = pl.BlockSpec((genomes, rows, tile), lambda f, p: (0, 0, f))
-    w_spec = lambda c: pl.BlockSpec((tile, 4 * chans), lambda f, p: (f, (p[0] >> 1) ^ c))
-    in_specs = [whole(a) for a in mine + other] + [whole(cross)] + [w_spec(c) for c in columns]
-    operands = mine + other + [cross] + [w_out] * hops
-    scratch = [pltpu.VMEM((hops, genomes * rows, 4 * chans), jnp.bfloat16)]
-    depth = hops * 4 * chans
+    tiles = feats // tile
+    vmem = pl.BlockSpec(memory_space=pltpu.VMEM)
+    anywhere = pl.BlockSpec(memory_space=pl.ANY)
+    operands = mine + other + [cross, w_out]
+    in_specs = [pl.BlockSpec(memory_space=pltpu.SMEM)] + [vmem] * (2 * hops + 1) + [anywhere]
+    scratch = [
+        pltpu.VMEM((genomes * rows, hops * 4 * chans), jnp.bfloat16),
+        pltpu.VMEM((tiles, tile, hops * 4 * chans), jnp.bfloat16),
+        pltpu.SemaphoreType.DMA((tiles, hops)),
+    ]
     if first:
-        tokens, table = start
-        vocab = table.shape[0]
-        in_specs += [whole(tokens), pl.BlockSpec((vocab, tile), lambda f, p: (0, f))]
-        scratch.append(pltpu.VMEM((genomes * rows, vocab), jnp.bfloat16))
-        operands += [tokens, table]
-        depth += vocab
+        operands += list(start)
+        in_specs += [vmem, vmem]
+        scratch.append(pltpu.VMEM((genomes * rows, start[1].shape[0]), jnp.bfloat16))
     else:
-        in_specs.append(slab)
         operands.append(start)
+        in_specs.append(vmem)
+    shape = (genomes, rows, feats)
+    if last:
+        scratch += [pltpu.VMEM(shape, jnp.bfloat16), pltpu.SemaphoreType.DMA((tiles,))]
     return pl.pallas_call(
-        functools.partial(project_body, hops=hops, first=first),
-        grid_spec=pltpu.PrefetchScalarGridSpec(
-            num_scalar_prefetch=1,
-            grid=(feats // tile,),
-            in_specs=in_specs,
-            out_specs=slab,
-            scratch_shapes=scratch,
-        ),
-        out_shape=jax.ShapeDtypeStruct((genomes, rows, feats), out_dtype),
-        compiler_params=pltpu.CompilerParams(vmem_limit_bytes=26 * MIB),
+        functools.partial(project_body, columns=columns, first=first, last=last, tile=tile),
+        in_specs=in_specs,
+        out_specs=anywhere if last else vmem,
+        scratch_shapes=scratch,
+        out_shape=jax.ShapeDtypeStruct(shape, jnp.bfloat16 if last else jnp.float32),
+        compiler_params=pltpu.CompilerParams(vmem_limit_bytes=40 * MIB),
         cost_estimate=pl.CostEstimate(
-            flops=2 * genomes * rows * feats * depth,
-            bytes_accessed=2 * feats * depth + 6 * genomes * rows * feats,
+            flops=2 * genomes * rows * feats * hops * 4 * chans,
+            bytes_accessed=2 * feats * hops * 4 * chans + 6 * genomes * rows * feats,
             transcendentals=0,
         ),
         name="project",
@@ -405,15 +462,7 @@
 
 
 def swap_core(mine, other):
-    parts = [a[1] for a in mine] + [other[j, 1] for j in range(len(mine))]
-    return swap_seq(jnp.stack(parts), 1)
-
-
-def gather_tokens(tokens):
-    size = lax.axis_size("seq") * lax.axis_size("wt")
-    copies = jnp.broadcast_to(tokens[None], (size,) + tokens.shape)
-    everyone = lax.all_to_all(copies, ("seq", "wt"), 0, 0, tiled=True)
-    return everyone.reshape(lax.axis_size("seq"), lax.axis_size("wt"), tokens.shape[1])
+    return swap_seq(jnp.stack([a[1] for a in mine + other]), 1)
 
 
 def shared_block(tokens, embed_table, norm_gain, w_in, short_taps, filters, w_out):
@@ -425,41 +474,51 @@
     w_streams = jnp.transpose(w_in, (1, 0, 2))
     place = jnp.stack([lax.axis_index("seq"), me]).astype(jnp.int32)
     pick = lambda which: jnp.reshape(which, (1,)).astype(jnp.int32)
-    sent, squares = vocab_share(
-        pick(1 - me), embed_table, norm_gain, w_streams, jnp.bfloat16, True
-    )
-    tokens, sent, squares = lax.optimization_barrier((tokens, sent, squares))
+    seqs, planes = lax.axis_size("seq"), lax.axis_size("wt")
+    sent, squares, copies = vocab_share(
+        pick(1 - me), embed_table, norm_gain, w_streams, jnp.bfloat16, tokens, seqs * planes
+    )
     got = swap_wt(sent)
-    squares_got = swap_wt(squares)
-    all_tokens = gather_tokens(tokens)
-    (own,) = vocab_share(pick(me), embed_table, norm_gain, w_streams, jnp.float32, False)
+    all_tokens = lax.all_to_all(copies, ("seq", "wt"), 0, 0, tiled=True)
+    all_tokens = all_tokens.reshape(seqs, planes, tokens.shape[1])
+    (own,) = vocab_share(pick(me), embed_table, norm_gain, w_streams, jnp.float32)
     taps_rows = lax.dynamic_slice_in_dim(
         short_taps.astype(jnp.float32).reshape(9, local_chans), me * chans, chans, 1
     )
     taps_rows = jnp.pad(taps_rows, ((0, 7), (0, 0)))
     filt = lax.dynamic_slice_in_dim(filters, me * groups, groups, 0)
-    *near, far = mixer(
-        place, all_tokens, own, got, squares, squares_got, taps_rows, filt, feature_count
-    )
-    hops = len(near)
+    home, *near, far = mixer(
+        place, all_tokens, own, got, squares, taps_rows, filt, feature_count
+    )
+    hops = len(near) + 1
     order = sorted(range(1, hops), key=lambda k: (k == 1, k))
+    bar = lax.optimization_barrier
     arrived = swap_seq(far, 2)
-    near_side = near[:1] + [None] * (hops - 1)
-    far_side = [arrived[0]] + [None] * (hops - 1)
-    for k in order:
-        near_side[k] = swap_seq(near[k], 4 * k)
-    for k in order:
-        far_side[k] = swap_seq(arrived[k], 4 * k)
-    near_other = swap_wt(jnp.stack(near_side))
-    near_cross = swap_core(near_side, near_other)
-    far_other = swap_wt(jnp.stack(far_side))
-    near_cross, _ = lax.optimization_barrier((near_cross, far_side[1]))
+    home_other = swap_wt(home)
+    near_mine = {k: swap_seq(near[k - 1], 4 * k) for k in order}
+    far_mine = {k: swap_seq(arrived[k - 1], 4 * k) for k in order}
+    crossed = swap_seq(jnp.stack([home[1], home_other[1]]), 2)
+    first_mine, first_other = [home[0]], [home_other[0]]
+    cross = swap_core(first_mine, first_other)
     total = project(
-        place, near_side, near_other, near_cross, 0, w_out, (all_tokens, embed_table), jnp.float32
-    )
-    far_other, total = lax.optimization_barrier((far_other, total))
-    far_cross = swap_core(far_side, far_other)
-    return project(place, far_side, far_other, far_cross, 1, w_out, total, jnp.bfloat16)
+        place, first_mine, first_other, cross, [0], w_out, (all_tokens, embed_table)
+    )
+    near_mine = [near_mine[k] for k in range(1, hops)]
+    near_other = swap_wt(jnp.stack(near_mine))
+    near_mine = [crossed[0]] + near_mine
+    near_other = [crossed[1]] + [near_other[k] for k in range(hops - 1)]
+    cross = swap_core(near_mine, near_other)
+    far_mine = [far_mine[k] for k in range(1, hops)]
+    far_mine, cross = bar((far_mine, cross))
+    far_other = swap_wt(jnp.stack(far_mine))
+    columns = [1] + [2 * k for k in range(1, hops)]
+    total, _ = bar((total, far_mine))
+    total = project(place, near_mine, near_other, cross, columns, w_out, total)
+    far_other, total = bar((far_other, total))
+    far_other = [far_other[k] for k in range(hops - 1)]
+    cross = swap_core(far_mine, far_other)
+    columns = [2 * k + 1 for k in range(1, hops)]
+    return project(place, far_mine, far_other, cross, columns, w_out, total, True)
 
 
 def local(*args):

time: 91.5 us -> 83.6 us (0.914)
  waiting for transfers between devices: 25 us -> 16.5 us
    ppermute x4, waiting for transfers between devices: 9.06 us -> 0.14 us  [swap_wt(): return lax.ppermute(shard, 'wt', [(0, 1), (1, 0)])]
    ppermute x9 -> x11, starting transfers between devices: 10.7 us -> 12.8 us  [swap_seq(): lax.ppermute(shard, 'seq', [(i, i ^ step) for i in range(lax.axis_size('s...]
    ppermute x4, starting transfers between devices: 7.05 us -> 5.65 us  [swap_wt(): return lax.ppermute(shard, 'wt', [(0, 1), (1, 0)])]
    all_to_all x1, waiting for transfers between devices: 0.01 us -> 1.4 us  [shared_block(): all_tokens = lax.all_to_all(copies, ('seq', 'wt'), 0, 0, tiled=True)]
    ppermute x9 -> x11, waiting for transfers between devices: 15.9 us -> 15 us  [swap_seq(): lax.ppermute(shard, 'seq', [(i, i ^ step) for i in range(lax.axis_size('s...]
    pallas_call x2 -> x3, Pallas kernels: 20.7 us -> 20.2 us  [project(): pl.pallas_call(functools.partial(project_body, columns=columns, first=fir...]
  transfers between devices with their start and end apart: 14 -> 16, of which waited for: 9 -> 7; matrix products, arithmetic and copies ran while one was open for 1% -> 1% of each run, Pallas kernels for 18% -> 22%
where the time goes in v2:
time: 83.6 us; the launch traced here: 82.8 us
  Pallas kernels  40.8 us (49%)
  starting transfers between devices  23.3 us (28%)
  waiting for transfers between devices  16.5 us (20%)
  local copies, waits for them, and re-layouts  1.52 us (2%)
    pallas_call x3, Pallas kernels, project(): pl.pallas_call(functools.partial(project_body, columns=columns, first=fir...  20.2 us
    ppermute x11, waiting for transfers between devices, swap_seq(): lax.ppermute(shard, 'seq', [(i, i ^ step) for i in range(lax.axis_size('s...  15 us
    ppermute x11, starting transfers between devices, swap_seq(): lax.ppermute(shard, 'seq', [(i, i ^ step) for i in range(lax.axis_size('s...  12.8 us
    pallas_call x2, Pallas kernels, vocab_share(): pl.pallas_call(functools.partial(vocab_share_body, slabs=slabs, steps=ste...  11.4 us
    pallas_call x1, Pallas kernels, mixer(): pl.pallas_call(functools.partial(mixer_body, feature_count=feature_count,...  9.22 us
    ppermute x4, starting transfers between devices, swap_wt(): return lax.ppermute(shard, 'wt', [(0, 1), (1, 0)])  5.65 us
    all_to_all x1, starting transfers between devices, shared_block(): all_tokens = lax.all_to_all(copies, ('seq', 'wt'), 0, 0, tiled=True)  4.89 us
  transfers between devices with their start and end apart: 16, of which 7 were waited for; matrix products, arithmetic and copies ran while one was open for 1% of the time, Pallas kernels for 22%

profile of v2, /device:TPU:0, one launch (start us, length us, event | category | flops | bytes accessed | tf_op | source)
XLA Modules:
  0.0 82.8 jit_solution(8074555454763878579)
XLA Ops:
  0.0 0.0 copy-start
  0.0 0.0 copy-start.4
  0.0 5.7 %vocab_share.2 = (bf16[544,384]{1,0:T(8,128)(2,1)}, f32[1,512]{1,0:T(1,128)}, s32[32,1,128]{2,1,0:T(1,128)}) custom-call(s32[1]{0:T(128)} %bitcast.2.half_ref, bf16[4096]{0:T(1024)(128)(2,1)} %gain_ref.3, bf16[512,4096]{1,0:T(8,128)(2,1)} %refs_5_.1, bf16[512,4096]{1,0:T(8,128)(2,1)} %refs_5_.1, bf16[3,4096,256]{2,1,0:T(8,128)(2,1)} %bitcast.75, ...), custom_call_target="tpu_custom_call" | custom-call | tf_op jit(solution)/shard_map/vocab_share/pallas_call | solution.py:187
  5.7 3.0 %collective-permute-start = (bf16[544,384]{1,0:T(8,128)(2,1)}, bf16[544,384]{1,0:T(8,128)(2,1)S(1)}, u32[]{:S(2)}, u32[]{:S(2)}) collective-permute-start(bf16[544,384]{1,0:T(8,128)(2,1)} %get-tuple-element.21), channel_id=1, source_target_pairs={{0,1},{1,0},{2,3},{3,2},{4,5},{5,4},{6,7},{7,6},{8,9},{9,8},{10,11... | collective-permute-start | bytes 1253384 | tf_op jit(solution)/shard_map/ppermute | solution.py:457
  8.7 4.9 %all-to-all-start = ((s32[32,1,128]{2,1,0:T(1,128)}), s32[32,1,128]{2,1,0:T(1,128)S(1)}, u32[]{:S(2)}, u32[]{:S(2)}) async-start(s32[32,1,128]{2,1,0:T(1,128)} %get-tuple-element.20), calls=%async_computation | async-start | bytes 32768 | tf_op jit(solution)/shard_map/all_to_all | solution.py:482
  13.6 0.0 copy-done.4
  13.6 0.0 copy-done
  13.7 0.1 pad_add_fusion.place_ref
  13.8 0.0 copy-start.3
  13.8 5.6 %vocab_share.3.own_ref = f32[512,384]{1,0:T(8,128)} custom-call(s32[1]{0:T(128)} %bitcast.1.half_ref, bf16[4096]{0:T(1024)(128)(2,1)} %gain_ref.3, bf16[512,4096]{1,0:T(8,128)(2,1)} %refs_5_.1, bf16[512,4096]{1,0:T(8,128)(2,1)} %refs_5_.1, bf16[3,4096,256]{2,1,0:T(8,128)(2,1)} %bitcast.77, bf16[3,4096,256]{2,1,0:T(8,128)(2,1)} %bitcast.78), custom_call_target="tpu_custom_call" | custom-call | tf_op jit(solution)/shard_map/vocab_share/pallas_call | solution.py:187
  19.4 1.4 %all-to-all-done = s32[32,1,128]{2,1,0:T(1,128)S(1)} async-done(((s32[32,1,128]{2,1,0:T(1,128)}), s32[32,1,128]{2,1,0:T(1,128)S(1)}, u32[]{:S(2)}, u32[]{:S(2)}) %all-to-all-start) | async-done | bytes 16416 | tf_op jit(solution)/shard_map/all_to_all | solution.py:482
  20.8 0.0 collective-permute-done.got_ref
  20.8 0.0 copy-done.3
  20.8 0.0 copy-start.2
  20.8 1.1 %copy-done.2 = f32[512,384]{1,0:T(8,128)S(1)} copy-done((f32[512,384]{1,0:T(8,128)S(1)}, f32[512,384]{1,0:T(8,128)}, u32[]{:S(2)}) %copy-start.2) | copy-done | bytes 786456
  21.9 9.2 %mixer.1 = (bf16[2,2,2,128,128]{4,3,2,1,0:T(8,128)(2,1)S(1)}, bf16[2,2,128,128]{3,2,1,0:T(8,128)(2,1)S(1)}, bf16[2,2,128,128]{3,2,1,0:T(8,128)(2,1)S(1)}, bf16[2...) custom-call(s32[2]{0:T(128)S(1)} %pad_add_fusion.place_ref, s32[16,2,128]{2,1,0:T(2,128)S(1)} %bitcast.73, ...), custom_call_target="tpu_custom_call" | custom-call | flops 1610612736 | bytes 2228224 | tf_op jit(solution)/shard_map/mixer/pallas_call | solution.py:301
  31.2 0.6 collective-permute-start.5
  31.8 1.4 %collective-permute-start.7 = (bf16[2,2,128,128]{3,2,1,0:T(8,128)(2,1)S(1)}, bf16[2,2,128,128]{3,2,1,0:T(8,128)(2,1)S(1)}, u32[]{:S(2)}, u32[]{:S(2)}) collective-permute-start(bf16[2,2,128,128]{3,2,1,0:T(8,128)(2,1)S(1)} %get-tuple-element.25), channel_id=1, source_target_pairs={{0,8},{2,10},{4,12},{6,14},{8,0},{10,2},{12,4},{14,6},{16,24},{18,... | collective-permute-start | bytes 393224 | tf_op jit(solution)/shard_map/ppermute | solution.py:461
  33.2 2.4 %collective-permute-start.8 = (bf16[2,2,128,128]{3,2,1,0:T(8,128)(2,1)S(1)}, bf16[2,2,128,128]{3,2,1,0:T(8,128)(2,1)S(1)}, u32[]{:S(2)}, u32[]{:S(2)}) collective-permute-start(bf16[2,2,128,128]{3,2,1,0:T(8,128)(2,1)S(1)} %get-tuple-element.26), channel_id=1, source_target_pairs={{0,16},{2,18},{4,20},{6,22},{8,24},{10,26},{12,28},{14,30},{16,0},... | collective-permute-start | bytes 393224 | tf_op jit(solution)/shard_map/ppermute | solution.py:461
  35.6 0.6 collective-permute-start.9
  36.2 1.4 %collective-permute-start.1 = (bf16[3,2,2,128,128]{4,3,2,1,0:T(8,128)(2,1)S(1)}, bf16[3,2,2,128,128]{4,3,2,1,0:T(8,128)(2,1)S(1)}, u32[]{:S(2)}, u32[]{:S(2)}) collective-permute-start(bf16[3,2,2,128,128]{4,3,2,1,0:T(8,128)(2,1)S(1)} %get-tuple-element.23), channel_id=1, source_target_pairs={{0,4},{2,6},{4,0},{6,2},{8,12},{10,14},{12,8},{14,10},{16,20},{18,... | collective-permute-start | bytes 1179656 | tf_op jit(solution)/shard_map/ppermute | solution.py:461
  37.6 1.0 %collective-permute-done.7.refs_1_ = bf16[2,2,128,128]{3,2,1,0:T(8,128)(2,1)S(1)} collective-permute-done((bf16[2,2,128,128]{3,2,1,0:T(8,128)(2,1)S(1)}, bf16[2,2,128,128]{3,2,1,0:T(8,128)(2,1)S(1)}, u32[]{:S(2)}, u32[]{:S(2)}) %collective-permute-start.7) | collective-permute-done | bytes 131104 | tf_op jit(solution)/shard_map/ppermute | solution.py:461
  38.6 7.5 %collective-permute-done.8.refs_2_ = bf16[2,2,128,128]{3,2,1,0:T(8,128)(2,1)S(1)} collective-permute-done((bf16[2,2,128,128]{3,2,1,0:T(8,128)(2,1)S(1)}, bf16[2,2,128,128]{3,2,1,0:T(8,128)(2,1)S(1)}, u32[]{:S(2)}, u32[]{:S(2)}) %collective-permute-start.8) | collective-permute-done | bytes 131104 | tf_op jit(solution)/shard_map/ppermute | solution.py:461
  46.1 0.0 collective-permute-done.9.refs_3_
  46.2 0.6 collective-permute-start.10
  46.7 0.0 collective-permute-done.5
  46.8 1.6 %collective-permute-start.6 = (bf16[2,2,2,128,128]{4,3,2,1,0:T(8,128)(2,1)S(1)}, bf16[2,2,2,128,128]{4,3,2,1,0:T(8,128)(2,1)S(1)}, u32[]{:S(2)}, u32[]{:S(2)}) collective-permute-start(bf16[2,2,2,128,128]{4,3,2,1,0:T(8,128)(2,1)S(1)} %pad_maximum_fusion.2), channel_id=1, source_target_pairs={{0,4},{2,6},{4,0},{6,2},{8,12},{10,14},{12,8},{14,10},{16,20},{18,... | collective-permute-start | bytes 786440 | tf_op jit(solution)/shard_map/ppermute | solution.py:461
  48.4 0.1 collective-permute-start.13
  48.5 0.0 collective-permute-done.1
  48.5 2.0 %collective-permute-start.2 = (bf16[2,2,128,128]{3,2,1,0:T(8,128)(2,1)S(1)}, bf16[2,2,128,128]{3,2,1,0:T(8,128)(2,1)S(1)}, u32[]{:S(2)}, u32[]{:S(2)}) collective-permute-start(bf16[2,2,128,128]{3,2,1,0:T(8,128)(2,1)S(1)} %get-tuple-element.43), channel_id=1, source_target_pairs={{0,8},{2,10},{4,12},{6,14},{8,0},{10,2},{12,4},{14,6},{16,24},{18,... | collective-permute-start | bytes 393224 | tf_op jit(solution)/shard_map/ppermute | solution.py:461
  50.6 1.0 %collective-permute-start.3 = (bf16[2,2,128,128]{3,2,1,0:T(8,128)(2,1)S(1)}, bf16[2,2,128,128]{3,2,1,0:T(8,128)(2,1)S(1)}, u32[]{:S(2)}, u32[]{:S(2)}) collective-permute-start(bf16[2,2,128,128]{3,2,1,0:T(8,128)(2,1)S(1)} %get-tuple-element.42), channel_id=1, source_target_pairs={{0,16},{2,18},{4,20},{6,22},{8,24},{10,26},{12,28},{14,30},{16,0},... | collective-permute-start | bytes 393224 | tf_op jit(solution)/shard_map/ppermute | solution.py:461
  51.5 1.7 %collective-permute-done.6 = bf16[2,2,2,128,128]{4,3,2,1,0:T(8,128)(2,1)S(1)} collective-permute-done((bf16[2,2,2,128,128]{4,3,2,1,0:T(8,128)(2,1)S(1)}, bf16[2,2,2,128,128]{4,3,2,1,0:T(8,128)(2,1)S(1)}, u32[]{:S(2)}, u32[]{:S(2)}) %collective-permute-start.6) | collective-permute-done | bytes 262176 | tf_op jit(solution)/shard_map/ppermute | solution.py:461
  53.2 2.2 %collective-permute-start.4 = (bf16[2,2,128,128]{3,2,1,0:T(8,128)(2,1)S(1)}, bf16[2,2,128,128]{3,2,1,0:T(8,128)(2,1)S(1)}, u32[]{:S(2)}, u32[]{:S(2)}) collective-permute-start(bf16[2,2,128,128]{3,2,1,0:T(8,128)(2,1)S(1)} %get-tuple-element.41), channel_id=1, source_target_pairs={{0,24},{2,26},{4,28},{6,30},{8,16},{10,18},{12,20},{14,22},{16,8},... | collective-permute-start | bytes 393224 | tf_op jit(solution)/shard_map/ppermute | solution.py:461
  55.5 0.0 collective-permute-done.10
  55.6 0.1 collective-permute-start.11
  55.7 0.0 collective-permute-done.13.refs_2_
  55.7 0.0 copy-done.1
  55.7 4.7 %project.3.refs_10_ = f32[2,128,4096]{2,1,0:T(8,128)S(1)} custom-call(s32[2]{0:T(128)S(1)} %pad_add_fusion.place_ref, bf16[2,2,128,128]{3,2,1,0:T(8,128)(2,1)S(1)} %get-tuple-element.46.refs_0_, bf16[2,2,128,128]{3,2,1,0:T(8,128)(2,1)S(1)} %get-tuple-element.44.refs_1_, bf16[2,2,128,128]{3,2,1,0:T(8,128)(2,1)S(1)} %collective-permute-done.13.refs_2_, ...), custom_call_target="tpu_custom_call" | custom-call | flops 1073741824 | bytes 10485760 | tf_op jit(solution)/shard_map/project/pallas_call | solution.py:440
  60.4 0.0 collective-permute-done.2.refs_0_
  60.4 3.0 %collective-permute-done.3.refs_1_ = bf16[2,2,128,128]{3,2,1,0:T(8,128)(2,1)S(1)} collective-permute-done((bf16[2,2,128,128]{3,2,1,0:T(8,128)(2,1)S(1)}, bf16[2,2,128,128]{3,2,1,0:T(8,128)(2,1)S(1)}, u32[]{:S(2)}, u32[]{:S(2)}) %collective-permute-start.3) | collective-permute-done | bytes 131104 | tf_op jit(solution)/shard_map/ppermute | solution.py:461
  63.5 0.0 collective-permute-done.4.refs_2_
  63.5 0.0 collective-permute-done.11.refs_8_
  63.6 1.5 %collective-permute-start.12 = (bf16[3,2,2,128,128]{4,3,2,1,0:T(8,128)(2,1)S(1)}, bf16[3,2,2,128,128]{4,3,2,1,0:T(8,128)(2,1)S(1)}, u32[]{:S(2)}, u32[]{:S(2)}) collective-permute-start(bf16[3,2,2,128,128]{4,3,2,1,0:T(8,128)(2,1)S(1)} %pad_maximum_fusion.1), channel_id=1, source_target_pairs={{0,1},{1,0},{2,3},{3,2},{4,5},{5,4},{6,7},{7,6},{8,9},{9,8},{10,11... | collective-permute-start | bytes 1179656 | tf_op jit(solution)/shard_map/ppermute | solution.py:457
  65.1 8.1 %project.4.refs_8_ = f32[2,128,4096]{2,1,0:T(8,128)S(1)} custom-call(s32[2]{0:T(128)S(1)} %pad_add_fusion.place_ref, bf16[2,2,128,128]{3,2,1,0:T(8,128)(2,1)S(1)} %get-tuple-element.49.refs_0_, bf16[2,2,128,128]{3,2,1,0:T(8,128)(2,1)S(1)} %collective-permute-done.7.refs_1_, bf16[2,2,128,128]{3,2,1,0:T(8,128)(2,1)S(1)} %collective-permute-done.8.refs_2_, ...), custom_call_target="tpu_custom_call" | custom-call | flops 4294967296 | bytes 23068672 | tf_op jit(solution)/shard_map/project/pallas_call | solution.py:440
  73.2 0.1 collective-permute-done.12
  73.4 0.1 collective-permute-start.14
  73.5 1.7 %collective-permute-done.14.refs_6_ = bf16[6,2,128,128]{3,2,1,0:T(8,128)(2,1)S(1)} collective-permute-done((bf16[6,2,128,128]{3,2,1,0:T(8,128)(2,1)S(1)}, bf16[6,2,128,128]{3,2,1,0:T(8,128)(2,1)S(1)}, u32[]{:S(2)}, u32[]{:S(2)}) %collective-permute-start.14) | collective-permute-done | bytes 393248 | tf_op jit(solution)/shard_map/ppermute | solution.py:461
  75.2 7.5 %project.5 = bf16[2,128,4096]{2,1,0:T(8,128)(2,1)} custom-call(s32[2]{0:T(128)S(1)} %pad_add_fusion.place_ref, bf16[2,2,128,128]{3,2,1,0:T(8,128)(2,1)S(1)} %collective-permute-done.2.refs_0_, bf16[2,2,128,128]{3,2,1,0:T(8,128)(2,1)S(1)} %collective-permute-done.3.refs_1_, bf16[2,2,128,128]{3,2,1,0:T(8,128)(2,1)S(1)} %collective-permute-done.4.refs_2_, ...), custom_call_target="tpu_custom_call" | custom-call | flops 3221225472 | bytes 18874368 | tf_op jit(solution)/shard_map/project/pallas_call | solution.py:440
  (31 shorter events, 0.5 us)
Async XLA Ops:
  0.0 13.6 %copy-start = (bf16[16,128]{1,0:T(8,128)(2,1)S(1)}, bf16[16,128]{1,0:T(8,128)(2,1)}, u32[]{:S(2)}) copy-start(bf16[16,128]{1,0:T(8,128)(2,1)} %param.12) | copy-start | bytes 12292
  0.0 13.6 %copy-start.4 = (bf16[3,3,256]{2,1,0:T(4,128)(2,1)S(1)}, bf16[3,3,256]{2,1,0:T(4,128)(2,1)}, u32[]{:S(2)}) copy-start(bf16[3,3,256]{2,1,0:T(4,128)(2,1)} %param.11) | copy-start | bytes 13828
  5.7 15.1 %collective-permute-start = (bf16[544,384]{1,0:T(8,128)(2,1)}, bf16[544,384]{1,0:T(8,128)(2,1)S(1)}, u32[]{:S(2)}, u32[]{:S(2)}) collective-permute-start(bf16[544,384]{1,0:T(8,128)(2,1)} %get-tuple-element.21), channel_id=1, source_target_pairs={{0,1},{1,0},{2,3},{3,2},{4,5},{5,4},{6,7},{7,6},{8,9},{9,8},{10,11... | collective-permute-start | bytes 1253384 | tf_op jit(solution)/shard_map/ppermute | solution.py:457
  8.7 12.1 %all-to-all-start = ((s32[32,1,128]{2,1,0:T(1,128)}), s32[32,1,128]{2,1,0:T(1,128)S(1)}, u32[]{:S(2)}, u32[]{:S(2)}) async-start(s32[32,1,128]{2,1,0:T(1,128)} %get-tuple-element.20), calls=%async_computation | async-start | bytes 32768 | tf_op jit(solution)/shard_map/all_to_all | solution.py:482
  13.8 7.0 %copy-start.3 = (f32[1,512]{1,0:T(1,128)S(1)}, f32[1,512]{1,0:T(1,128)}, u32[]{:S(2)}) copy-start(f32[1,512]{1,0:T(1,128)} %get-tuple-element.22.sq_ref) | copy-start | bytes 6148
  20.8 1.1 %copy-start.2 = (f32[512,384]{1,0:T(8,128)S(1)}, f32[512,384]{1,0:T(8,128)}, u32[]{:S(2)}) copy-start(f32[512,384]{1,0:T(8,128)} %vocab_share.3.own_ref) | copy-start | bytes 2359300
  21.9 33.7 %copy-start.1 = (bf16[512,4096]{1,0:T(8,128)(2,1)S(1)}, bf16[512,4096]{1,0:T(8,128)(2,1)}, u32[]{:S(2)}) copy-start(bf16[512,4096]{1,0:T(8,128)(2,1)} %refs_5_.1) | copy-start | bytes 12582916
  31.2 15.6 %collective-permute-start.5 = (bf16[2,2,2,128,128]{4,3,2,1,0:T(8,128)(2,1)S(1)}, bf16[2,2,2,128,128]{4,3,2,1,0:T(8,128)(2,1)S(1)}, u32[]{:S(2)}, u32[]{:S(2)}) collective-permute-start(bf16[2,2,2,128,128]{4,3,2,1,0:T(8,128)(2,1)S(1)} %get-tuple-element.24), channel_id=1, source_target_pairs={{0,1},{1,0},{2,3},{3,2},{4,5},{5,4},{6,7},{7,6},{8,9},{9,8},{10,11... | collective-permute-start | bytes 786440 | tf_op jit(solution)/shard_map/ppermute | solution.py:457
  31.8 6.8 %collective-permute-start.7 = (bf16[2,2,128,128]{3,2,1,0:T(8,128)(2,1)S(1)}, bf16[2,2,128,128]{3,2,1,0:T(8,128)(2,1)S(1)}, u32[]{:S(2)}, u32[]{:S(2)}) collective-permute-start(bf16[2,2,128,128]{3,2,1,0:T(8,128)(2,1)S(1)} %get-tuple-element.25), channel_id=1, source_target_pairs={{0,8},{2,10},{4,12},{6,14},{8,0},{10,2},{12,4},{14,6},{16,24},{18,... | collective-permute-start | bytes 393224 | tf_op jit(solution)/shard_map/ppermute | solution.py:461
  33.2 12.9 %collective-permute-start.8 = (bf16[2,2,128,128]{3,2,1,0:T(8,128)(2,1)S(1)}, bf16[2,2,128,128]{3,2,1,0:T(8,128)(2,1)S(1)}, u32[]{:S(2)}, u32[]{:S(2)}) collective-permute-start(bf16[2,2,128,128]{3,2,1,0:T(8,128)(2,1)S(1)} %get-tuple-element.26), channel_id=1, source_target_pairs={{0,16},{2,18},{4,20},{6,22},{8,24},{10,26},{12,28},{14,30},{16,0},... | collective-permute-start | bytes 393224 | tf_op jit(solution)/shard_map/ppermute | solution.py:461
  35.6 10.5 %collective-permute-start.9 = (bf16[2,2,128,128]{3,2,1,0:T(8,128)(2,1)S(1)}, bf16[2,2,128,128]{3,2,1,0:T(8,128)(2,1)S(1)}, u32[]{:S(2)}, u32[]{:S(2)}) collective-permute-start(bf16[2,2,128,128]{3,2,1,0:T(8,128)(2,1)S(1)} %get-tuple-element.27), channel_id=1, source_target_pairs={{0,24},{2,26},{4,28},{6,30},{8,16},{10,18},{12,20},{14,22},{16,8},... | collective-permute-start | bytes 393224 | tf_op jit(solution)/shard_map/ppermute | solution.py:461
  36.2 12.3 %collective-permute-start.1 = (bf16[3,2,2,128,128]{4,3,2,1,0:T(8,128)(2,1)S(1)}, bf16[3,2,2,128,128]{4,3,2,1,0:T(8,128)(2,1)S(1)}, u32[]{:S(2)}, u32[]{:S(2)}) collective-permute-start(bf16[3,2,2,128,128]{4,3,2,1,0:T(8,128)(2,1)S(1)} %get-tuple-element.23), channel_id=1, source_target_pairs={{0,4},{2,6},{4,0},{6,2},{8,12},{10,14},{12,8},{14,10},{16,20},{18,... | collective-permute-start | bytes 1179656 | tf_op jit(solution)/shard_map/ppermute | solution.py:461
  46.2 9.3 %collective-permute-start.10 = (bf16[3,2,2,128,128]{4,3,2,1,0:T(8,128)(2,1)S(1)}, bf16[3,2,2,128,128]{4,3,2,1,0:T(8,128)(2,1)S(1)}, u32[]{:S(2)}, u32[]{:S(2)}) collective-permute-start(bf16[3,2,2,128,128]{4,3,2,1,0:T(8,128)(2,1)S(1)} %pad_maximum_fusion), channel_id=1, source_target_pairs={{0,1},{1,0},{2,3},{3,2},{4,5},{5,4},{6,7},{7,6},{8,9},{9,8},{10,11... | collective-permute-start | bytes 1179656 | tf_op jit(solution)/shard_map/ppermute | solution.py:457
  46.8 6.4 %collective-permute-start.6 = (bf16[2,2,2,128,128]{4,3,2,1,0:T(8,128)(2,1)S(1)}, bf16[2,2,2,128,128]{4,3,2,1,0:T(8,128)(2,1)S(1)}, u32[]{:S(2)}, u32[]{:S(2)}) collective-permute-start(bf16[2,2,2,128,128]{4,3,2,1,0:T(8,128)(2,1)S(1)} %pad_maximum_fusion.2), channel_id=1, source_target_pairs={{0,4},{2,6},{4,0},{6,2},{8,12},{10,14},{12,8},{14,10},{16,20},{18,... | collective-permute-start | bytes 786440 | tf_op jit(solution)/shard_map/ppermute | solution.py:461
  48.4 7.3 %collective-permute-start.13 = (bf16[2,2,128,128]{3,2,1,0:T(8,128)(2,1)S(1)}, bf16[2,2,128,128]{3,2,1,0:T(8,128)(2,1)S(1)}, u32[]{:S(2)}, u32[]{:S(2)}) collective-permute-start(bf16[2,2,128,128]{3,2,1,0:T(8,128)(2,1)S(1)} %pad_maximum_fusion.3), channel_id=1, source_target_pairs={{0,2},{2,0},{4,6},{6,4},{8,10},{10,8},{12,14},{14,12},{16,18},{18,... | collective-permute-start | bytes 393224 | tf_op jit(solution)/shard_map/ppermute | solution.py:461
  48.5 11.9 %collective-permute-start.2 = (bf16[2,2,128,128]{3,2,1,0:T(8,128)(2,1)S(1)}, bf16[2,2,128,128]{3,2,1,0:T(8,128)(2,1)S(1)}, u32[]{:S(2)}, u32[]{:S(2)}) collective-permute-start(bf16[2,2,128,128]{3,2,1,0:T(8,128)(2,1)S(1)} %get-tuple-element.43), channel_id=1, source_target_pairs={{0,8},{2,10},{4,12},{6,14},{8,0},{10,2},{12,4},{14,6},{16,24},{18,... | collective-permute-start | bytes 393224 | tf_op jit(solution)/shard_map/ppermute | solution.py:461
  50.6 12.9 %collective-permute-start.3 = (bf16[2,2,128,128]{3,2,1,0:T(8,128)(2,1)S(1)}, bf16[2,2,128,128]{3,2,1,0:T(8,128)(2,1)S(1)}, u32[]{:S(2)}, u32[]{:S(2)}) collective-permute-start(bf16[2,2,128,128]{3,2,1,0:T(8,128)(2,1)S(1)} %get-tuple-element.42), channel_id=1, source_target_pairs={{0,16},{2,18},{4,20},{6,22},{8,24},{10,26},{12,28},{14,30},{16,0},... | collective-permute-start | bytes 393224 | tf_op jit(solution)/shard_map/ppermute | solution.py:461
  53.2 10.2 %collective-permute-start.4 = (bf16[2,2,128,128]{3,2,1,0:T(8,128)(2,1)S(1)}, bf16[2,2,128,128]{3,2,1,0:T(8,128)(2,1)S(1)}, u32[]{:S(2)}, u32[]{:S(2)}) collective-permute-start(bf16[2,2,128,128]{3,2,1,0:T(8,128)(2,1)S(1)} %get-tuple-element.41), channel_id=1, source_target_pairs={{0,24},{2,26},{4,28},{6,30},{8,16},{10,18},{12,20},{14,22},{16,8},... | collective-permute-start | bytes 393224 | tf_op jit(solution)/shard_map/ppermute | solution.py:461
  55.6 7.9 %collective-permute-start.11 = (bf16[8,2,128,128]{3,2,1,0:T(8,128)(2,1)S(1)}, bf16[8,2,128,128]{3,2,1,0:T(8,128)(2,1)S(1)}, u32[]{:S(2)}, u32[]{:S(2)}) collective-permute-start(bf16[8,2,128,128]{3,2,1,0:T(8,128)(2,1)S(1)} %fusion), channel_id=1, source_target_pairs={{0,2},{2,0},{4,6},{6,4},{8,10},{10,8},{12,14},{14,12},{16,18},{18,... | collective-permute-start | bytes 1572872 | tf_op jit(solution)/shard_map/ppermute | solution.py:461
  63.6 9.7 %collective-permute-start.12 = (bf16[3,2,2,128,128]{4,3,2,1,0:T(8,128)(2,1)S(1)}, bf16[3,2,2,128,128]{4,3,2,1,0:T(8,128)(2,1)S(1)}, u32[]{:S(2)}, u32[]{:S(2)}) collective-permute-start(bf16[3,2,2,128,128]{4,3,2,1,0:T(8,128)(2,1)S(1)} %pad_maximum_fusion.1), channel_id=1, source_target_pairs={{0,1},{1,0},{2,3},{3,2},{4,5},{5,4},{6,7},{7,6},{8,9},{9,8},{10,11... | collective-permute-start | bytes 1179656 | tf_op jit(solution)/shard_map/ppermute | solution.py:457
  73.4 1.8 %collective-permute-start.14 = (bf16[6,2,128,128]{3,2,1,0:T(8,128)(2,1)S(1)}, bf16[6,2,128,128]{3,2,1,0:T(8,128)(2,1)S(1)}, u32[]{:S(2)}, u32[]{:S(2)}) collective-permute-start(bf16[6,2,128,128]{3,2,1,0:T(8,128)(2,1)S(1)} %bitcast_dynamic-update-slice_fusion), channel_id=1, source_target_pairs={{0,2},{2,0},{4,6},{6,4},{8,10},{10,8},{12,14},{14,12},{16,18},{18,... | collective-permute-start | bytes 1179656 | tf_op jit(solution)/shard_map/ppermute | solution.py:461

commit v3 on v2

--- a/solution.py
+++ b/solution.py
@@ -237,7 +237,9 @@
             )
             toeplitz[g, :taps] = jnp.where(col < row, circ, 0.0).astype(jnp.bfloat16)
             toeplitz[g, taps:] = jnp.where(col >= row, circ, 0.0).astype(jnp.bfloat16)
-        tap_cols[...] = taps_ref[...].T
+        cols = taps_ref[...].T
+        for i in range(9):
+            tap_cols[i] = jnp.broadcast_to(cols[:, i : i + 1], (chans, LANES))
         prod[:, :gsz, :] = jnp.zeros((groups, gsz, taps), jnp.bfloat16)
 
     for k in range(2):
@@ -255,13 +257,19 @@
         mixed = []
         for s in range(3):
             cur = proj[s * chans : (s + 1) * chans]
-            total = tap_cols[:, s : s + 1] * cur
+            wide = lambda i: jnp.concatenate([tap_cols[i]] * per, axis=1)
+            total = wide(s) * cur
+            backs = []
             for k in (1, 2):
-                back = pltpu.roll(cur, k, 1)
-                head = jnp.where(lane < k, carry[k - 1, s], back[:, :LANES])
-                carry[k - 1, s] = back[:, :LANES]
-                back = jnp.concatenate([head, back[:, LANES:]], axis=1)
-                total = total + tap_cols[:, 3 * k + s : 3 * k + s + 1] * back
+                tiles = []
+                before = carry[k - 1, s]
+                for b in range(per):
+                    turned = pltpu.roll(cur[:, b * LANES : (b + 1) * LANES], k, 1)
+                    tiles.append(jnp.where(lane < k, before, turned))
+                    before = turned
+                carry[k - 1, s] = before
+                backs.append(jnp.concatenate(tiles, axis=1))
+                total = total + wide(3 * k + s) * backs[-1]
             mixed.append(total)
         inner = (mixed[0] * mixed[2]).astype(jnp.bfloat16)
         for b in range(per):
@@ -277,7 +285,7 @@
         b = place_ref[0] ^ r
         at = pl.ds(pl.multiple_of(b * gsz, gsz), gsz)
         filtered = jnp.concatenate([conv[g, at, :] for g in range(groups)], axis=0)
-        gated = (gate[b] * filtered).T.astype(jnp.bfloat16)
+        gated = (gate[b] * filtered).astype(jnp.bfloat16).T
         k, dx, dc = r >> 2, (r >> 1) & 1, r & 1
         if k == 0:
             home[dx, dc, 0] = gated
@@ -299,7 +307,7 @@
     near_shape = (2, genomes, taps, chans)
     packs = lambda n: pl.BlockSpec((n, 2, 1, taps, chans), lambda g, p: (0, 0, g, 0, 0))
     return pl.pallas_call(
-        functools.partial(mixer_body, feature_count=feature_count, chunk=2 * taps),
+        functools.partial(mixer_body, feature_count=feature_count, chunk=4 * taps),
         grid_spec=pltpu.PrefetchScalarGridSpec(
             num_scalar_prefetch=1,
             grid=(genomes,),
@@ -317,7 +325,7 @@
             scratch_shapes=[
                 pltpu.VMEM((width, vocab), jnp.bfloat16),
                 pltpu.VMEM((groups, 2 * taps, taps), jnp.bfloat16),
-                pltpu.VMEM((chans, taps_rows.shape[0]), jnp.float32),
+                pltpu.VMEM((9, chans, LANES), jnp.float32),
                 pltpu.VMEM((2, 3, chans, LANES), jnp.float32),
                 pltpu.VMEM((groups, (blocks + 1) * gsz, taps), jnp.bfloat16),
                 pltpu.VMEM((blocks, chans, taps), jnp.float32),

time: 83.6 us -> 81.1 us (0.970)
  Pallas kernels: 40.8 us -> 38.2 us
    pallas_call x1, Pallas kernels: 9.22 us -> 6.68 us  [mixer(): pl.pallas_call(functools.partial(mixer_body, feature_count=feature_count,...]
  transfers between devices with their start and end apart: 16 -> 16, of which waited for: 7 -> 7; matrix products, arithmetic and copies ran while one was open for 1% -> 1% of each run, Pallas kernels for 22% -> 23%
where the time goes in v3:
time: 81.1 us; the launch traced here: 80.3 us
  Pallas kernels  38.2 us (47%)
  starting transfers between devices  23.3 us (29%)
  waiting for transfers between devices  16.6 us (20%)
  local copies, waits for them, and re-layouts  1.52 us (2%)
    pallas_call x3, Pallas kernels, project(): pl.pallas_call(functools.partial(project_body, columns=columns, first=fir...  20.2 us
    ppermute x11, waiting for transfers between devices, swap_seq(): lax.ppermute(shard, 'seq', [(i, i ^ step) for i in range(lax.axis_size('s...  15 us
    ppermute x11, starting transfers between devices, swap_seq(): lax.ppermute(shard, 'seq', [(i, i ^ step) for i in range(lax.axis_size('s...  12.7 us
    pallas_call x2, Pallas kernels, vocab_share(): pl.pallas_call(functools.partial(vocab_share_body, slabs=slabs, steps=ste...  11.4 us
    pallas_call x1, Pallas kernels, mixer(): pl.pallas_call(functools.partial(mixer_body, feature_count=feature_count,...  6.68 us
    ppermute x4, starting transfers between devices, swap_wt(): return lax.ppermute(shard, 'wt', [(0, 1), (1, 0)])  5.68 us
    all_to_all x1, starting transfers between devices, shared_block(): all_tokens = lax.all_to_all(copies, ('seq', 'wt'), 0, 0, tiled=True)  4.89 us
  transfers between devices with their start and end apart: 16, of which 7 were waited for; matrix products, arithmetic and copies ran while one was open for 1% of the time, Pallas kernels for 23%

profile of v3, /device:TPU:0, one launch (start us, length us, event | category | flops | bytes accessed | tf_op | source)
XLA Modules:
  0.0 80.3 jit_solution(14890165283588012264)
XLA Ops:
  0.0 0.0 copy-start
  0.0 0.0 copy-start.4
  0.0 5.7 %vocab_share.2 = (bf16[544,384]{1,0:T(8,128)(2,1)}, f32[1,512]{1,0:T(1,128)}, s32[32,1,128]{2,1,0:T(1,128)}) custom-call(s32[1]{0:T(128)} %bitcast.2.half_ref, bf16[4096]{0:T(1024)(128)(2,1)} %gain_ref.3, bf16[512,4096]{1,0:T(8,128)(2,1)} %refs_5_.1, bf16[512,4096]{1,0:T(8,128)(2,1)} %refs_5_.1, bf16[3,4096,256]{2,1,0:T(8,128)(2,1)} %bitcast.75, ...), custom_call_target="tpu_custom_call" | custom-call | tf_op jit(solution)/shard_map/vocab_share/pallas_call | solution.py:187
  5.7 3.0 %collective-permute-start = (bf16[544,384]{1,0:T(8,128)(2,1)}, bf16[544,384]{1,0:T(8,128)(2,1)S(1)}, u32[]{:S(2)}, u32[]{:S(2)}) collective-permute-start(bf16[544,384]{1,0:T(8,128)(2,1)} %get-tuple-element.21), channel_id=1, source_target_pairs={{0,1},{1,0},{2,3},{3,2},{4,5},{5,4},{6,7},{7,6},{8,9},{9,8},{10,11... | collective-permute-start | bytes 1253384 | tf_op jit(solution)/shard_map/ppermute | solution.py:465
  8.7 4.9 %all-to-all-start = ((s32[32,1,128]{2,1,0:T(1,128)}), s32[32,1,128]{2,1,0:T(1,128)S(1)}, u32[]{:S(2)}, u32[]{:S(2)}) async-start(s32[32,1,128]{2,1,0:T(1,128)} %get-tuple-element.20), calls=%async_computation | async-start | bytes 32768 | tf_op jit(solution)/shard_map/all_to_all | solution.py:490
  13.6 0.0 copy-done.4
  13.6 0.0 copy-done
  13.7 0.1 pad_add_fusion.place_ref
  13.8 0.0 copy-start.3
  13.8 5.6 %vocab_share.3.own_ref = f32[512,384]{1,0:T(8,128)} custom-call(s32[1]{0:T(128)} %bitcast.1.half_ref, bf16[4096]{0:T(1024)(128)(2,1)} %gain_ref.3, bf16[512,4096]{1,0:T(8,128)(2,1)} %refs_5_.1, bf16[512,4096]{1,0:T(8,128)(2,1)} %refs_5_.1, bf16[3,4096,256]{2,1,0:T(8,128)(2,1)} %bitcast.77, bf16[3,4096,256]{2,1,0:T(8,128)(2,1)} %bitcast.78), custom_call_target="tpu_custom_call" | custom-call | tf_op jit(solution)/shard_map/vocab_share/pallas_call | solution.py:187
  19.4 1.4 %all-to-all-done = s32[32,1,128]{2,1,0:T(1,128)S(1)} async-done(((s32[32,1,128]{2,1,0:T(1,128)}), s32[32,1,128]{2,1,0:T(1,128)S(1)}, u32[]{:S(2)}, u32[]{:S(2)}) %all-to-all-start) | async-done | bytes 16416 | tf_op jit(solution)/shard_map/all_to_all | solution.py:490
  20.8 0.0 collective-permute-done.got_ref
  20.8 0.0 copy-done.3
  20.8 0.0 copy-start.2
  20.8 1.1 %copy-done.2 = f32[512,384]{1,0:T(8,128)S(1)} copy-done((f32[512,384]{1,0:T(8,128)S(1)}, f32[512,384]{1,0:T(8,128)}, u32[]{:S(2)}) %copy-start.2) | copy-done | bytes 786456
  21.9 6.7 %mixer.1 = (bf16[2,2,2,128,128]{4,3,2,1,0:T(8,128)(2,1)S(1)}, bf16[2,2,128,128]{3,2,1,0:T(8,128)(2,1)S(1)}, bf16[2,2,128,128]{3,2,1,0:T(8,128)(2,1)S(1)}, bf16[2...) custom-call(s32[2]{0:T(128)S(1)} %pad_add_fusion.place_ref, s32[16,2,128]{2,1,0:T(2,128)S(1)} %bitcast.73, ...), custom_call_target="tpu_custom_call" | custom-call | flops 1610612736 | bytes 2228224 | tf_op jit(solution)/shard_map/mixer/pallas_call | solution.py:309
  28.6 0.6 collective-permute-start.5
  29.2 1.4 %collective-permute-start.7 = (bf16[2,2,128,128]{3,2,1,0:T(8,128)(2,1)S(1)}, bf16[2,2,128,128]{3,2,1,0:T(8,128)(2,1)S(1)}, u32[]{:S(2)}, u32[]{:S(2)}) collective-permute-start(bf16[2,2,128,128]{3,2,1,0:T(8,128)(2,1)S(1)} %get-tuple-element.25), channel_id=1, source_target_pairs={{0,8},{2,10},{4,12},{6,14},{8,0},{10,2},{12,4},{14,6},{16,24},{18,... | collective-permute-start | bytes 393224 | tf_op jit(solution)/shard_map/ppermute | solution.py:469
  30.6 2.4 %collective-permute-start.8 = (bf16[2,2,128,128]{3,2,1,0:T(8,128)(2,1)S(1)}, bf16[2,2,128,128]{3,2,1,0:T(8,128)(2,1)S(1)}, u32[]{:S(2)}, u32[]{:S(2)}) collective-permute-start(bf16[2,2,128,128]{3,2,1,0:T(8,128)(2,1)S(1)} %get-tuple-element.26), channel_id=1, source_target_pairs={{0,16},{2,18},{4,20},{6,22},{8,24},{10,26},{12,28},{14,30},{16,0},... | collective-permute-start | bytes 393224 | tf_op jit(solution)/shard_map/ppermute | solution.py:469
  33.1 0.6 collective-permute-start.9
  33.7 1.4 %collective-permute-start.1 = (bf16[3,2,2,128,128]{4,3,2,1,0:T(8,128)(2,1)S(1)}, bf16[3,2,2,128,128]{4,3,2,1,0:T(8,128)(2,1)S(1)}, u32[]{:S(2)}, u32[]{:S(2)}) collective-permute-start(bf16[3,2,2,128,128]{4,3,2,1,0:T(8,128)(2,1)S(1)} %get-tuple-element.23), channel_id=1, source_target_pairs={{0,4},{2,6},{4,0},{6,2},{8,12},{10,14},{12,8},{14,10},{16,20},{18,... | collective-permute-start | bytes 1179656 | tf_op jit(solution)/shard_map/ppermute | solution.py:469
  35.0 1.1 %collective-permute-done.7.refs_1_ = bf16[2,2,128,128]{3,2,1,0:T(8,128)(2,1)S(1)} collective-permute-done((bf16[2,2,128,128]{3,2,1,0:T(8,128)(2,1)S(1)}, bf16[2,2,128,128]{3,2,1,0:T(8,128)(2,1)S(1)}, u32[]{:S(2)}, u32[]{:S(2)}) %collective-permute-start.7) | collective-permute-done | bytes 131104 | tf_op jit(solution)/shard_map/ppermute | solution.py:469
  36.1 7.5 %collective-permute-done.8.refs_2_ = bf16[2,2,128,128]{3,2,1,0:T(8,128)(2,1)S(1)} collective-permute-done((bf16[2,2,128,128]{3,2,1,0:T(8,128)(2,1)S(1)}, bf16[2,2,128,128]{3,2,1,0:T(8,128)(2,1)S(1)}, u32[]{:S(2)}, u32[]{:S(2)}) %collective-permute-start.8) | collective-permute-done | bytes 131104 | tf_op jit(solution)/shard_map/ppermute | solution.py:469
  43.6 0.0 collective-permute-done.9.refs_3_
  43.6 0.6 collective-permute-start.10
  44.3 0.0 collective-permute-done.5
  44.3 1.5 %collective-permute-start.6 = (bf16[2,2,2,128,128]{4,3,2,1,0:T(8,128)(2,1)S(1)}, bf16[2,2,2,128,128]{4,3,2,1,0:T(8,128)(2,1)S(1)}, u32[]{:S(2)}, u32[]{:S(2)}) collective-permute-start(bf16[2,2,2,128,128]{4,3,2,1,0:T(8,128)(2,1)S(1)} %pad_maximum_fusion.2), channel_id=1, source_target_pairs={{0,4},{2,6},{4,0},{6,2},{8,12},{10,14},{12,8},{14,10},{16,20},{18,... | collective-permute-start | bytes 786440 | tf_op jit(solution)/shard_map/ppermute | solution.py:469
  45.9 0.1 collective-permute-start.13
  45.9 0.0 collective-permute-done.1
  46.0 2.1 %collective-permute-start.2 = (bf16[2,2,128,128]{3,2,1,0:T(8,128)(2,1)S(1)}, bf16[2,2,128,128]{3,2,1,0:T(8,128)(2,1)S(1)}, u32[]{:S(2)}, u32[]{:S(2)}) collective-permute-start(bf16[2,2,128,128]{3,2,1,0:T(8,128)(2,1)S(1)} %get-tuple-element.43), channel_id=1, source_target_pairs={{0,8},{2,10},{4,12},{6,14},{8,0},{10,2},{12,4},{14,6},{16,24},{18,... | collective-permute-start | bytes 393224 | tf_op jit(solution)/shard_map/ppermute | solution.py:469
  48.1 1.0 %collective-permute-start.3 = (bf16[2,2,128,128]{3,2,1,0:T(8,128)(2,1)S(1)}, bf16[2,2,128,128]{3,2,1,0:T(8,128)(2,1)S(1)}, u32[]{:S(2)}, u32[]{:S(2)}) collective-permute-start(bf16[2,2,128,128]{3,2,1,0:T(8,128)(2,1)S(1)} %get-tuple-element.42), channel_id=1, source_target_pairs={{0,16},{2,18},{4,20},{6,22},{8,24},{10,26},{12,28},{14,30},{16,0},... | collective-permute-start | bytes 393224 | tf_op jit(solution)/shard_map/ppermute | solution.py:469
  49.0 1.7 %collective-permute-done.6 = bf16[2,2,2,128,128]{4,3,2,1,0:T(8,128)(2,1)S(1)} collective-permute-done((bf16[2,2,2,128,128]{4,3,2,1,0:T(8,128)(2,1)S(1)}, bf16[2,2,2,128,128]{4,3,2,1,0:T(8,128)(2,1)S(1)}, u32[]{:S(2)}, u32[]{:S(2)}) %collective-permute-start.6) | collective-permute-done | bytes 262176 | tf_op jit(solution)/shard_map/ppermute | solution.py:469
  50.8 2.2 %collective-permute-start.4 = (bf16[2,2,128,128]{3,2,1,0:T(8,128)(2,1)S(1)}, bf16[2,2,128,128]{3,2,1,0:T(8,128)(2,1)S(1)}, u32[]{:S(2)}, u32[]{:S(2)}) collective-permute-start(bf16[2,2,128,128]{3,2,1,0:T(8,128)(2,1)S(1)} %get-tuple-element.41), channel_id=1, source_target_pairs={{0,24},{2,26},{4,28},{6,30},{8,16},{10,18},{12,20},{14,22},{16,8},... | collective-permute-start | bytes 393224 | tf_op jit(solution)/shard_map/ppermute | solution.py:469
  53.0 0.0 collective-permute-done.10
  53.1 0.1 collective-permute-start.11
  53.1 0.0 collective-permute-done.13.refs_2_
  53.2 0.0 copy-done.1
  53.2 4.7 %project.3.refs_10_ = f32[2,128,4096]{2,1,0:T(8,128)S(1)} custom-call(s32[2]{0:T(128)S(1)} %pad_add_fusion.place_ref, bf16[2,2,128,128]{3,2,1,0:T(8,128)(2,1)S(1)} %get-tuple-element.46.refs_0_, bf16[2,2,128,128]{3,2,1,0:T(8,128)(2,1)S(1)} %get-tuple-element.44.refs_1_, bf16[2,2,128,128]{3,2,1,0:T(8,128)(2,1)S(1)} %collective-permute-done.13.refs_2_, ...), custom_call_target="tpu_custom_call" | custom-call | flops 1073741824 | bytes 10485760 | tf_op jit(solution)/shard_map/project/pallas_call | solution.py:448
  57.9 0.0 collective-permute-done.2.refs_0_
  57.9 3.1 %collective-permute-done.3.refs_1_ = bf16[2,2,128,128]{3,2,1,0:T(8,128)(2,1)S(1)} collective-permute-done((bf16[2,2,128,128]{3,2,1,0:T(8,128)(2,1)S(1)}, bf16[2,2,128,128]{3,2,1,0:T(8,128)(2,1)S(1)}, u32[]{:S(2)}, u32[]{:S(2)}) %collective-permute-start.3) | collective-permute-done | bytes 131104 | tf_op jit(solution)/shard_map/ppermute | solution.py:469
  61.0 0.0 collective-permute-done.4.refs_2_
  61.0 0.0 collective-permute-done.11.refs_8_
  61.1 1.5 %collective-permute-start.12 = (bf16[3,2,2,128,128]{4,3,2,1,0:T(8,128)(2,1)S(1)}, bf16[3,2,2,128,128]{4,3,2,1,0:T(8,128)(2,1)S(1)}, u32[]{:S(2)}, u32[]{:S(2)}) collective-permute-start(bf16[3,2,2,128,128]{4,3,2,1,0:T(8,128)(2,1)S(1)} %pad_maximum_fusion.1), channel_id=1, source_target_pairs={{0,1},{1,0},{2,3},{3,2},{4,5},{5,4},{6,7},{7,6},{8,9},{9,8},{10,11... | collective-permute-start | bytes 1179656 | tf_op jit(solution)/shard_map/ppermute | solution.py:465
  62.6 8.1 %project.4.refs_8_ = f32[2,128,4096]{2,1,0:T(8,128)S(1)} custom-call(s32[2]{0:T(128)S(1)} %pad_add_fusion.place_ref, bf16[2,2,128,128]{3,2,1,0:T(8,128)(2,1)S(1)} %get-tuple-element.49.refs_0_, bf16[2,2,128,128]{3,2,1,0:T(8,128)(2,1)S(1)} %collective-permute-done.7.refs_1_, bf16[2,2,128,128]{3,2,1,0:T(8,128)(2,1)S(1)} %collective-permute-done.8.refs_2_, ...), custom_call_target="tpu_custom_call" | custom-call | flops 4294967296 | bytes 23068672 | tf_op jit(solution)/shard_map/project/pallas_call | solution.py:448
  70.7 0.1 collective-permute-done.12
  70.9 0.1 collective-permute-start.14
  71.0 1.7 %collective-permute-done.14.refs_6_ = bf16[6,2,128,128]{3,2,1,0:T(8,128)(2,1)S(1)} collective-permute-done((bf16[6,2,128,128]{3,2,1,0:T(8,128)(2,1)S(1)}, bf16[6,2,128,128]{3,2,1,0:T(8,128)(2,1)S(1)}, u32[]{:S(2)}, u32[]{:S(2)}) %collective-permute-start.14) | collective-permute-done | bytes 393248 | tf_op jit(solution)/shard_map/ppermute | solution.py:469
  72.7 7.5 %project.5 = bf16[2,128,4096]{2,1,0:T(8,128)(2,1)} custom-call(s32[2]{0:T(128)S(1)} %pad_add_fusion.place_ref, bf16[2,2,128,128]{3,2,1,0:T(8,128)(2,1)S(1)} %collective-permute-done.2.refs_0_, bf16[2,2,128,128]{3,2,1,0:T(8,128)(2,1)S(1)} %collective-permute-done.3.refs_1_, bf16[2,2,128,128]{3,2,1,0:T(8,128)(2,1)S(1)} %collective-permute-done.4.refs_2_, ...), custom_call_target="tpu_custom_call" | custom-call | flops 3221225472 | bytes 18874368 | tf_op jit(solution)/shard_map/project/pallas_call | solution.py:448
  (31 shorter events, 0.5 us)
Async XLA Ops:
  0.0 13.6 %copy-start = (bf16[16,128]{1,0:T(8,128)(2,1)S(1)}, bf16[16,128]{1,0:T(8,128)(2,1)}, u32[]{:S(2)}) copy-start(bf16[16,128]{1,0:T(8,128)(2,1)} %param.12) | copy-start | bytes 12292
  0.0 13.6 %copy-start.4 = (bf16[3,3,256]{2,1,0:T(4,128)(2,1)S(1)}, bf16[3,3,256]{2,1,0:T(4,128)(2,1)}, u32[]{:S(2)}) copy-start(bf16[3,3,256]{2,1,0:T(4,128)(2,1)} %param.11) | copy-start | bytes 13828
  5.7 15.1 %collective-permute-start = (bf16[544,384]{1,0:T(8,128)(2,1)}, bf16[544,384]{1,0:T(8,128)(2,1)S(1)}, u32[]{:S(2)}, u32[]{:S(2)}) collective-permute-start(bf16[544,384]{1,0:T(8,128)(2,1)} %get-tuple-element.21), channel_id=1, source_target_pairs={{0,1},{1,0},{2,3},{3,2},{4,5},{5,4},{6,7},{7,6},{8,9},{9,8},{10,11... | collective-permute-start | bytes 1253384 | tf_op jit(solution)/shard_map/ppermute | solution.py:465
  8.7 12.1 %all-to-all-start = ((s32[32,1,128]{2,1,0:T(1,128)}), s32[32,1,128]{2,1,0:T(1,128)S(1)}, u32[]{:S(2)}, u32[]{:S(2)}) async-start(s32[32,1,128]{2,1,0:T(1,128)} %get-tuple-element.20), calls=%async_computation | async-start | bytes 32768 | tf_op jit(solution)/shard_map/all_to_all | solution.py:490
  13.8 7.0 %copy-start.3 = (f32[1,512]{1,0:T(1,128)S(1)}, f32[1,512]{1,0:T(1,128)}, u32[]{:S(2)}) copy-start(f32[1,512]{1,0:T(1,128)} %get-tuple-element.22.sq_ref) | copy-start | bytes 6148
  20.8 1.1 %copy-start.2 = (f32[512,384]{1,0:T(8,128)S(1)}, f32[512,384]{1,0:T(8,128)}, u32[]{:S(2)}) copy-start(f32[512,384]{1,0:T(8,128)} %vocab_share.3.own_ref) | copy-start | bytes 2359300
  21.9 31.2 %copy-start.1 = (bf16[512,4096]{1,0:T(8,128)(2,1)S(1)}, bf16[512,4096]{1,0:T(8,128)(2,1)}, u32[]{:S(2)}) copy-start(bf16[512,4096]{1,0:T(8,128)(2,1)} %refs_5_.1) | copy-start | bytes 12582916
  28.6 15.6 %collective-permute-start.5 = (bf16[2,2,2,128,128]{4,3,2,1,0:T(8,128)(2,1)S(1)}, bf16[2,2,2,128,128]{4,3,2,1,0:T(8,128)(2,1)S(1)}, u32[]{:S(2)}, u32[]{:S(2)}) collective-permute-start(bf16[2,2,2,128,128]{4,3,2,1,0:T(8,128)(2,1)S(1)} %get-tuple-element.24), channel_id=1, source_target_pairs={{0,1},{1,0},{2,3},{3,2},{4,5},{5,4},{6,7},{7,6},{8,9},{9,8},{10,11... | collective-permute-start | bytes 786440 | tf_op jit(solution)/shard_map/ppermute | solution.py:465
  29.2 6.9 %collective-permute-start.7 = (bf16[2,2,128,128]{3,2,1,0:T(8,128)(2,1)S(1)}, bf16[2,2,128,128]{3,2,1,0:T(8,128)(2,1)S(1)}, u32[]{:S(2)}, u32[]{:S(2)}) collective-permute-start(bf16[2,2,128,128]{3,2,1,0:T(8,128)(2,1)S(1)} %get-tuple-element.25), channel_id=1, source_target_pairs={{0,8},{2,10},{4,12},{6,14},{8,0},{10,2},{12,4},{14,6},{16,24},{18,... | collective-permute-start | bytes 393224 | tf_op jit(solution)/shard_map/ppermute | solution.py:469
  30.6 12.9 %collective-permute-start.8 = (bf16[2,2,128,128]{3,2,1,0:T(8,128)(2,1)S(1)}, bf16[2,2,128,128]{3,2,1,0:T(8,128)(2,1)S(1)}, u32[]{:S(2)}, u32[]{:S(2)}) collective-permute-start(bf16[2,2,128,128]{3,2,1,0:T(8,128)(2,1)S(1)} %get-tuple-element.26), channel_id=1, source_target_pairs={{0,16},{2,18},{4,20},{6,22},{8,24},{10,26},{12,28},{14,30},{16,0},... | collective-permute-start | bytes 393224 | tf_op jit(solution)/shard_map/ppermute | solution.py:469
  33.1 10.5 %collective-permute-start.9 = (bf16[2,2,128,128]{3,2,1,0:T(8,128)(2,1)S(1)}, bf16[2,2,128,128]{3,2,1,0:T(8,128)(2,1)S(1)}, u32[]{:S(2)}, u32[]{:S(2)}) collective-permute-start(bf16[2,2,128,128]{3,2,1,0:T(8,128)(2,1)S(1)} %get-tuple-element.27), channel_id=1, source_target_pairs={{0,24},{2,26},{4,28},{6,30},{8,16},{10,18},{12,20},{14,22},{16,8},... | collective-permute-start | bytes 393224 | tf_op jit(solution)/shard_map/ppermute | solution.py:469
  33.7 12.3 %collective-permute-start.1 = (bf16[3,2,2,128,128]{4,3,2,1,0:T(8,128)(2,1)S(1)}, bf16[3,2,2,128,128]{4,3,2,1,0:T(8,128)(2,1)S(1)}, u32[]{:S(2)}, u32[]{:S(2)}) collective-permute-start(bf16[3,2,2,128,128]{4,3,2,1,0:T(8,128)(2,1)S(1)} %get-tuple-element.23), channel_id=1, source_target_pairs={{0,4},{2,6},{4,0},{6,2},{8,12},{10,14},{12,8},{14,10},{16,20},{18,... | collective-permute-start | bytes 1179656 | tf_op jit(solution)/shard_map/ppermute | solution.py:469
  43.6 9.4 %collective-permute-start.10 = (bf16[3,2,2,128,128]{4,3,2,1,0:T(8,128)(2,1)S(1)}, bf16[3,2,2,128,128]{4,3,2,1,0:T(8,128)(2,1)S(1)}, u32[]{:S(2)}, u32[]{:S(2)}) collective-permute-start(bf16[3,2,2,128,128]{4,3,2,1,0:T(8,128)(2,1)S(1)} %pad_maximum_fusion), channel_id=1, source_target_pairs={{0,1},{1,0},{2,3},{3,2},{4,5},{5,4},{6,7},{7,6},{8,9},{9,8},{10,11... | collective-permute-start | bytes 1179656 | tf_op jit(solution)/shard_map/ppermute | solution.py:465
  44.3 6.4 %collective-permute-start.6 = (bf16[2,2,2,128,128]{4,3,2,1,0:T(8,128)(2,1)S(1)}, bf16[2,2,2,128,128]{4,3,2,1,0:T(8,128)(2,1)S(1)}, u32[]{:S(2)}, u32[]{:S(2)}) collective-permute-start(bf16[2,2,2,128,128]{4,3,2,1,0:T(8,128)(2,1)S(1)} %pad_maximum_fusion.2), channel_id=1, source_target_pairs={{0,4},{2,6},{4,0},{6,2},{8,12},{10,14},{12,8},{14,10},{16,20},{18,... | collective-permute-start | bytes 786440 | tf_op jit(solution)/shard_map/ppermute | solution.py:469
  45.9 7.3 %collective-permute-start.13 = (bf16[2,2,128,128]{3,2,1,0:T(8,128)(2,1)S(1)}, bf16[2,2,128,128]{3,2,1,0:T(8,128)(2,1)S(1)}, u32[]{:S(2)}, u32[]{:S(2)}) collective-permute-start(bf16[2,2,128,128]{3,2,1,0:T(8,128)(2,1)S(1)} %pad_maximum_fusion.3), channel_id=1, source_target_pairs={{0,2},{2,0},{4,6},{6,4},{8,10},{10,8},{12,14},{14,12},{16,18},{18,... | collective-permute-start | bytes 393224 | tf_op jit(solution)/shard_map/ppermute | solution.py:469
  46.0 11.9 %collective-permute-start.2 = (bf16[2,2,128,128]{3,2,1,0:T(8,128)(2,1)S(1)}, bf16[2,2,128,128]{3,2,1,0:T(8,128)(2,1)S(1)}, u32[]{:S(2)}, u32[]{:S(2)}) collective-permute-start(bf16[2,2,128,128]{3,2,1,0:T(8,128)(2,1)S(1)} %get-tuple-element.43), channel_id=1, source_target_pairs={{0,8},{2,10},{4,12},{6,14},{8,0},{10,2},{12,4},{14,6},{16,24},{18,... | collective-permute-start | bytes 393224 | tf_op jit(solution)/shard_map/ppermute | solution.py:469
  48.1 12.9 %collective-permute-start.3 = (bf16[2,2,128,128]{3,2,1,0:T(8,128)(2,1)S(1)}, bf16[2,2,128,128]{3,2,1,0:T(8,128)(2,1)S(1)}, u32[]{:S(2)}, u32[]{:S(2)}) collective-permute-start(bf16[2,2,128,128]{3,2,1,0:T(8,128)(2,1)S(1)} %get-tuple-element.42), channel_id=1, source_target_pairs={{0,16},{2,18},{4,20},{6,22},{8,24},{10,26},{12,28},{14,30},{16,0},... | collective-permute-start | bytes 393224 | tf_op jit(solution)/shard_map/ppermute | solution.py:469
  50.8 10.2 %collective-permute-start.4 = (bf16[2,2,128,128]{3,2,1,0:T(8,128)(2,1)S(1)}, bf16[2,2,128,128]{3,2,1,0:T(8,128)(2,1)S(1)}, u32[]{:S(2)}, u32[]{:S(2)}) collective-permute-start(bf16[2,2,128,128]{3,2,1,0:T(8,128)(2,1)S(1)} %get-tuple-element.41), channel_id=1, source_target_pairs={{0,24},{2,26},{4,28},{6,30},{8,16},{10,18},{12,20},{14,22},{16,8},... | collective-permute-start | bytes 393224 | tf_op jit(solution)/shard_map/ppermute | solution.py:469
  53.1 7.9 %collective-permute-start.11 = (bf16[8,2,128,128]{3,2,1,0:T(8,128)(2,1)S(1)}, bf16[8,2,128,128]{3,2,1,0:T(8,128)(2,1)S(1)}, u32[]{:S(2)}, u32[]{:S(2)}) collective-permute-start(bf16[8,2,128,128]{3,2,1,0:T(8,128)(2,1)S(1)} %fusion), channel_id=1, source_target_pairs={{0,2},{2,0},{4,6},{6,4},{8,10},{10,8},{12,14},{14,12},{16,18},{18,... | collective-permute-start | bytes 1572872 | tf_op jit(solution)/shard_map/ppermute | solution.py:469
  61.1 9.7 %collective-permute-start.12 = (bf16[3,2,2,128,128]{4,3,2,1,0:T(8,128)(2,1)S(1)}, bf16[3,2,2,128,128]{4,3,2,1,0:T(8,128)(2,1)S(1)}, u32[]{:S(2)}, u32[]{:S(2)}) collective-permute-start(bf16[3,2,2,128,128]{4,3,2,1,0:T(8,128)(2,1)S(1)} %pad_maximum_fusion.1), channel_id=1, source_target_pairs={{0,1},{1,0},{2,3},{3,2},{4,5},{5,4},{6,7},{7,6},{8,9},{9,8},{10,11... | collective-permute-start | bytes 1179656 | tf_op jit(solution)/shard_map/ppermute | solution.py:465
  70.9 1.8 %collective-permute-start.14 = (bf16[6,2,128,128]{3,2,1,0:T(8,128)(2,1)S(1)}, bf16[6,2,128,128]{3,2,1,0:T(8,128)(2,1)S(1)}, u32[]{:S(2)}, u32[]{:S(2)}) collective-permute-start(bf16[6,2,128,128]{3,2,1,0:T(8,128)(2,1)S(1)} %bitcast_dynamic-update-slice_fusion), channel_id=1, source_target_pairs={{0,2},{2,0},{4,6},{6,4},{8,10},{10,8},{12,14},{14,12},{16,18},{18,... | collective-permute-start | bytes 1179656 | tf_op jit(solution)/shard_map/ppermute | solution.py:469

commit v4 on v3

--- a/solution.py
+++ b/solution.py
@@ -245,15 +245,16 @@
     for k in range(2):
         carry[k] = jnp.zeros(carry.shape[1:], jnp.float32)
 
-    ids = lax.broadcasted_iota(jnp.int32, (vocab, chunk), 0)
+    ids = lax.broadcasted_iota(jnp.int32, (vocab, chunk), 0).astype(jnp.int16)
+    one, zero = jnp.ones((), jnp.bfloat16), jnp.zeros((), jnp.bfloat16)
     lane = lax.broadcasted_iota(jnp.int32, (chans, LANES), 1)
     per = chunk // taps
     for n in range(length // chunk):
         toks = jnp.concatenate(
             [tok_ref[n * per + b, pl.ds(genome, 1), :] for b in range(per)], axis=1
         )
-        picks = jnp.where(ids == toks, 1.0, 0.0)
-        proj = jnp.dot(vocab_t[...], picks.astype(jnp.bfloat16), preferred_element_type=jnp.float32)
+        picks = jnp.where(ids == toks.astype(jnp.int16), one, zero)
+        proj = jnp.dot(vocab_t[...], picks, preferred_element_type=jnp.float32)
         mixed = []
         for s in range(3):
             cur = proj[s * chans : (s + 1) * chans]
@@ -504,6 +505,7 @@
     arrived = swap_seq(far, 2)
     home_other = swap_wt(home)
     near_mine = {k: swap_seq(near[k - 1], 4 * k) for k in order}
+    arrived, near_mine[1] = bar((arrived, near_mine[1]))
     far_mine = {k: swap_seq(arrived[k - 1], 4 * k) for k in order}
     crossed = swap_seq(jnp.stack([home[1], home_other[1]]), 2)
     first_mine, first_other = [home[0]], [home_other[0]]

time: 81.1 us -> 79.7 us (0.983)
  starting transfers between devices: 23.3 us -> 21.8 us
    ppermute x11, waiting for transfers between devices: 15 us -> 10.2 us  [swap_seq(): lax.ppermute(shard, 'seq', [(i, i ^ step) for i in range(lax.axis_size('s...]
    ppermute x4, waiting for transfers between devices: 0.15 us -> 4.9 us  [swap_wt(): return lax.ppermute(shard, 'wt', [(0, 1), (1, 0)])]
    ppermute x11, starting transfers between devices: 12.7 us -> 11.3 us  [swap_seq(): lax.ppermute(shard, 'seq', [(i, i ^ step) for i in range(lax.axis_size('s...]
  transfers between devices with their start and end apart: 16 -> 16, of which waited for: 7 -> 8; matrix products, arithmetic and copies ran while one was open for 1% -> 1% of each run, Pallas kernels for 23% -> 23%
where the time goes in v4:
time: 79.7 us; the launch traced here: 78.3 us
  Pallas kernels  37.9 us (48%)
  starting transfers between devices  21.8 us (27%)
  waiting for transfers between devices  16.5 us (21%)
  local copies, waits for them, and re-layouts  1.51 us (2%)
    pallas_call x3, Pallas kernels, project(): pl.pallas_call(functools.partial(project_body, columns=columns, first=fir...  20.2 us
    pallas_call x2, Pallas kernels, vocab_share(): pl.pallas_call(functools.partial(vocab_share_body, slabs=slabs, steps=ste...  11.4 us
    ppermute x11, starting transfers between devices, swap_seq(): lax.ppermute(shard, 'seq', [(i, i ^ step) for i in range(lax.axis_size('s...  11.3 us
    ppermute x11, waiting for transfers between devices, swap_seq(): lax.ppermute(shard, 'seq', [(i, i ^ step) for i in range(lax.axis_size('s...  10.2 us
    pallas_call x1, Pallas kernels, mixer(): pl.pallas_call(functools.partial(mixer_body, feature_count=feature_count,...  6.31 us
    ppermute x4, starting transfers between devices, swap_wt(): return lax.ppermute(shard, 'wt', [(0, 1), (1, 0)])  5.67 us
    ppermute x4, waiting for transfers between devices, swap_wt(): return lax.ppermute(shard, 'wt', [(0, 1), (1, 0)])  4.9 us
    all_to_all x1, starting transfers between devices, shared_block(): all_tokens = lax.all_to_all(copies, ('seq', 'wt'), 0, 0, tiled=True)  4.89 us
  transfers between devices with their start and end apart: 16, of which 8 were waited for; matrix products, arithmetic and copies ran while one was open for 1% of the time, Pallas kernels for 23%

profile of v4, /device:TPU:0, one launch (start us, length us, event | category | flops | bytes accessed | tf_op | source)
XLA Modules:
  0.0 78.3 jit_solution(14837813294245231107)
XLA Ops:
  0.0 0.0 copy-start
  0.0 0.0 copy-start.4
  0.0 5.7 %vocab_share.2 = (bf16[544,384]{1,0:T(8,128)(2,1)}, f32[1,512]{1,0:T(1,128)}, s32[32,1,128]{2,1,0:T(1,128)}) custom-call(s32[1]{0:T(128)} %bitcast.2.half_ref, bf16[4096]{0:T(1024)(128)(2,1)} %gain_ref.3, bf16[512,4096]{1,0:T(8,128)(2,1)} %refs_5_.1, bf16[512,4096]{1,0:T(8,128)(2,1)} %refs_5_.1, bf16[3,4096,256]{2,1,0:T(8,128)(2,1)} %bitcast.75, ...), custom_call_target="tpu_custom_call" | custom-call | tf_op jit(solution)/shard_map/vocab_share/pallas_call | solution.py:187
  5.7 3.0 %collective-permute-start = (bf16[544,384]{1,0:T(8,128)(2,1)}, bf16[544,384]{1,0:T(8,128)(2,1)S(1)}, u32[]{:S(2)}, u32[]{:S(2)}) collective-permute-start(bf16[544,384]{1,0:T(8,128)(2,1)} %get-tuple-element.23), channel_id=1, source_target_pairs={{0,1},{1,0},{2,3},{3,2},{4,5},{5,4},{6,7},{7,6},{8,9},{9,8},{10,11... | collective-permute-start | bytes 1253384 | tf_op jit(solution)/shard_map/ppermute | solution.py:466
  8.7 4.9 %all-to-all-start = ((s32[32,1,128]{2,1,0:T(1,128)}), s32[32,1,128]{2,1,0:T(1,128)S(1)}, u32[]{:S(2)}, u32[]{:S(2)}) async-start(s32[32,1,128]{2,1,0:T(1,128)} %get-tuple-element.22), calls=%async_computation | async-start | bytes 32768 | tf_op jit(solution)/shard_map/all_to_all | solution.py:491
  13.6 0.0 copy-done.4
  13.6 0.0 copy-done
  13.7 0.1 pad_add_fusion.place_ref
  13.8 0.0 copy-start.3
  13.8 5.6 %vocab_share.3.own_ref = f32[512,384]{1,0:T(8,128)} custom-call(s32[1]{0:T(128)} %bitcast.1.half_ref, bf16[4096]{0:T(1024)(128)(2,1)} %gain_ref.3, bf16[512,4096]{1,0:T(8,128)(2,1)} %refs_5_.1, bf16[512,4096]{1,0:T(8,128)(2,1)} %refs_5_.1, bf16[3,4096,256]{2,1,0:T(8,128)(2,1)} %bitcast.77, bf16[3,4096,256]{2,1,0:T(8,128)(2,1)} %bitcast.78), custom_call_target="tpu_custom_call" | custom-call | tf_op jit(solution)/shard_map/vocab_share/pallas_call | solution.py:187
  19.4 1.4 %all-to-all-done = s32[32,1,128]{2,1,0:T(1,128)S(1)} async-done(((s32[32,1,128]{2,1,0:T(1,128)}), s32[32,1,128]{2,1,0:T(1,128)S(1)}, u32[]{:S(2)}, u32[]{:S(2)}) %all-to-all-start) | async-done | bytes 16416 | tf_op jit(solution)/shard_map/all_to_all | solution.py:491
  20.8 0.0 collective-permute-done.got_ref
  20.8 0.0 copy-done.3
  20.8 0.0 copy-start.2
  20.8 1.1 %copy-done.2 = f32[512,384]{1,0:T(8,128)S(1)} copy-done((f32[512,384]{1,0:T(8,128)S(1)}, f32[512,384]{1,0:T(8,128)}, u32[]{:S(2)}) %copy-start.2) | copy-done | bytes 786456
  21.9 6.3 %mixer.1 = (bf16[2,2,2,128,128]{4,3,2,1,0:T(8,128)(2,1)S(1)}, bf16[2,2,128,128]{3,2,1,0:T(8,128)(2,1)S(1)}, bf16[2,2,128,128]{3,2,1,0:T(8,128)(2,1)S(1)}, bf16[2...) custom-call(s32[2]{0:T(128)S(1)} %pad_add_fusion.place_ref, s32[16,2,128]{2,1,0:T(2,128)S(1)} %bitcast.73, ...), custom_call_target="tpu_custom_call" | custom-call | flops 1610612736 | bytes 2228224 | tf_op jit(solution)/shard_map/mixer/pallas_call | solution.py:310
  28.3 0.6 collective-permute-start.6
  28.8 1.4 %collective-permute-start.1 = (bf16[3,2,2,128,128]{4,3,2,1,0:T(8,128)(2,1)S(1)}, bf16[3,2,2,128,128]{4,3,2,1,0:T(8,128)(2,1)S(1)}, u32[]{:S(2)}, u32[]{:S(2)}) collective-permute-start(bf16[3,2,2,128,128]{4,3,2,1,0:T(8,128)(2,1)S(1)} %get-tuple-element.25), channel_id=1, source_target_pairs={{0,4},{2,6},{4,0},{6,2},{8,12},{10,14},{12,8},{14,10},{16,20},{18,... | collective-permute-start | bytes 1179656 | tf_op jit(solution)/shard_map/ppermute | solution.py:470
  30.2 1.5 %collective-permute-start.2 = (bf16[2,2,128,128]{3,2,1,0:T(8,128)(2,1)S(1)}, bf16[2,2,128,128]{3,2,1,0:T(8,128)(2,1)S(1)}, u32[]{:S(2)}, u32[]{:S(2)}) collective-permute-start(bf16[2,2,128,128]{3,2,1,0:T(8,128)(2,1)S(1)} %get-tuple-element.26), channel_id=1, source_target_pairs={{0,8},{2,10},{4,12},{6,14},{8,0},{10,2},{12,4},{14,6},{16,24},{18,... | collective-permute-start | bytes 393224 | tf_op jit(solution)/shard_map/ppermute | solution.py:470
  31.7 2.5 %collective-permute-start.8 = (bf16[2,2,128,128]{3,2,1,0:T(8,128)(2,1)S(1)}, bf16[2,2,128,128]{3,2,1,0:T(8,128)(2,1)S(1)}, u32[]{:S(2)}, u32[]{:S(2)}) collective-permute-start(bf16[2,2,128,128]{3,2,1,0:T(8,128)(2,1)S(1)} %get-tuple-element.30), channel_id=1, source_target_pairs={{0,16},{2,18},{4,20},{6,22},{8,24},{10,26},{12,28},{14,30},{16,0},... | collective-permute-start | bytes 393224 | tf_op jit(solution)/shard_map/ppermute | solution.py:470
  34.1 0.5 collective-permute-start.9
  34.6 1.7 %collective-permute-done.6 = bf16[2,2,2,128,128]{4,3,2,1,0:T(8,128)(2,1)S(1)} collective-permute-done((bf16[2,2,2,128,128]{4,3,2,1,0:T(8,128)(2,1)S(1)}, bf16[2,2,2,128,128]{4,3,2,1,0:T(8,128)(2,1)S(1)}, u32[]{:S(2)}, u32[]{:S(2)}) %collective-permute-start.6) | collective-permute-done | bytes 262176 | tf_op jit(solution)/shard_map/ppermute | solution.py:466
  36.4 0.8 %collective-permute-start.7 = (bf16[2,2,2,128,128]{4,3,2,1,0:T(8,128)(2,1)S(1)}, bf16[2,2,2,128,128]{4,3,2,1,0:T(8,128)(2,1)S(1)}, u32[]{:S(2)}, u32[]{:S(2)}) collective-permute-start(bf16[2,2,2,128,128]{4,3,2,1,0:T(8,128)(2,1)S(1)} %pad_maximum_fusion.2), channel_id=1, source_target_pairs={{0,4},{2,6},{4,0},{6,2},{8,12},{10,14},{12,8},{14,10},{16,20},{18,... | collective-permute-start | bytes 786440 | tf_op jit(solution)/shard_map/ppermute | solution.py:470
  37.2 0.0 collective-permute-done.2.refs_1_
  37.2 0.1 collective-permute-start.13
  37.3 3.5 %collective-permute-done.1 = bf16[3,2,2,128,128]{4,3,2,1,0:T(8,128)(2,1)S(1)} collective-permute-done((bf16[3,2,2,128,128]{4,3,2,1,0:T(8,128)(2,1)S(1)}, bf16[3,2,2,128,128]{4,3,2,1,0:T(8,128)(2,1)S(1)}, u32[]{:S(2)}, u32[]{:S(2)}) %collective-permute-start.1) | collective-permute-done | bytes 393248 | tf_op jit(solution)/shard_map/ppermute | solution.py:470
  40.9 3.5 %collective-permute-done.8.refs_2_ = bf16[2,2,128,128]{3,2,1,0:T(8,128)(2,1)S(1)} collective-permute-done((bf16[2,2,128,128]{3,2,1,0:T(8,128)(2,1)S(1)}, bf16[2,2,128,128]{3,2,1,0:T(8,128)(2,1)S(1)}, u32[]{:S(2)}, u32[]{:S(2)}) %collective-permute-start.8) | collective-permute-done | bytes 131104 | tf_op jit(solution)/shard_map/ppermute | solution.py:470
  44.4 0.0 collective-permute-done.9.refs_3_
  44.4 0.6 collective-permute-start.10
  45.0 2.0 %collective-permute-start.3 = (bf16[2,2,128,128]{3,2,1,0:T(8,128)(2,1)S(1)}, bf16[2,2,128,128]{3,2,1,0:T(8,128)(2,1)S(1)}, u32[]{:S(2)}, u32[]{:S(2)}) collective-permute-start(bf16[2,2,128,128]{3,2,1,0:T(8,128)(2,1)S(1)} %get-tuple-element.47), channel_id=1, source_target_pairs={{0,8},{2,10},{4,12},{6,14},{8,0},{10,2},{12,4},{14,6},{16,24},{18,... | collective-permute-start | bytes 393224 | tf_op jit(solution)/shard_map/ppermute | solution.py:470
  47.1 0.9 %collective-permute-start.4 = (bf16[2,2,128,128]{3,2,1,0:T(8,128)(2,1)S(1)}, bf16[2,2,128,128]{3,2,1,0:T(8,128)(2,1)S(1)}, u32[]{:S(2)}, u32[]{:S(2)}) collective-permute-start(bf16[2,2,128,128]{3,2,1,0:T(8,128)(2,1)S(1)} %get-tuple-element.46), channel_id=1, source_target_pairs={{0,16},{2,18},{4,20},{6,22},{8,24},{10,26},{12,28},{14,30},{16,0},... | collective-permute-start | bytes 393224 | tf_op jit(solution)/shard_map/ppermute | solution.py:470
  48.0 0.0 collective-permute-done.7
  48.0 1.5 %collective-permute-start.5 = (bf16[2,2,128,128]{3,2,1,0:T(8,128)(2,1)S(1)}, bf16[2,2,128,128]{3,2,1,0:T(8,128)(2,1)S(1)}, u32[]{:S(2)}, u32[]{:S(2)}) collective-permute-start(bf16[2,2,128,128]{3,2,1,0:T(8,128)(2,1)S(1)} %get-tuple-element.45), channel_id=1, source_target_pairs={{0,24},{2,26},{4,28},{6,30},{8,16},{10,18},{12,20},{14,22},{16,8},... | collective-permute-start | bytes 393224 | tf_op jit(solution)/shard_map/ppermute | solution.py:470
  49.6 2.6 %collective-permute-done.10 = bf16[3,2,2,128,128]{4,3,2,1,0:T(8,128)(2,1)S(1)} collective-permute-done((bf16[3,2,2,128,128]{4,3,2,1,0:T(8,128)(2,1)S(1)}, bf16[3,2,2,128,128]{4,3,2,1,0:T(8,128)(2,1)S(1)}, u32[]{:S(2)}, u32[]{:S(2)}) %collective-permute-start.10) | collective-permute-done | bytes 393248 | tf_op jit(solution)/shard_map/ppermute | solution.py:466
  52.3 0.1 collective-permute-start.11
  52.4 0.0 collective-permute-done.13.refs_2_
  52.4 0.0 copy-done.1
  52.4 4.7 %project.3.refs_10_ = f32[2,128,4096]{2,1,0:T(8,128)S(1)} custom-call(s32[2]{0:T(128)S(1)} %pad_add_fusion.place_ref, bf16[2,2,128,128]{3,2,1,0:T(8,128)(2,1)S(1)} %get-tuple-element.50.refs_0_, bf16[2,2,128,128]{3,2,1,0:T(8,128)(2,1)S(1)} %get-tuple-element.48.refs_1_, bf16[2,2,128,128]{3,2,1,0:T(8,128)(2,1)S(1)} %collective-permute-done.13.refs_2_, ...), custom_call_target="tpu_custom_call" | custom-call | flops 1073741824 | bytes 10485760 | tf_op jit(solution)/shard_map/project/pallas_call | solution.py:449
  57.1 0.0 collective-permute-done.3.refs_0_
  57.1 1.5 %collective-permute-done.4.refs_1_ = bf16[2,2,128,128]{3,2,1,0:T(8,128)(2,1)S(1)} collective-permute-done((bf16[2,2,128,128]{3,2,1,0:T(8,128)(2,1)S(1)}, bf16[2,2,128,128]{3,2,1,0:T(8,128)(2,1)S(1)}, u32[]{:S(2)}, u32[]{:S(2)}) %collective-permute-start.4) | collective-permute-done | bytes 131104 | tf_op jit(solution)/shard_map/ppermute | solution.py:470
  58.6 0.0 collective-permute-done.5.refs_2_
  58.6 0.0 collective-permute-done.11.refs_8_
  58.7 1.5 %collective-permute-start.12 = (bf16[3,2,2,128,128]{4,3,2,1,0:T(8,128)(2,1)S(1)}, bf16[3,2,2,128,128]{4,3,2,1,0:T(8,128)(2,1)S(1)}, u32[]{:S(2)}, u32[]{:S(2)}) collective-permute-start(bf16[3,2,2,128,128]{4,3,2,1,0:T(8,128)(2,1)S(1)} %pad_maximum_fusion.1), channel_id=1, source_target_pairs={{0,1},{1,0},{2,3},{3,2},{4,5},{5,4},{6,7},{7,6},{8,9},{9,8},{10,11... | collective-permute-start | bytes 1179656 | tf_op jit(solution)/shard_map/ppermute | solution.py:466
  60.2 8.1 %project.4.refs_8_ = f32[2,128,4096]{2,1,0:T(8,128)S(1)} custom-call(s32[2]{0:T(128)S(1)} %pad_add_fusion.place_ref, bf16[2,2,128,128]{3,2,1,0:T(8,128)(2,1)S(1)} %get-tuple-element.53.refs_0_, bf16[2,2,128,128]{3,2,1,0:T(8,128)(2,1)S(1)} %collective-permute-done.2.refs_1_, bf16[2,2,128,128]{3,2,1,0:T(8,128)(2,1)S(1)} %collective-permute-done.8.refs_2_, ...), custom_call_target="tpu_custom_call" | custom-call | flops 4294967296 | bytes 23068672 | tf_op jit(solution)/shard_map/project/pallas_call | solution.py:449
  68.3 0.5 collective-permute-done.12
  68.9 0.1 collective-permute-start.14
  69.0 1.7 %collective-permute-done.14.refs_6_ = bf16[6,2,128,128]{3,2,1,0:T(8,128)(2,1)S(1)} collective-permute-done((bf16[6,2,128,128]{3,2,1,0:T(8,128)(2,1)S(1)}, bf16[6,2,128,128]{3,2,1,0:T(8,128)(2,1)S(1)}, u32[]{:S(2)}, u32[]{:S(2)}) %collective-permute-start.14) | collective-permute-done | bytes 393248 | tf_op jit(solution)/shard_map/ppermute | solution.py:470
  70.7 7.5 %project.5 = bf16[2,128,4096]{2,1,0:T(8,128)(2,1)} custom-call(s32[2]{0:T(128)S(1)} %pad_add_fusion.place_ref, bf16[2,2,128,128]{3,2,1,0:T(8,128)(2,1)S(1)} %collective-permute-done.3.refs_0_, bf16[2,2,128,128]{3,2,1,0:T(8,128)(2,1)S(1)} %collective-permute-done.4.refs_1_, bf16[2,2,128,128]{3,2,1,0:T(8,128)(2,1)S(1)} %collective-permute-done.5.refs_2_, ...), custom_call_target="tpu_custom_call" | custom-call | flops 3221225472 | bytes 18874368 | tf_op jit(solution)/shard_map/project/pallas_call | solution.py:449
  (31 shorter events, 0.5 us)
Async XLA Ops:
  0.0 13.6 %copy-start = (bf16[16,128]{1,0:T(8,128)(2,1)S(1)}, bf16[16,128]{1,0:T(8,128)(2,1)}, u32[]{:S(2)}) copy-start(bf16[16,128]{1,0:T(8,128)(2,1)} %param.12) | copy-start | bytes 12292
  0.0 13.6 %copy-start.4 = (bf16[3,3,256]{2,1,0:T(4,128)(2,1)S(1)}, bf16[3,3,256]{2,1,0:T(4,128)(2,1)}, u32[]{:S(2)}) copy-start(bf16[3,3,256]{2,1,0:T(4,128)(2,1)} %param.11) | copy-start | bytes 13828
  5.7 15.1 %collective-permute-start = (bf16[544,384]{1,0:T(8,128)(2,1)}, bf16[544,384]{1,0:T(8,128)(2,1)S(1)}, u32[]{:S(2)}, u32[]{:S(2)}) collective-permute-start(bf16[544,384]{1,0:T(8,128)(2,1)} %get-tuple-element.23), channel_id=1, source_target_pairs={{0,1},{1,0},{2,3},{3,2},{4,5},{5,4},{6,7},{7,6},{8,9},{9,8},{10,11... | collective-permute-start | bytes 1253384 | tf_op jit(solution)/shard_map/ppermute | solution.py:466
  8.7 12.1 %all-to-all-start = ((s32[32,1,128]{2,1,0:T(1,128)}), s32[32,1,128]{2,1,0:T(1,128)S(1)}, u32[]{:S(2)}, u32[]{:S(2)}) async-start(s32[32,1,128]{2,1,0:T(1,128)} %get-tuple-element.22), calls=%async_computation | async-start | bytes 32768 | tf_op jit(solution)/shard_map/all_to_all | solution.py:491
  13.8 7.0 %copy-start.3 = (f32[1,512]{1,0:T(1,128)S(1)}, f32[1,512]{1,0:T(1,128)}, u32[]{:S(2)}) copy-start(f32[1,512]{1,0:T(1,128)} %get-tuple-element.24.sq_ref) | copy-start | bytes 6148
  20.8 1.1 %copy-start.2 = (f32[512,384]{1,0:T(8,128)S(1)}, f32[512,384]{1,0:T(8,128)}, u32[]{:S(2)}) copy-start(f32[512,384]{1,0:T(8,128)} %vocab_share.3.own_ref) | copy-start | bytes 2359300
  21.9 30.4 %copy-start.1 = (bf16[512,4096]{1,0:T(8,128)(2,1)S(1)}, bf16[512,4096]{1,0:T(8,128)(2,1)}, u32[]{:S(2)}) copy-start(bf16[512,4096]{1,0:T(8,128)(2,1)} %refs_5_.1) | copy-start | bytes 12582916
  28.3 8.1 %collective-permute-start.6 = (bf16[2,2,2,128,128]{4,3,2,1,0:T(8,128)(2,1)S(1)}, bf16[2,2,2,128,128]{4,3,2,1,0:T(8,128)(2,1)S(1)}, u32[]{:S(2)}, u32[]{:S(2)}) collective-permute-start(bf16[2,2,2,128,128]{4,3,2,1,0:T(8,128)(2,1)S(1)} %get-tuple-element.28), channel_id=1, source_target_pairs={{0,1},{1,0},{2,3},{3,2},{4,5},{5,4},{6,7},{7,6},{8,9},{9,8},{10,11... | collective-permute-start | bytes 786440 | tf_op jit(solution)/shard_map/ppermute | solution.py:466
  28.8 12.0 %collective-permute-start.1 = (bf16[3,2,2,128,128]{4,3,2,1,0:T(8,128)(2,1)S(1)}, bf16[3,2,2,128,128]{4,3,2,1,0:T(8,128)(2,1)S(1)}, u32[]{:S(2)}, u32[]{:S(2)}) collective-permute-start(bf16[3,2,2,128,128]{4,3,2,1,0:T(8,128)(2,1)S(1)} %get-tuple-element.25), channel_id=1, source_target_pairs={{0,4},{2,6},{4,0},{6,2},{8,12},{10,14},{12,8},{14,10},{16,20},{18,... | collective-permute-start | bytes 1179656 | tf_op jit(solution)/shard_map/ppermute | solution.py:470
  30.2 7.0 %collective-permute-start.2 = (bf16[2,2,128,128]{3,2,1,0:T(8,128)(2,1)S(1)}, bf16[2,2,128,128]{3,2,1,0:T(8,128)(2,1)S(1)}, u32[]{:S(2)}, u32[]{:S(2)}) collective-permute-start(bf16[2,2,128,128]{3,2,1,0:T(8,128)(2,1)S(1)} %get-tuple-element.26), channel_id=1, source_target_pairs={{0,8},{2,10},{4,12},{6,14},{8,0},{10,2},{12,4},{14,6},{16,24},{18,... | collective-permute-start | bytes 393224 | tf_op jit(solution)/shard_map/ppermute | solution.py:470
  31.7 12.7 %collective-permute-start.8 = (bf16[2,2,128,128]{3,2,1,0:T(8,128)(2,1)S(1)}, bf16[2,2,128,128]{3,2,1,0:T(8,128)(2,1)S(1)}, u32[]{:S(2)}, u32[]{:S(2)}) collective-permute-start(bf16[2,2,128,128]{3,2,1,0:T(8,128)(2,1)S(1)} %get-tuple-element.30), channel_id=1, source_target_pairs={{0,16},{2,18},{4,20},{6,22},{8,24},{10,26},{12,28},{14,30},{16,0},... | collective-permute-start | bytes 393224 | tf_op jit(solution)/shard_map/ppermute | solution.py:470
  34.1 10.2 %collective-permute-start.9 = (bf16[2,2,128,128]{3,2,1,0:T(8,128)(2,1)S(1)}, bf16[2,2,128,128]{3,2,1,0:T(8,128)(2,1)S(1)}, u32[]{:S(2)}, u32[]{:S(2)}) collective-permute-start(bf16[2,2,128,128]{3,2,1,0:T(8,128)(2,1)S(1)} %get-tuple-element.31), channel_id=1, source_target_pairs={{0,24},{2,26},{4,28},{6,30},{8,16},{10,18},{12,20},{14,22},{16,8},... | collective-permute-start | bytes 393224 | tf_op jit(solution)/shard_map/ppermute | solution.py:470
  36.4 11.6 %collective-permute-start.7 = (bf16[2,2,2,128,128]{4,3,2,1,0:T(8,128)(2,1)S(1)}, bf16[2,2,2,128,128]{4,3,2,1,0:T(8,128)(2,1)S(1)}, u32[]{:S(2)}, u32[]{:S(2)}) collective-permute-start(bf16[2,2,2,128,128]{4,3,2,1,0:T(8,128)(2,1)S(1)} %pad_maximum_fusion.2), channel_id=1, source_target_pairs={{0,4},{2,6},{4,0},{6,2},{8,12},{10,14},{12,8},{14,10},{16,20},{18,... | collective-permute-start | bytes 786440 | tf_op jit(solution)/shard_map/ppermute | solution.py:470
  37.2 15.1 %collective-permute-start.13 = (bf16[2,2,128,128]{3,2,1,0:T(8,128)(2,1)S(1)}, bf16[2,2,128,128]{3,2,1,0:T(8,128)(2,1)S(1)}, u32[]{:S(2)}, u32[]{:S(2)}) collective-permute-start(bf16[2,2,128,128]{3,2,1,0:T(8,128)(2,1)S(1)} %pad_maximum_fusion.3), channel_id=1, source_target_pairs={{0,2},{2,0},{4,6},{6,4},{8,10},{10,8},{12,14},{14,12},{16,18},{18,... | collective-permute-start | bytes 393224 | tf_op jit(solution)/shard_map/ppermute | solution.py:470
  44.4 7.8 %collective-permute-start.10 = (bf16[3,2,2,128,128]{4,3,2,1,0:T(8,128)(2,1)S(1)}, bf16[3,2,2,128,128]{4,3,2,1,0:T(8,128)(2,1)S(1)}, u32[]{:S(2)}, u32[]{:S(2)}) collective-permute-start(bf16[3,2,2,128,128]{4,3,2,1,0:T(8,128)(2,1)S(1)} %pad_maximum_fusion), channel_id=1, source_target_pairs={{0,1},{1,0},{2,3},{3,2},{4,5},{5,4},{6,7},{7,6},{8,9},{9,8},{10,11... | collective-permute-start | bytes 1179656 | tf_op jit(solution)/shard_map/ppermute | solution.py:466
  45.0 12.1 %collective-permute-start.3 = (bf16[2,2,128,128]{3,2,1,0:T(8,128)(2,1)S(1)}, bf16[2,2,128,128]{3,2,1,0:T(8,128)(2,1)S(1)}, u32[]{:S(2)}, u32[]{:S(2)}) collective-permute-start(bf16[2,2,128,128]{3,2,1,0:T(8,128)(2,1)S(1)} %get-tuple-element.47), channel_id=1, source_target_pairs={{0,8},{2,10},{4,12},{6,14},{8,0},{10,2},{12,4},{14,6},{16,24},{18,... | collective-permute-start | bytes 393224 | tf_op jit(solution)/shard_map/ppermute | solution.py:470
  47.1 11.5 %collective-permute-start.4 = (bf16[2,2,128,128]{3,2,1,0:T(8,128)(2,1)S(1)}, bf16[2,2,128,128]{3,2,1,0:T(8,128)(2,1)S(1)}, u32[]{:S(2)}, u32[]{:S(2)}) collective-permute-start(bf16[2,2,128,128]{3,2,1,0:T(8,128)(2,1)S(1)} %get-tuple-element.46), channel_id=1, source_target_pairs={{0,16},{2,18},{4,20},{6,22},{8,24},{10,26},{12,28},{14,30},{16,0},... | collective-permute-start | bytes 393224 | tf_op jit(solution)/shard_map/ppermute | solution.py:470
  48.0 10.6 %collective-permute-start.5 = (bf16[2,2,128,128]{3,2,1,0:T(8,128)(2,1)S(1)}, bf16[2,2,128,128]{3,2,1,0:T(8,128)(2,1)S(1)}, u32[]{:S(2)}, u32[]{:S(2)}) collective-permute-start(bf16[2,2,128,128]{3,2,1,0:T(8,128)(2,1)S(1)} %get-tuple-element.45), channel_id=1, source_target_pairs={{0,24},{2,26},{4,28},{6,30},{8,16},{10,18},{12,20},{14,22},{16,8},... | collective-permute-start | bytes 393224 | tf_op jit(solution)/shard_map/ppermute | solution.py:470
  52.3 6.3 %collective-permute-start.11 = (bf16[8,2,128,128]{3,2,1,0:T(8,128)(2,1)S(1)}, bf16[8,2,128,128]{3,2,1,0:T(8,128)(2,1)S(1)}, u32[]{:S(2)}, u32[]{:S(2)}) collective-permute-start(bf16[8,2,128,128]{3,2,1,0:T(8,128)(2,1)S(1)} %fusion), channel_id=1, source_target_pairs={{0,2},{2,0},{4,6},{6,4},{8,10},{10,8},{12,14},{14,12},{16,18},{18,... | collective-permute-start | bytes 1572872 | tf_op jit(solution)/shard_map/ppermute | solution.py:470
  58.7 10.1 %collective-permute-start.12 = (bf16[3,2,2,128,128]{4,3,2,1,0:T(8,128)(2,1)S(1)}, bf16[3,2,2,128,128]{4,3,2,1,0:T(8,128)(2,1)S(1)}, u32[]{:S(2)}, u32[]{:S(2)}) collective-permute-start(bf16[3,2,2,128,128]{4,3,2,1,0:T(8,128)(2,1)S(1)} %pad_maximum_fusion.1), channel_id=1, source_target_pairs={{0,1},{1,0},{2,3},{3,2},{4,5},{5,4},{6,7},{7,6},{8,9},{9,8},{10,11... | collective-permute-start | bytes 1179656 | tf_op jit(solution)/shard_map/ppermute | solution.py:466
  68.9 1.8 %collective-permute-start.14 = (bf16[6,2,128,128]{3,2,1,0:T(8,128)(2,1)S(1)}, bf16[6,2,128,128]{3,2,1,0:T(8,128)(2,1)S(1)}, u32[]{:S(2)}, u32[]{:S(2)}) collective-permute-start(bf16[6,2,128,128]{3,2,1,0:T(8,128)(2,1)S(1)} %bitcast_dynamic-update-slice_fusion), channel_id=1, source_target_pairs={{0,2},{2,0},{4,6},{6,4},{8,10},{10,8},{12,14},{14,12},{16,18},{18,... | collective-permute-start | bytes 1179656 | tf_op jit(solution)/shard_map/ppermute | solution.py:470

commit v5 on v4

--- a/solution.py
+++ b/solution.py
@@ -346,10 +346,11 @@
     )(place, tokens, own, got, squares, taps_rows, filt)
 
 
-def project_body(place_ref, *refs, columns, first, last, tile):
+def project_body(place_ref, *refs, columns, skip, first, last, tile):
     hops = len(columns)
-    mine, other, cross, w_hbm = refs[:hops], refs[hops : 2 * hops], refs[2 * hops], refs[2 * hops + 1]
-    rest = refs[2 * hops + 2 :]
+    mine, other = refs[:hops], refs[hops : 2 * hops]
+    cross, cross_other, w_hbm = refs[2 * hops : 2 * hops + 3]
+    rest = refs[2 * hops + 3 :]
     if first:
         tok_ref, table_ref, out_ref, gated, slabs, arrivals, picks = rest
     elif last:
@@ -378,7 +379,7 @@
             (mine[j], 0, core, plane),
             (other[j], 0, core, 1 - plane),
             (cross, j, 1 - core, plane),
-            (cross, hops + j, 1 - core, 1 - plane),
+            (cross_other, skip + j, 1 - core, 1 - plane),
         )
         for ref, lead, from_core, from_plane in pieces:
             at = j * wide + (2 * from_core + from_plane) * chans
@@ -423,14 +424,16 @@
 def project(place, mine, other, cross, columns, w_out, start, last=False):
     hops = len(mine)
     first = isinstance(start, tuple)
+    cross, cross_other = cross if isinstance(cross, tuple) else (cross, cross)
+    skip = cross_other.shape[0] - hops
     _, genomes, rows, chans = cross.shape
     feats = w_out.shape[0]
     tile = 1024
     tiles = feats // tile
     vmem = pl.BlockSpec(memory_space=pltpu.VMEM)
     anywhere = pl.BlockSpec(memory_space=pl.ANY)
-    operands = mine + other + [cross, w_out]
-    in_specs = [pl.BlockSpec(memory_space=pltpu.SMEM)] + [vmem] * (2 * hops + 1) + [anywhere]
+    operands = mine + other + [cross, cross_other, w_out]
+    in_specs = [pl.BlockSpec(memory_space=pltpu.SMEM)] + [vmem] * (2 * hops + 2) + [anywhere]
     scratch = [
         pltpu.VMEM((genomes * rows, hops * 4 * chans), jnp.bfloat16),
         pltpu.VMEM((tiles, tile, hops * 4 * chans), jnp.bfloat16),
@@ -447,7 +450,9 @@
     if last:
         scratch += [pltpu.VMEM(shape, jnp.bfloat16), pltpu.SemaphoreType.DMA((tiles,))]
     return pl.pallas_call(
-        functools.partial(project_body, columns=columns, first=first, last=last, tile=tile),
+        functools.partial(
+            project_body, columns=columns, skip=skip, first=first, last=last, tile=tile
+        ),
         in_specs=in_specs,
         out_specs=anywhere if last else vmem,
         scratch_shapes=scratch,
@@ -521,12 +526,13 @@
     far_mine = [far_mine[k] for k in range(1, hops)]
     far_mine, cross = bar((far_mine, cross))
     far_other = swap_wt(jnp.stack(far_mine))
+    far_cross = swap_seq(jnp.stack([a[1] for a in far_mine]), 1)
     columns = [1] + [2 * k for k in range(1, hops)]
     total, _ = bar((total, far_mine))
     total = project(place, near_mine, near_other, cross, columns, w_out, total)
     far_other, total = bar((far_other, total))
     far_other = [far_other[k] for k in range(hops - 1)]
-    cross = swap_core(far_mine, far_other)
+    cross = (far_cross, swap_seq(jnp.stack([a[1] for a in far_other]), 1))
     columns = [2 * k + 1 for k in range(1, hops)]
     return project(place, far_mine, far_other, cross, columns, w_out, total, True)
 

time: 79.7 us -> 79.4 us (level)
    ppermute x11 -> x12, waiting for transfers between devices: 10.2 us -> 9.99 us  [swap_seq(): lax.ppermute(shard, 'seq', [(i, i ^ step) for i in range(lax.axis_size('s...]
    ppermute x11 -> x12, starting transfers between devices: 11.3 us -> 11.2 us  [swap_seq(): lax.ppermute(shard, 'seq', [(i, i ^ step) for i in range(lax.axis_size('s...]
  transfers between devices with their start and end apart: 16 -> 17, of which waited for: 8 -> 9; matrix products, arithmetic and copies ran while one was open for 1% -> 1% of each run, Pallas kernels for 23% -> 24%
where the time goes in v5:
time: 79.4 us; the launch traced here: 78 us
  Pallas kernels  37.9 us (48%)
  starting transfers between devices  21.8 us (27%)
  waiting for transfers between devices  16.2 us (20%)
  local copies, waits for them, and re-layouts  1.47 us (2%)
    pallas_call x3, Pallas kernels, project(): pl.pallas_call(functools.partial(project_body, columns=columns, skip=skip...  20.2 us
    pallas_call x2, Pallas kernels, vocab_share(): pl.pallas_call(functools.partial(vocab_share_body, slabs=slabs, steps=ste...  11.3 us
    ppermute x12, starting transfers between devices, swap_seq(): lax.ppermute(shard, 'seq', [(i, i ^ step) for i in range(lax.axis_size('s...  11.2 us
    ppermute x12, waiting for transfers between devices, swap_seq(): lax.ppermute(shard, 'seq', [(i, i ^ step) for i in range(lax.axis_size('s...  9.99 us
    pallas_call x1, Pallas kernels, mixer(): pl.pallas_call(functools.partial(mixer_body, feature_count=feature_count,...  6.31 us
    ppermute x4, starting transfers between devices, swap_wt(): return lax.ppermute(shard, 'wt', [(0, 1), (1, 0)])  5.67 us
    all_to_all x1, starting transfers between devices, shared_block(): all_tokens = lax.all_to_all(copies, ('seq', 'wt'), 0, 0, tiled=True)  4.89 us
    ppermute x4, waiting for transfers between devices, swap_wt(): return lax.ppermute(shard, 'wt', [(0, 1), (1, 0)])  4.79 us
  transfers between devices with their start and end apart: 17, of which 9 were waited for; matrix products, arithmetic and copies ran while one was open for 1% of the time, Pallas kernels for 24%

profile of v5, /device:TPU:0, one launch (start us, length us, event | category | flops | bytes accessed | tf_op | source)
XLA Modules:
  0.0 78.0 jit_solution(40941344023944099)
XLA Ops:
  0.0 0.0 copy-start
  0.0 5.7 %vocab_share.2 = (bf16[544,384]{1,0:T(8,128)(2,1)}, f32[1,512]{1,0:T(1,128)}, s32[32,1,128]{2,1,0:T(1,128)}) custom-call(s32[1]{0:T(128)} %bitcast.2.half_ref, bf16[4096]{0:T(1024)(128)(2,1)} %gain_ref.3, bf16[512,4096]{1,0:T(8,128)(2,1)} %refs_6_.1, bf16[512,4096]{1,0:T(8,128)(2,1)} %refs_6_.1, bf16[3,4096,256]{2,1,0:T(8,128)(2,1)} %bitcast.75, ...), custom_call_target="tpu_custom_call" | custom-call | tf_op jit(solution)/shard_map/vocab_share/pallas_call | solution.py:187
  5.7 3.0 %collective-permute-start = (bf16[544,384]{1,0:T(8,128)(2,1)}, bf16[544,384]{1,0:T(8,128)(2,1)S(1)}, u32[]{:S(2)}, u32[]{:S(2)}) collective-permute-start(bf16[544,384]{1,0:T(8,128)(2,1)} %get-tuple-element.23), channel_id=1, source_target_pairs={{0,1},{1,0},{2,3},{3,2},{4,5},{5,4},{6,7},{7,6},{8,9},{9,8},{10,11... | collective-permute-start | bytes 1253384 | tf_op jit(solution)/shard_map/ppermute | solution.py:471
  8.7 4.9 %all-to-all-start = ((s32[32,1,128]{2,1,0:T(1,128)}), s32[32,1,128]{2,1,0:T(1,128)S(1)}, u32[]{:S(2)}, u32[]{:S(2)}) async-start(s32[32,1,128]{2,1,0:T(1,128)} %get-tuple-element.22), calls=%async_computation | async-start | bytes 32768 | tf_op jit(solution)/shard_map/all_to_all | solution.py:496
  13.6 0.0 copy-done.4
  13.6 0.0 copy-done
  13.7 0.1 pad_add_fusion.place_ref
  13.7 0.0 copy-start.3
  13.7 5.6 %vocab_share.3.own_ref = f32[512,384]{1,0:T(8,128)} custom-call(s32[1]{0:T(128)} %bitcast.1.half_ref, bf16[4096]{0:T(1024)(128)(2,1)} %gain_ref.3, bf16[512,4096]{1,0:T(8,128)(2,1)} %refs_6_.1, bf16[512,4096]{1,0:T(8,128)(2,1)} %refs_6_.1, bf16[3,4096,256]{2,1,0:T(8,128)(2,1)} %bitcast.77, bf16[3,4096,256]{2,1,0:T(8,128)(2,1)} %bitcast.78), custom_call_target="tpu_custom_call" | custom-call | tf_op jit(solution)/shard_map/vocab_share/pallas_call | solution.py:187
  19.4 1.4 %all-to-all-done = s32[32,1,128]{2,1,0:T(1,128)S(1)} async-done(((s32[32,1,128]{2,1,0:T(1,128)}), s32[32,1,128]{2,1,0:T(1,128)S(1)}, u32[]{:S(2)}, u32[]{:S(2)}) %all-to-all-start) | async-done | bytes 16416 | tf_op jit(solution)/shard_map/all_to_all | solution.py:496
  20.8 0.0 collective-permute-done.got_ref
  20.8 0.0 copy-done.3
  20.8 1.1 %copy-done.2 = f32[512,384]{1,0:T(8,128)S(1)} copy-done((f32[512,384]{1,0:T(8,128)S(1)}, f32[512,384]{1,0:T(8,128)}, u32[]{:S(2)}) %copy-start.2) | copy-done | bytes 786456
  21.9 6.3 %mixer.1 = (bf16[2,2,2,128,128]{4,3,2,1,0:T(8,128)(2,1)S(1)}, bf16[2,2,128,128]{3,2,1,0:T(8,128)(2,1)S(1)}, bf16[2,2,128,128]{3,2,1,0:T(8,128)(2,1)S(1)}, bf16[2...) custom-call(s32[2]{0:T(128)S(1)} %pad_add_fusion.place_ref, s32[16,2,128]{2,1,0:T(2,128)S(1)} %bitcast.73, ...), custom_call_target="tpu_custom_call" | custom-call | flops 1610612736 | bytes 2228224 | tf_op jit(solution)/shard_map/mixer/pallas_call | solution.py:310
  28.3 0.6 collective-permute-start.6
  28.8 1.4 %collective-permute-start.1 = (bf16[3,2,2,128,128]{4,3,2,1,0:T(8,128)(2,1)S(1)}, bf16[3,2,2,128,128]{4,3,2,1,0:T(8,128)(2,1)S(1)}, u32[]{:S(2)}, u32[]{:S(2)}) collective-permute-start(bf16[3,2,2,128,128]{4,3,2,1,0:T(8,128)(2,1)S(1)} %get-tuple-element.25), channel_id=1, source_target_pairs={{0,4},{2,6},{4,0},{6,2},{8,12},{10,14},{12,8},{14,10},{16,20},{18,... | collective-permute-start | bytes 1179656 | tf_op jit(solution)/shard_map/ppermute | solution.py:475
  30.2 1.5 %collective-permute-start.2 = (bf16[2,2,128,128]{3,2,1,0:T(8,128)(2,1)S(1)}, bf16[2,2,128,128]{3,2,1,0:T(8,128)(2,1)S(1)}, u32[]{:S(2)}, u32[]{:S(2)}) collective-permute-start(bf16[2,2,128,128]{3,2,1,0:T(8,128)(2,1)S(1)} %get-tuple-element.26), channel_id=1, source_target_pairs={{0,8},{2,10},{4,12},{6,14},{8,0},{10,2},{12,4},{14,6},{16,24},{18,... | collective-permute-start | bytes 393224 | tf_op jit(solution)/shard_map/ppermute | solution.py:475
  31.6 2.5 %collective-permute-start.8 = (bf16[2,2,128,128]{3,2,1,0:T(8,128)(2,1)S(1)}, bf16[2,2,128,128]{3,2,1,0:T(8,128)(2,1)S(1)}, u32[]{:S(2)}, u32[]{:S(2)}) collective-permute-start(bf16[2,2,128,128]{3,2,1,0:T(8,128)(2,1)S(1)} %get-tuple-element.30), channel_id=1, source_target_pairs={{0,16},{2,18},{4,20},{6,22},{8,24},{10,26},{12,28},{14,30},{16,0},... | collective-permute-start | bytes 393224 | tf_op jit(solution)/shard_map/ppermute | solution.py:475
  34.1 0.5 collective-permute-start.9
  34.6 1.7 %collective-permute-done.6 = bf16[2,2,2,128,128]{4,3,2,1,0:T(8,128)(2,1)S(1)} collective-permute-done((bf16[2,2,2,128,128]{4,3,2,1,0:T(8,128)(2,1)S(1)}, bf16[2,2,2,128,128]{4,3,2,1,0:T(8,128)(2,1)S(1)}, u32[]{:S(2)}, u32[]{:S(2)}) %collective-permute-start.6) | collective-permute-done | bytes 262176 | tf_op jit(solution)/shard_map/ppermute | solution.py:471
  36.3 0.1 collective-permute-start.13
  36.5 0.2 collective-permute-done.2.refs_1_
  36.7 0.7 collective-permute-start.7
  37.4 2.3 %collective-permute-done.1 = bf16[3,2,2,128,128]{4,3,2,1,0:T(8,128)(2,1)S(1)} collective-permute-done((bf16[3,2,2,128,128]{4,3,2,1,0:T(8,128)(2,1)S(1)}, bf16[3,2,2,128,128]{4,3,2,1,0:T(8,128)(2,1)S(1)}, u32[]{:S(2)}, u32[]{:S(2)}) %collective-permute-start.1) | collective-permute-done | bytes 393248 | tf_op jit(solution)/shard_map/ppermute | solution.py:475
  39.6 4.7 %collective-permute-done.8.refs_2_ = bf16[2,2,128,128]{3,2,1,0:T(8,128)(2,1)S(1)} collective-permute-done((bf16[2,2,128,128]{3,2,1,0:T(8,128)(2,1)S(1)}, bf16[2,2,128,128]{3,2,1,0:T(8,128)(2,1)S(1)}, u32[]{:S(2)}, u32[]{:S(2)}) %collective-permute-start.8) | collective-permute-done | bytes 131104 | tf_op jit(solution)/shard_map/ppermute | solution.py:475
  44.3 0.0 collective-permute-done.9.refs_3_
  44.4 0.6 collective-permute-start.10
  45.0 2.0 %collective-permute-start.3 = (bf16[2,2,128,128]{3,2,1,0:T(8,128)(2,1)S(1)}, bf16[2,2,128,128]{3,2,1,0:T(8,128)(2,1)S(1)}, u32[]{:S(2)}, u32[]{:S(2)}) collective-permute-start(bf16[2,2,128,128]{3,2,1,0:T(8,128)(2,1)S(1)} %get-tuple-element.50), channel_id=1, source_target_pairs={{0,8},{2,10},{4,12},{6,14},{8,0},{10,2},{12,4},{14,6},{16,24},{18,... | collective-permute-start | bytes 393224 | tf_op jit(solution)/shard_map/ppermute | solution.py:475
  47.1 0.9 %collective-permute-start.4 = (bf16[2,2,128,128]{3,2,1,0:T(8,128)(2,1)S(1)}, bf16[2,2,128,128]{3,2,1,0:T(8,128)(2,1)S(1)}, u32[]{:S(2)}, u32[]{:S(2)}) collective-permute-start(bf16[2,2,128,128]{3,2,1,0:T(8,128)(2,1)S(1)} %get-tuple-element.49), channel_id=1, source_target_pairs={{0,16},{2,18},{4,20},{6,22},{8,24},{10,26},{12,28},{14,30},{16,0},... | collective-permute-start | bytes 393224 | tf_op jit(solution)/shard_map/ppermute | solution.py:475
  48.0 0.0 collective-permute-done.7
  48.0 1.5 %collective-permute-start.5 = (bf16[2,2,128,128]{3,2,1,0:T(8,128)(2,1)S(1)}, bf16[2,2,128,128]{3,2,1,0:T(8,128)(2,1)S(1)}, u32[]{:S(2)}, u32[]{:S(2)}) collective-permute-start(bf16[2,2,128,128]{3,2,1,0:T(8,128)(2,1)S(1)} %get-tuple-element.48), channel_id=1, source_target_pairs={{0,24},{2,26},{4,28},{6,30},{8,16},{10,18},{12,20},{14,22},{16,8},... | collective-permute-start | bytes 393224 | tf_op jit(solution)/shard_map/ppermute | solution.py:475
  49.6 2.6 %collective-permute-done.10 = bf16[3,2,2,128,128]{4,3,2,1,0:T(8,128)(2,1)S(1)} collective-permute-done((bf16[3,2,2,128,128]{4,3,2,1,0:T(8,128)(2,1)S(1)}, bf16[3,2,2,128,128]{4,3,2,1,0:T(8,128)(2,1)S(1)}, u32[]{:S(2)}, u32[]{:S(2)}) %collective-permute-start.10) | collective-permute-done | bytes 393248 | tf_op jit(solution)/shard_map/ppermute | solution.py:471
  52.3 0.1 collective-permute-start.11
  52.4 0.0 collective-permute-done.13.refs_2_.refs_3_
  52.4 0.0 copy-done.1
  52.4 4.7 %project.3.refs_11_ = f32[2,128,4096]{2,1,0:T(8,128)S(1)} custom-call(s32[2]{0:T(128)S(1)} %pad_add_fusion.place_ref, bf16[2,2,128,128]{3,2,1,0:T(8,128)(2,1)S(1)} %get-tuple-element.53.refs_0_, bf16[2,2,128,128]{3,2,1,0:T(8,128)(2,1)S(1)} %get-tuple-element.51.refs_1_, bf16[2,2,128,128]{3,2,1,0:T(8,128)(2,1)S(1)} %collective-permute-done.13.refs_2_.refs_3_, ...), custom_call_target="tpu_custom_call" | custom-call | flops 1073741824 | bytes 10485760 | tf_op jit(solution)/shard_map/project/pallas_call | solution.py:452
  57.1 0.0 collective-permute-done.3.refs_0_
  57.1 1.5 %collective-permute-done.4.refs_1_ = bf16[2,2,128,128]{3,2,1,0:T(8,128)(2,1)S(1)} collective-permute-done((bf16[2,2,128,128]{3,2,1,0:T(8,128)(2,1)S(1)}, bf16[2,2,128,128]{3,2,1,0:T(8,128)(2,1)S(1)}, u32[]{:S(2)}, u32[]{:S(2)}) %collective-permute-start.4) | collective-permute-done | bytes 131104 | tf_op jit(solution)/shard_map/ppermute | solution.py:475
  58.6 0.0 collective-permute-done.5.refs_2_
  58.6 0.0 collective-permute-done.11.refs_8_.refs_9_
  58.7 1.5 %collective-permute-start.12 = (bf16[3,2,2,128,128]{4,3,2,1,0:T(8,128)(2,1)S(1)}, bf16[3,2,2,128,128]{4,3,2,1,0:T(8,128)(2,1)S(1)}, u32[]{:S(2)}, u32[]{:S(2)}) collective-permute-start(bf16[3,2,2,128,128]{4,3,2,1,0:T(8,128)(2,1)S(1)} %pad_maximum_fusion.1), channel_id=1, source_target_pairs={{0,1},{1,0},{2,3},{3,2},{4,5},{5,4},{6,7},{7,6},{8,9},{9,8},{10,11... | collective-permute-start | bytes 1179656 | tf_op jit(solution)/shard_map/ppermute | solution.py:471
  60.2 0.1 collective-permute-start.14
  60.3 8.1 %project.4.refs_9_ = f32[2,128,4096]{2,1,0:T(8,128)S(1)} custom-call(s32[2]{0:T(128)S(1)} %pad_add_fusion.place_ref, bf16[2,2,128,128]{3,2,1,0:T(8,128)(2,1)S(1)} %get-tuple-element.56.refs_0_, bf16[2,2,128,128]{3,2,1,0:T(8,128)(2,1)S(1)} %collective-permute-done.2.refs_1_, bf16[2,2,128,128]{3,2,1,0:T(8,128)(2,1)S(1)} %collective-permute-done.8.refs_2_, ...), custom_call_target="tpu_custom_call" | custom-call | flops 4294967296 | bytes 23068672 | tf_op jit(solution)/shard_map/project/pallas_call | solution.py:452
  68.4 0.4 collective-permute-done.12
  68.9 0.2 collective-permute-start.15
  69.1 0.0 collective-permute-done.14.refs_6_
  69.1 1.3 %collective-permute-done.15.refs_7_ = bf16[3,2,128,128]{3,2,1,0:T(8,128)(2,1)S(1)} collective-permute-done((bf16[3,2,128,128]{3,2,1,0:T(8,128)(2,1)S(1)}, bf16[3,2,128,128]{3,2,1,0:T(8,128)(2,1)S(1)}, u32[]{:S(2)}, u32[]{:S(2)}) %collective-permute-start.15) | collective-permute-done | bytes 196640 | tf_op jit(solution)/shard_map/ppermute | solution.py:475
  70.4 7.5 %project.5 = bf16[2,128,4096]{2,1,0:T(8,128)(2,1)} custom-call(s32[2]{0:T(128)S(1)} %pad_add_fusion.place_ref, bf16[2,2,128,128]{3,2,1,0:T(8,128)(2,1)S(1)} %collective-permute-done.3.refs_0_, bf16[2,2,128,128]{3,2,1,0:T(8,128)(2,1)S(1)} %collective-permute-done.4.refs_1_, bf16[2,2,128,128]{3,2,1,0:T(8,128)(2,1)S(1)} %collective-permute-done.5.refs_2_, ...), custom_call_target="tpu_custom_call" | custom-call | flops 3221225472 | bytes 18874368 | tf_op jit(solution)/shard_map/project/pallas_call | solution.py:452
  (33 shorter events, 0.5 us)
Async XLA Ops:
  0.0 13.6 %copy-start = (bf16[16,128]{1,0:T(8,128)(2,1)S(1)}, bf16[16,128]{1,0:T(8,128)(2,1)}, u32[]{:S(2)}) copy-start(bf16[16,128]{1,0:T(8,128)(2,1)} %param.12) | copy-start | bytes 12292
  0.0 13.6 %copy-start.4 = (bf16[3,3,256]{2,1,0:T(4,128)(2,1)S(1)}, bf16[3,3,256]{2,1,0:T(4,128)(2,1)}, u32[]{:S(2)}) copy-start(bf16[3,3,256]{2,1,0:T(4,128)(2,1)} %param.11) | copy-start | bytes 13828
  5.7 15.1 %collective-permute-start = (bf16[544,384]{1,0:T(8,128)(2,1)}, bf16[544,384]{1,0:T(8,128)(2,1)S(1)}, u32[]{:S(2)}, u32[]{:S(2)}) collective-permute-start(bf16[544,384]{1,0:T(8,128)(2,1)} %get-tuple-element.23), channel_id=1, source_target_pairs={{0,1},{1,0},{2,3},{3,2},{4,5},{5,4},{6,7},{7,6},{8,9},{9,8},{10,11... | collective-permute-start | bytes 1253384 | tf_op jit(solution)/shard_map/ppermute | solution.py:471
  8.7 12.1 %all-to-all-start = ((s32[32,1,128]{2,1,0:T(1,128)}), s32[32,1,128]{2,1,0:T(1,128)S(1)}, u32[]{:S(2)}, u32[]{:S(2)}) async-start(s32[32,1,128]{2,1,0:T(1,128)} %get-tuple-element.22), calls=%async_computation | async-start | bytes 32768 | tf_op jit(solution)/shard_map/all_to_all | solution.py:496
  13.7 7.0 %copy-start.3 = (f32[1,512]{1,0:T(1,128)S(1)}, f32[1,512]{1,0:T(1,128)}, u32[]{:S(2)}) copy-start(f32[1,512]{1,0:T(1,128)} %get-tuple-element.24.sq_ref) | copy-start | bytes 6148
  20.8 1.1 %copy-start.2 = (f32[512,384]{1,0:T(8,128)S(1)}, f32[512,384]{1,0:T(8,128)}, u32[]{:S(2)}) copy-start(f32[512,384]{1,0:T(8,128)} %vocab_share.3.own_ref) | copy-start | bytes 2359300
  21.9 30.4 %copy-start.1 = (bf16[512,4096]{1,0:T(8,128)(2,1)S(1)}, bf16[512,4096]{1,0:T(8,128)(2,1)}, u32[]{:S(2)}) copy-start(bf16[512,4096]{1,0:T(8,128)(2,1)} %refs_6_.1) | copy-start | bytes 12582916
  28.3 8.1 %collective-permute-start.6 = (bf16[2,2,2,128,128]{4,3,2,1,0:T(8,128)(2,1)S(1)}, bf16[2,2,2,128,128]{4,3,2,1,0:T(8,128)(2,1)S(1)}, u32[]{:S(2)}, u32[]{:S(2)}) collective-permute-start(bf16[2,2,2,128,128]{4,3,2,1,0:T(8,128)(2,1)S(1)} %get-tuple-element.28), channel_id=1, source_target_pairs={{0,1},{1,0},{2,3},{3,2},{4,5},{5,4},{6,7},{7,6},{8,9},{9,8},{10,11... | collective-permute-start | bytes 786440 | tf_op jit(solution)/shard_map/ppermute | solution.py:471
  28.8 10.8 %collective-permute-start.1 = (bf16[3,2,2,128,128]{4,3,2,1,0:T(8,128)(2,1)S(1)}, bf16[3,2,2,128,128]{4,3,2,1,0:T(8,128)(2,1)S(1)}, u32[]{:S(2)}, u32[]{:S(2)}) collective-permute-start(bf16[3,2,2,128,128]{4,3,2,1,0:T(8,128)(2,1)S(1)} %get-tuple-element.25), channel_id=1, source_target_pairs={{0,4},{2,6},{4,0},{6,2},{8,12},{10,14},{12,8},{14,10},{16,20},{18,... | collective-permute-start | bytes 1179656 | tf_op jit(solution)/shard_map/ppermute | solution.py:475
  30.2 6.5 %collective-permute-start.2 = (bf16[2,2,128,128]{3,2,1,0:T(8,128)(2,1)S(1)}, bf16[2,2,128,128]{3,2,1,0:T(8,128)(2,1)S(1)}, u32[]{:S(2)}, u32[]{:S(2)}) collective-permute-start(bf16[2,2,128,128]{3,2,1,0:T(8,128)(2,1)S(1)} %get-tuple-element.26), channel_id=1, source_target_pairs={{0,8},{2,10},{4,12},{6,14},{8,0},{10,2},{12,4},{14,6},{16,24},{18,... | collective-permute-start | bytes 393224 | tf_op jit(solution)/shard_map/ppermute | solution.py:475
  31.6 12.7 %collective-permute-start.8 = (bf16[2,2,128,128]{3,2,1,0:T(8,128)(2,1)S(1)}, bf16[2,2,128,128]{3,2,1,0:T(8,128)(2,1)S(1)}, u32[]{:S(2)}, u32[]{:S(2)}) collective-permute-start(bf16[2,2,128,128]{3,2,1,0:T(8,128)(2,1)S(1)} %get-tuple-element.30), channel_id=1, source_target_pairs={{0,16},{2,18},{4,20},{6,22},{8,24},{10,26},{12,28},{14,30},{16,0},... | collective-permute-start | bytes 393224 | tf_op jit(solution)/shard_map/ppermute | solution.py:475
  34.1 10.2 %collective-permute-start.9 = (bf16[2,2,128,128]{3,2,1,0:T(8,128)(2,1)S(1)}, bf16[2,2,128,128]{3,2,1,0:T(8,128)(2,1)S(1)}, u32[]{:S(2)}, u32[]{:S(2)}) collective-permute-start(bf16[2,2,128,128]{3,2,1,0:T(8,128)(2,1)S(1)} %get-tuple-element.31), channel_id=1, source_target_pairs={{0,24},{2,26},{4,28},{6,30},{8,16},{10,18},{12,20},{14,22},{16,8},... | collective-permute-start | bytes 393224 | tf_op jit(solution)/shard_map/ppermute | solution.py:475
  36.3 16.0 %collective-permute-start.13 = (bf16[2,2,128,128]{3,2,1,0:T(8,128)(2,1)S(1)}, bf16[2,2,128,128]{3,2,1,0:T(8,128)(2,1)S(1)}, u32[]{:S(2)}, u32[]{:S(2)}) collective-permute-start(bf16[2,2,128,128]{3,2,1,0:T(8,128)(2,1)S(1)} %pad_maximum_fusion.5), channel_id=1, source_target_pairs={{0,2},{2,0},{4,6},{6,4},{8,10},{10,8},{12,14},{14,12},{16,18},{18,... | collective-permute-start | bytes 393224 | tf_op jit(solution)/shard_map/ppermute | solution.py:475
  36.7 11.3 %collective-permute-start.7 = (bf16[2,2,2,128,128]{4,3,2,1,0:T(8,128)(2,1)S(1)}, bf16[2,2,2,128,128]{4,3,2,1,0:T(8,128)(2,1)S(1)}, u32[]{:S(2)}, u32[]{:S(2)}) collective-permute-start(bf16[2,2,2,128,128]{4,3,2,1,0:T(8,128)(2,1)S(1)} %pad_maximum_fusion.2), channel_id=1, source_target_pairs={{0,4},{2,6},{4,0},{6,2},{8,12},{10,14},{12,8},{14,10},{16,20},{18,... | collective-permute-start | bytes 786440 | tf_op jit(solution)/shard_map/ppermute | solution.py:475
  44.4 7.8 %collective-permute-start.10 = (bf16[3,2,2,128,128]{4,3,2,1,0:T(8,128)(2,1)S(1)}, bf16[3,2,2,128,128]{4,3,2,1,0:T(8,128)(2,1)S(1)}, u32[]{:S(2)}, u32[]{:S(2)}) collective-permute-start(bf16[3,2,2,128,128]{4,3,2,1,0:T(8,128)(2,1)S(1)} %pad_maximum_fusion), channel_id=1, source_target_pairs={{0,1},{1,0},{2,3},{3,2},{4,5},{5,4},{6,7},{7,6},{8,9},{9,8},{10,11... | collective-permute-start | bytes 1179656 | tf_op jit(solution)/shard_map/ppermute | solution.py:471
  45.0 12.1 %collective-permute-start.3 = (bf16[2,2,128,128]{3,2,1,0:T(8,128)(2,1)S(1)}, bf16[2,2,128,128]{3,2,1,0:T(8,128)(2,1)S(1)}, u32[]{:S(2)}, u32[]{:S(2)}) collective-permute-start(bf16[2,2,128,128]{3,2,1,0:T(8,128)(2,1)S(1)} %get-tuple-element.50), channel_id=1, source_target_pairs={{0,8},{2,10},{4,12},{6,14},{8,0},{10,2},{12,4},{14,6},{16,24},{18,... | collective-permute-start | bytes 393224 | tf_op jit(solution)/shard_map/ppermute | solution.py:475
  47.1 11.5 %collective-permute-start.4 = (bf16[2,2,128,128]{3,2,1,0:T(8,128)(2,1)S(1)}, bf16[2,2,128,128]{3,2,1,0:T(8,128)(2,1)S(1)}, u32[]{:S(2)}, u32[]{:S(2)}) collective-permute-start(bf16[2,2,128,128]{3,2,1,0:T(8,128)(2,1)S(1)} %get-tuple-element.49), channel_id=1, source_target_pairs={{0,16},{2,18},{4,20},{6,22},{8,24},{10,26},{12,28},{14,30},{16,0},... | collective-permute-start | bytes 393224 | tf_op jit(solution)/shard_map/ppermute | solution.py:475
  48.0 10.6 %collective-permute-start.5 = (bf16[2,2,128,128]{3,2,1,0:T(8,128)(2,1)S(1)}, bf16[2,2,128,128]{3,2,1,0:T(8,128)(2,1)S(1)}, u32[]{:S(2)}, u32[]{:S(2)}) collective-permute-start(bf16[2,2,128,128]{3,2,1,0:T(8,128)(2,1)S(1)} %get-tuple-element.48), channel_id=1, source_target_pairs={{0,24},{2,26},{4,28},{6,30},{8,16},{10,18},{12,20},{14,22},{16,8},... | collective-permute-start | bytes 393224 | tf_op jit(solution)/shard_map/ppermute | solution.py:475
  52.3 6.3 %collective-permute-start.11 = (bf16[8,2,128,128]{3,2,1,0:T(8,128)(2,1)S(1)}, bf16[8,2,128,128]{3,2,1,0:T(8,128)(2,1)S(1)}, u32[]{:S(2)}, u32[]{:S(2)}) collective-permute-start(bf16[8,2,128,128]{3,2,1,0:T(8,128)(2,1)S(1)} %fusion), channel_id=1, source_target_pairs={{0,2},{2,0},{4,6},{6,4},{8,10},{10,8},{12,14},{14,12},{16,18},{18,... | collective-permute-start | bytes 1572872 | tf_op jit(solution)/shard_map/ppermute | solution.py:475
  58.7 10.1 %collective-permute-start.12 = (bf16[3,2,2,128,128]{4,3,2,1,0:T(8,128)(2,1)S(1)}, bf16[3,2,2,128,128]{4,3,2,1,0:T(8,128)(2,1)S(1)}, u32[]{:S(2)}, u32[]{:S(2)}) collective-permute-start(bf16[3,2,2,128,128]{4,3,2,1,0:T(8,128)(2,1)S(1)} %pad_maximum_fusion.1), channel_id=1, source_target_pairs={{0,1},{1,0},{2,3},{3,2},{4,5},{5,4},{6,7},{7,6},{8,9},{9,8},{10,11... | collective-permute-start | bytes 1179656 | tf_op jit(solution)/shard_map/ppermute | solution.py:471
  60.2 8.8 %collective-permute-start.14 = (bf16[3,2,128,128]{3,2,1,0:T(8,128)(2,1)S(1)}, bf16[3,2,128,128]{3,2,1,0:T(8,128)(2,1)S(1)}, u32[]{:S(2)}, u32[]{:S(2)}) collective-permute-start(bf16[3,2,128,128]{3,2,1,0:T(8,128)(2,1)S(1)} %pad_maximum_fusion.3), channel_id=1, source_target_pairs={{0,2},{2,0},{4,6},{6,4},{8,10},{10,8},{12,14},{14,12},{16,18},{18,... | collective-permute-start | bytes 589832 | tf_op jit(solution)/shard_map/ppermute | solution.py:475
  68.9 1.5 %collective-permute-start.15 = (bf16[3,2,128,128]{3,2,1,0:T(8,128)(2,1)S(1)}, bf16[3,2,128,128]{3,2,1,0:T(8,128)(2,1)S(1)}, u32[]{:S(2)}, u32[]{:S(2)}) collective-permute-start(bf16[3,2,128,128]{3,2,1,0:T(8,128)(2,1)S(1)} %pad_maximum_fusion.4), channel_id=1, source_target_pairs={{0,2},{2,0},{4,6},{6,4},{8,10},{10,8},{12,14},{14,12},{16,18},{18,... | collective-permute-start | bytes 589832 | tf_op jit(solution)/shard_map/ppermute | solution.py:475
